TPU v7x, 32 devices: a whole 2x2x4 slice. The times are simulated.
32 devices in a mesh: seq: 2 (over x), hist: 8 (over z, y), chan: 2 (over core).
Axes of the slice: x: 2, y: 2, z: 4, core: 2. Of those that a mesh axis runs over, the one named last changes fastest.
Arguments:
- history: bfloat16 [4096, 4096], P(('seq', 'hist'), 'chan'), parts along dimension 0, may hold values from -6 to 6
- filter_taps: bfloat16 [2048, 4096], P('hist', 'chan'), may hold values from -0.125 to 0.125
- gate_values: bfloat16 [512, 4096], P(('seq', 'hist'), 'chan'), parts along dimension 0, may hold values from -6 to 6
- out_weight: bfloat16 [4096, 4096], P('chan', 'hist'), may hold values from -0.09375 to 0.09375
Outputs:
- output: bfloat16 [512, 4096], P(('seq', 'hist', 'chan')), parts along dimension 0
There are 2 independent parts, one for each index of `seq`. A program takes and returns all parts, laid end to end along the dimension named above; an argument that names none is the same for every part. Nothing has to cross between parts.
All inputs are finite; a program needn't handle non-finite values.
Results may differ from a plain program's by a relative error of at most 0.013.
Values may be sent and summed in bfloat16 or wider, within the bound.
No kernel may reach another device: no remote copies, remote signals or barrier semaphores. Data moves between devices by JAX's collectives and lax.ppermute only.
A program may use at most 64 MiB of HBM per device.

v0:
```python
import math

import jax
import jax.numpy as jnp
from jax import lax
from jax.sharding import PartitionSpec as P


def shifted(value, axis, steps):
    count = lax.axis_size(axis)
    initial, last = (max(0, -steps), min(count, count - steps))
    return lax.ppermute(value, axis, [(source, source + steps) for source in range(initial, last)])


def split_product(table_high, table_low, values):
    first = jnp.dot(table_high, values, preferred_element_type=jnp.float32)
    return first + jnp.dot(table_low, values, preferred_element_type=jnp.float32)


def inverse_part(real_part, imag_part, block_tokens, period, row_count):
    scale = 2.0 * math.pi / period
    lags = block_tokens - 1 - lax.broadcasted_iota(jnp.int32, (row_count, period), 0)
    orders = lax.broadcasted_iota(jnp.int32, (row_count, period), 1)
    phases = (lags * orders % period).astype(jnp.float32) * scale
    cosines = jnp.dot(
        jnp.cos(phases),
        real_part,
        precision=lax.Precision.HIGHEST,
        preferred_element_type=jnp.float32,
    )
    sines = jnp.dot(
        jnp.sin(phases),
        imag_part,
        precision=lax.Precision.HIGHEST,
        preferred_element_type=jnp.float32,
    )
    return (cosines - sines) / period


def local(history, filter_taps, gate_values, out_weight):
    local_rows, channels = history.shape
    owned_rows = gate_values.shape[0]
    count_hist = lax.axis_size("hist")
    count_chan = lax.axis_size("chan")
    block_tokens = owned_rows * count_hist
    period = local_rows + block_tokens
    next_taps = shifted(filter_taps, "hist", -1)
    extended = jnp.concatenate([filter_taps, next_taps], 0)
    scale = 2.0 * math.pi / period
    modes = lax.broadcasted_iota(jnp.int32, (period, period), 0)
    places = lax.broadcasted_iota(jnp.int32, (period, period), 1)
    angles = (modes * places % period).astype(jnp.float32) * scale
    table = jnp.concatenate([jnp.cos(angles), jnp.sin(angles)], 0)
    table_high = table.astype(jnp.bfloat16)
    table_low = (table - table_high.astype(jnp.float32)).astype(jnp.bfloat16)
    spec_taps = split_product(table_high, table_low, extended)
    spec_input = split_product(table_high[:, :local_rows], table_low[:, :local_rows], history)
    taps_cos, taps_sin = (spec_taps[:period], spec_taps[period:])
    input_cos, input_sin = (spec_input[:period], spec_input[period:])
    real_part = taps_cos * input_cos + taps_sin * input_sin
    imag_part = taps_cos * input_sin - taps_sin * input_cos
    conv = lax.psum_scatter(
        inverse_part(
            real_part, imag_part, block_tokens, period, owned_rows * lax.axis_size("hist")
        ),
        "hist",
        scatter_dimension=0,
        tiled=True,
    )
    gated = (conv * gate_values.astype(jnp.float32)).astype(jnp.bfloat16)
    partial_value = jnp.dot(
        lax.all_gather(gated, "hist", axis=0, tiled=True),
        out_weight,
        preferred_element_type=jnp.float32,
    )
    columns = partial_value.shape[1]
    half_rows = owned_rows // count_chan
    ordered = partial_value.reshape(count_hist, count_chan, half_rows, columns).transpose(
        1, 0, 2, 3
    )
    ordered = ordered.reshape(count_chan * count_hist * half_rows, columns)
    summed = lax.psum_scatter(ordered.astype(jnp.bfloat16), "chan", scatter_dimension=0, tiled=True)
    output = lax.all_to_all(summed, "hist", split_axis=0, concat_axis=1, tiled=True)
    return output


def solution(mesh):
    return jax.shard_map(
        local,
        mesh=mesh,
        in_specs=(
            P(("seq", "hist"), "chan"),
            P("hist", "chan"),
            P(("seq", "hist"), "chan"),
            P("chan", "hist"),
        ),
        out_specs=P(("seq", "hist", "chan"), None),
        check_vma=False,
    )
```

profile of v0, /device:TPU:0, one launch (start us, length us, event | category | flops | bytes accessed | tf_op | source)
XLA Modules:
  0.0 194.0 jit_solution(3666349346221288854)
XLA Ops:
  6.5 1.5 collective-permute-start
  8.1 4.1 %fusion.36 = (f32[512,512]{1,0:T(8,128)S(1)}, f32[512,512]{1,0:T(8,128)S(1)}) fusion(), kind=kLoop, calls=%fused_computation.43 | loop fusion | flops 3670016 | bytes 2097152 | tf_op jit(solution)/shard_map/sin | solution.py:53
  12.2 0.3 subtract_convert_fusion
  12.5 0.1 fusion.22
  12.6 1.3 fusion.33
  13.9 0.1 constant_dynamic-update-slice_fusion.1
  14.0 1.4 convolution_add_fusion
  15.5 19.6 %collective-permute-done = bf16[256,2048]{1,0:T(8,128)(2,1)S(1)} collective-permute-done((bf16[256,2048]{1,0:T(8,128)(2,1)}, bf16[256,2048]{1,0:T(8,128)(2,1)S(1)}, u32[]{:S(2)}, u32[]{:S(2)}) %collective-permute-start) | collective-permute-done | bytes 1048608 | tf_op jit(solution)/shard_map/ppermute | solution.py:12
  35.0 0.1 constant_dynamic-update-slice_fusion
  35.1 2.4 %fusion.53 = f32[1024,2048]{1,0:T(8,128)S(1)} fusion(bf16[1024,512]{1,0:T(8,128)(2,1)S(1)} %subtract_convert_fusion, bf16[512,2048]{1,0:T(8,128)(2,1)S(1)} %constant_dynamic-update-slice_fusion), kind=kOutput, calls=%fused_computation.61 | convolution fusion | flops 2147483648 | bytes 11534336 | tf_op jit(solution)/shard_map/dot_general | solution.py:17
  37.5 2.4 %convolution_add_fusion.1 = f32[1024,2048]{1,0:T(8,128)S(1)} fusion(f32[1024,2048]{1,0:T(8,128)S(1)} %fusion.53, bf16[512,2048]{1,0:T(8,128)(2,1)S(1)} %constant_dynamic-update-slice_fusion, f32[512,512]{1,0:T(8,128)S(1)} %get-tuple-element.5, f32[512,512]{1,0:T(8,128)S(1)} %get-tuple-element.6), kind=kOutput, calls=%fused_computation.17 | convolution fusion | flops 2151677952 | bytes 20971520 | tf_op jit(solution)/shard_map/dot_general | solution.py:16
  39.9 6.2 %fusion = f32[256,2048]{1,0:T(8,128)S(1)} fusion(f32[1024,2048]{1,0:T(8,128)S(1)} %convolution_add_fusion, f32[1024,2048]{1,0:T(8,128)S(1)} %convolution_add_fusion.1, s32[256]{0:T(256)S(1)} %iota_subtract_fusion), kind=kOutput, calls=%fused_computation.1 | convolution fusion | flops 3226206208 | bytes 18875392 | tf_op jit(solution)/shard_map/dot_general | solution.py:31
  46.1 7.4 %fusion.19 = f32[256,2048]{1,0:T(8,128)} fusion(f32[256,2048]{1,0:T(8,128)S(1)} %fusion, f32[1024,2048]{1,0:T(8,128)S(1)} %convolution_add_fusion, f32[1024,2048]{1,0:T(8,128)S(1)} %convolution_add_fusion.1, s32[256]{0:T(256)S(1)} %iota_subtract_fusion), kind=kOutput, calls=%fused_computation.19 | convolution fusion | flops 3227254784 | bytes 20972544 | tf_op jit(solution)/shard_map/dot_general | solution.py:25
  53.6 0.0 reduce-scatter.3.cloned.1.call-update
  53.6 0.0 all-gather.2.cloned.1.call-start
  53.6 69.3 %reduce-scatter.3.cloned.1.call-done = f32[32,2048]{1,0:T(8,128)} async-done(((f32[256,2048]{1,0:T(8,128)}), f32[32,2048]{1,0:T(8,128)}) %reduce-scatter.3.cloned.1.call-update) | async-done | bytes 262160 | tf_op jit(solution)/shard_map/reduce_scatter | solution.py:62
  122.9 1.6 multiply_convert_fusion
  124.6 0.0 reduce-scatter.5.cloned.1.call-start
  124.6 39.7 %all-gather.2.cloned.1.call-done = bf16[256,2048]{1,0:T(8,128)(2,1)} async-done(((bf16[32,2048]{1,0:T(8,128)(2,1)}), bf16[256,2048]{1,0:T(8,128)(2,1)}) %all-gather.2.cloned.1.call-update) | async-done | bytes 1048592 | tf_op jit(solution)/shard_map/all_gather | solution.py:72
  164.3 1.9 convolution_convert_fusion
  166.3 0.7 copy.6
  167.0 6.6 %reduce-scatter.5.cloned.1.call-done = bf16[128,512]{1,0:T(8,128)(2,1)} async-done(((bf16[256,512]{1,0:T(8,128)(2,1)}), bf16[128,512]{1,0:T(8,128)(2,1)}) %reduce-scatter.5.cloned.1.call-update) | async-done | bytes 131088 | tf_op jit(solution)/shard_map/reduce_scatter | solution.py:82
  173.6 13.2 %all_to_all.19 = bf16[8,16,512]{2,1,0:T(8,128)(2,1)S(1)} all-to-all(bf16[8,16,512]{2,1,0:T(8,128)(2,1)} %bitcast.18), channel_id=1, replica_groups=mesh['seq'=2,'hist'=8,'chan'=2] {'hist'}, dimensions={0} | all-to-all | bytes 262144 | tf_op jit(solution)/shard_map/all_to_all | solution.py:83
  186.8 0.7 copy.8
  (12 shorter events, 0.1 us)
Async XLA Ops:
  6.5 157.8 %copy-start = (bf16[2048,512]{1,0:T(8,128)(2,1)S(1)}, bf16[2048,512]{1,0:T(8,128)(2,1)}, u32[]{:S(2)}) copy-start(bf16[2048,512]{1,0:T(8,128)(2,1)} %param.7) | copy-start | bytes 6291460
  6.5 6.1 %copy-start.1 = (bf16[256,2048]{1,0:T(8,128)(2,1)S(1)}, bf16[256,2048]{1,0:T(8,128)(2,1)}, u32[]{:S(2)}) copy-start(bf16[256,2048]{1,0:T(8,128)(2,1)} %param.4) | copy-start | bytes 3145732
  6.5 116.4 %reduce-scatter.3.cloned.1.call-start = ((), (), s32[]{:S(2)}) async-start(), calls=%async_computation.3 | async-start | bytes 2359296 | tf_op jit(solution)/shard_map/reduce_scatter | solution.py:62
  6.5 28.5 %collective-permute-start = (bf16[256,2048]{1,0:T(8,128)(2,1)}, bf16[256,2048]{1,0:T(8,128)(2,1)S(1)}, u32[]{:S(2)}, u32[]{:S(2)}) collective-permute-start(bf16[256,2048]{1,0:T(8,128)(2,1)} %param.5), channel_id=1, source_target_pairs={{2,0},{4,2},{6,4},{8,6},{10,8},{12,10},{14,12},{3,1},{5,3},{7,5},{... | collective-permute-start | bytes 3145736 | tf_op jit(solution)/shard_map/ppermute | solution.py:12
  12.6 1.3 copy-start.2
  46.1 76.8 %copy-start.3 = (bf16[32,2048]{1,0:T(8,128)(2,1)S(1)}, bf16[32,2048]{1,0:T(8,128)(2,1)}, u32[]{:S(2)}) copy-start(bf16[32,2048]{1,0:T(8,128)(2,1)} %param.6) | copy-start | bytes 393220
  53.6 110.7 %all-gather.2.cloned.1.call-start = ((), (), s32[]{:S(2)}) async-start(), calls=%async_computation.4 | async-start | bytes 1179648 | tf_op jit(solution)/shard_map/all_gather | solution.py:72
  124.6 49.0 %reduce-scatter.5.cloned.1.call-start = ((), (), s32[]{:S(2)}) async-start(), calls=%async_computation.5 | async-start | bytes 393216 | tf_op jit(solution)/shard_map/reduce_scatter | solution.py:82
Sparse Core Ops, SparseCore 0:
  53.7 69.1 reduce-scatter.2
  125.1 39.2 all-gather.1
  167.1 6.4 reduce-scatter.4
where the time goes:
time: 194 us
  waiting for transfers between devices  135 us (70%)
  matrix products  23 us (12%)
  blocking collectives  13.2 us (7%)
  between operations  13.2 us (7%)
  other arithmetic  6.15 us (3%)
    reduce_scatter x1, waiting for transfers between devices, local(): lax.psum_scatter(inverse_part(real_part, imag_part, block_tokens, period,...  69.3 us
    all_gather x1, waiting for transfers between devices, local(): lax.all_gather(gated, 'hist', axis=0, tiled=True)  39.7 us
    ppermute x1, waiting for transfers between devices, shifted(): lax.ppermute(value, axis, [(source, source + steps) for source in range(i...  19.6 us
    all_to_all x1, blocking collectives, local(): lax.all_to_all(summed, 'hist', split_axis=0, concat_axis=1, tiled=True)  13.2 us
    dot_general x1, matrix products, inverse_part(): jnp.dot(jnp.cos(phases), real_part, precision=lax.Precision.HIGHEST, pref...  7.43 us
    reduce_scatter x1, waiting for transfers between devices, local(): lax.psum_scatter(ordered.astype(jnp.bfloat16), 'chan', scatter_dimension=...  6.58 us
    dot_general x1, matrix products, inverse_part(): jnp.dot(jnp.sin(phases), imag_part, precision=lax.Precision.HIGHEST, pref...  6.21 us
    sin x1, other arithmetic, local(): table = jnp.concatenate([jnp.cos(angles), jnp.sin(angles)], 0)  4.09 us
  transfers between devices with their start and end apart: 4, of which 4 were waited for; matrix products, arithmetic and copies ran while one was open for 4% of the time, Pallas kernels for 0%

commit v1 on v0

v1 whole, which is shorter than its diff:
```python
import numpy as np

import jax
import jax.numpy as jnp
from jax import lax
from jax.sharding import PartitionSpec as P

BF16 = jnp.bfloat16
F32 = jnp.float32


def halves(values):
    high = values.astype(jnp.bfloat16)
    return high, (values - high.astype(np.float32)).astype(jnp.bfloat16)


def tables(rows, tokens):
    period = rows + tokens
    orders = 2 * np.arange(period // 2)[:, None] + 1
    angles = (orders * np.arange(rows)[None, :] % (2 * period)) * (np.pi / period)
    forward = np.concatenate([np.cos(angles), np.sin(angles)], 0).astype(np.float32)
    lags = tokens - 1 - np.arange(tokens)
    angles = (orders.T * lags[:, None] % (2 * period)) * (np.pi / period)
    inverse = np.concatenate([np.cos(angles), -np.sin(angles)], 1).astype(np.float32)
    inverse = inverse * np.float32(2.0 / period)
    turn = ((orders * rows) % (2 * period)) * (np.pi / period)
    return halves(forward), halves(inverse), np.cos(turn).astype(np.float32), np.sin(turn).astype(np.float32)


def local(history, filter_taps, gate_values, out_weight):
    rows, channels = history.shape
    owned = gate_values.shape[0]
    seqs, hists, chans = (lax.axis_size(a) for a in ("seq", "hist", "chan"))
    tokens = owned * hists
    px = 2 if seqs % 2 == 0 else 1
    py = 2 if hists % 2 == 0 else 1
    nz = hists // py
    wide = channels // py
    quarter = wide // px
    group = tokens // nz
    sx = lax.axis_index("seq") % px
    y = lax.axis_index("hist") % py
    z = lax.axis_index("hist") // py

    def move(value, dx=0, dz=0, dy=0, wrap=True):
        pairs = []
        for s in range(seqs):
            for h in range(hists):
                to_z = h // py + dz
                if not wrap and not 0 <= to_z < nz:
                    continue
                target = (s ^ dx) * hists + (to_z % nz) * py + ((h % py) ^ dy)
                pairs.append((s * hists + h, target))
        return lax.ppermute(value, ("seq", "hist"), pairs)

    def cut(value, dx, dy):
        start = (y ^ dy) * wide + (sx ^ dx) * quarter
        return lax.dynamic_slice_in_dim(value, start, quarter, 1)

    def ordered(index, values):
        if len(values) == 1:
            return values
        first, second = values
        return [jnp.where(index == 0, first, second), jnp.where(index == 0, second, first)]

    (fwd_high, fwd_low), (inv_high, inv_low), turn_cos, turn_sin = tables(rows, tokens)
    modes = fwd_high.shape[0] // 2

    own_taps = cut(filter_taps, 0, 0)
    pieces = [own_taps] + [move(cut(filter_taps, 0, dy), dy=dy) for dy in range(1, py)]
    taps = ordered(y, pieces)
    taps.append(move(taps[0], dz=-1, wrap=False))

    inputs = []
    for dx in range(px):
        blocks = []
        for dy in range(py):
            piece = cut(history, dx, dy)
            blocks.append(piece if dx == dy == 0 else move(piece, dx=dx, dy=dy))
        inputs.append(ordered(y, blocks))

    gates = [lax.dynamic_slice_in_dim(gate_values, (y ^ dy) * wide, wide, 1) for dy in range(py)]
    gates = ordered(y, [gates[0]] + [move(gates[dy], dy=dy) for dy in range(1, py)])
    gate = jnp.concatenate(gates, 0).astype(F32)

    def transform(block):
        out = jnp.dot(fwd_high, block, preferred_element_type=F32)
        out = out + jnp.dot(fwd_low, block, preferred_element_type=F32)
        return out[:modes], out[modes:]

    own_spec = [transform(block) for block in taps]
    contributions = []
    spec = []
    for j in range(py):
        (a, b), (c, d) = own_spec[j], own_spec[j + 1]
        spec.append((a + turn_cos * c - turn_sin * d, b + turn_cos * d + turn_sin * c))
    for dx in range(px):
        real, imag = 0.0, 0.0
        for j in range(py):
            (tc, ts), (ic, is_) = spec[j], transform(inputs[dx][j])
            real = real + tc * ic + ts * is_
            imag = imag + tc * is_ - ts * ic
        product = jnp.concatenate([real, imag], 0)
        high = product.astype(BF16)
        low = (product - high.astype(F32)).astype(BF16)
        conv = jnp.dot(inv_high, high, preferred_element_type=F32)
        conv = conv + jnp.dot(inv_high, low, preferred_element_type=F32)
        conv = conv + jnp.dot(inv_low, high, preferred_element_type=F32)
        contributions.append(conv)

    sums = []
    for dx in range(px):
        total = 0.0
        for dz in range(nz):
            part = lax.dynamic_slice_in_dim(contributions[dx], (z + dz) % nz * group, group, 0)
            if dx or dz:
                part = move(part.astype(BF16), dx=dx, dz=dz).astype(F32)
            total = total + part
        sums.append(total)
    conv = jnp.concatenate(ordered(sx, sums), 1)
    gated = (conv * gate).astype(BF16)

    along = [gated] + [move(gated, dz=-dz) for dz in range(1, nz)]
    total = 0.0
    for dy in range(py):
        across = [move(v, dy=dy) if dy else v for v in along]
        weight = lax.dynamic_slice_in_dim(out_weight, (y ^ dy) * wide, wide, 0)
        total = total + jnp.dot(jnp.concatenate(across, 0), weight, preferred_element_type=F32)
    total = total.astype(BF16).reshape(nz, group, -1)
    total = jnp.roll(total, z, axis=0).reshape(tokens, -1)
    final = lax.all_to_all(total, ("hist", "chan"), split_axis=0, concat_axis=0, tiled=True)
    share = owned // chans
    final = final.reshape(hists, chans, share, -1).astype(F32).sum(1).astype(BF16)
    return final.transpose(1, 0, 2).reshape(share, -1)


def solution(mesh):
    return jax.shard_map(
        local,
        mesh=mesh,
        in_specs=(
            P(("seq", "hist"), "chan"),
            P("hist", "chan"),
            P(("seq", "hist"), "chan"),
            P("chan", "hist"),
        ),
        out_specs=P(("seq", "hist", "chan"), None),
        check_vma=False,
    )
```

time: 194 us -> 81.8 us (0.42)
  waiting for transfers between devices: 135 us -> 24 us
  starting transfers between devices: 1.63 us -> 25.1 us
  matrix products: 23 us -> 8.94 us
  between operations: 13.2 us -> 0.36 us
  local copies, waits for them, and re-layouts: 1.6 us -> 5.84 us
  other arithmetic: 6.15 us -> 3.48 us
    reduce_scatter x2 -> x0, waiting for transfers between devices: 75.9 us -> none  [the longest x1 69.3 us: local(): lax.psum_scatter(inverse_part(real_part, imag_part, block_tokens, period,...]
    all_gather x1 -> x0, waiting for transfers between devices: 39.7 us -> none  [local(): lax.all_gather(gated, 'hist', axis=0, tiled=True)]
    ppermute x1 -> x20, starting transfers between devices: 1.54 us -> 25.1 us  [move(): return lax.ppermute(value, ('seq', 'hist'), pairs)]
    dot_general x7 -> x22, matrix products: 23 us -> 8.94 us  [the longest x7 3.13 us: transform(): out = jnp.dot(fwd_high, block, preferred_element_type=F32)]
    dynamic_slice x0 -> x3, local copies, waits for them, and re-layouts: none -> 4.53 us  [the longest x2 3.9 us: cut(): return lax.dynamic_slice_in_dim(value, start, quarter, 1)]
    ppermute x1 -> x20, waiting for transfers between devices: 19.6 us -> 24 us  [move(): return lax.ppermute(value, ('seq', 'hist'), pairs)]
    sin x1 -> x0, other arithmetic: 4.09 us -> none  [local(): table = jnp.concatenate([jnp.cos(angles), jnp.sin(angles)], 0)]
    convert_element_type x3 -> x1, other arithmetic: 2.05 us -> 0.04 us  [local(): gated = (conv * gate).astype(BF16)]
  transfers between devices with their start and end apart: 4 -> 20, of which waited for: 4 -> 9; matrix products, arithmetic and copies ran while one was open for 4% -> 18% of each run, Pallas kernels for 0% -> 0%
where the time goes in v1:
time: 81.8 us; the launch traced here: 81.4 us
  starting transfers between devices  25.1 us (31%)
  waiting for transfers between devices  24 us (29%)
  blocking collectives  13.6 us (17%)
  matrix products  8.94 us (11%)
  local copies, waits for them, and re-layouts  5.84 us (7%)
  other arithmetic  3.48 us (4%)
    ppermute x20, starting transfers between devices, move(): return lax.ppermute(value, ('seq', 'hist'), pairs)  25.1 us
    ppermute x20, waiting for transfers between devices, move(): return lax.ppermute(value, ('seq', 'hist'), pairs)  24 us
    all_to_all x1, blocking collectives, local(): lax.all_to_all(total, ('hist', 'chan'), split_axis=0, concat_axis=0, tile...  13.6 us
    dynamic_slice x2, local copies, waits for them, and re-layouts, cut(): return lax.dynamic_slice_in_dim(value, start, quarter, 1)  3.9 us
    dot_general x7, matrix products, transform(): out = jnp.dot(fwd_high, block, preferred_element_type=F32)  3.13 us
    dot_general x7, matrix products, transform(): out = out + jnp.dot(fwd_low, block, preferred_element_type=F32)  3.11 us
    select_n x3, other arithmetic, ordered(): jnp.where(index == 0, first, second)  1.95 us
  transfers between devices with their start and end apart: 20, of which 9 were waited for; matrix products, arithmetic and copies ran while one was open for 18% of the time, Pallas kernels for 0%

profile of v1, /device:TPU:0, one launch (start us, length us, event | category | flops | bytes accessed | tf_op | source)
XLA Modules:
  0.0 81.4 jit_solution(2292098172019051868)
XLA Ops:
  0.0 1.8 %constant_dynamic-slice_fusion.4 = bf16[256,512]{1,0:T(8,128)(2,1)} fusion(bf16[256,2048]{1,0:T(8,128)(2,1)} %param.11, s32[]{:T(128)S(6)} %select_n.144), kind=kLoop, calls=%fused_computation.106 | loop fusion | bytes 524292 | tf_op jit(solution)/shard_map/dynamic_slice | solution.py:58
  1.8 3.0 %collective-permute-start = (bf16[256,512]{1,0:T(8,128)(2,1)}, bf16[256,512]{1,0:T(8,128)(2,1)}, u32[]{:S(2)}, u32[]{:S(2)}) collective-permute-start(bf16[256,512]{1,0:T(8,128)(2,1)} %constant_dynamic-slice_fusion.4), channel_id=1, source_target_pairs={{0,2},{2,0},{4,6},{6,4},{8,10},{10,8},{12,14},{14,12},{16,18},{18,... | collective-permute-start | bytes 786440 | tf_op jit(solution)/shard_map/ppermute | solution.py:54
  4.9 2.1 %constant_dynamic-slice_fusion.2 = (bf16[256,512]{1,0:T(8,128)(2,1)}, bf16[256,512]{1,0:T(8,128)(2,1)}, bf16[256,512]{1,0:T(8,128)(2,1)}) fusion(bf16[256,2048]{1,0:T(8,128)(2,1)} %param.10, s32[]{:T(128)S(6)} %select_n.158, s32[]{:T(128)S(6)} %select_n.144, s32[]{:T(128)S(6)} %select_n.159), kind=kLoop, calls=%fused_computation.103 | loop fusion | bytes 1572876 | tf_op jit(solution)/shard_map/dynamic_slice | solution.py:58
  6.9 3.0 %collective-permute-start.7 = (bf16[256,512]{1,0:T(8,128)(2,1)}, bf16[256,512]{1,0:T(8,128)(2,1)S(1)}, u32[]{:S(2)}, u32[]{:S(2)}) collective-permute-start(bf16[256,512]{1,0:T(8,128)(2,1)} %get-tuple-element.15), channel_id=1, source_target_pairs={{0,18},{2,16},{4,22},{6,20},{8,26},{10,24},{12,30},{14,28},{16,2},... | collective-permute-start | bytes 786440 | tf_op jit(solution)/shard_map/ppermute | solution.py:54
  11.1 6.8 %collective-permute-done = bf16[256,512]{1,0:T(8,128)(2,1)} collective-permute-done((bf16[256,512]{1,0:T(8,128)(2,1)}, bf16[256,512]{1,0:T(8,128)(2,1)}, u32[]{:S(2)}, u32[]{:S(2)}) %collective-permute-start) | collective-permute-done | bytes 262176 | tf_op jit(solution)/shard_map/ppermute | solution.py:54
  17.9 1.0 %broadcast_select_fusion.5 = bf16[256,512]{1,0:T(8,128)(2,1)S(1)} fusion(bf16[256,512]{1,0:T(8,128)(2,1)} %collective-permute-done, pred[]{:T(512)S(6)} %eq.29, bf16[256,2048]{1,0:T(8,128)(2,1)} %param.11, s32[]{:T(128)S(6)} %select_n.143), kind=kLoop, calls=%fused_computation.64 | loop fusion | flops 131072 | bytes 786437 | tf_op jit(solution)/shard_map/jit(_where)/select_n | solution.py:64
  19.0 1.4 %collective-permute-start.2 = (bf16[256,512]{1,0:T(8,128)(2,1)S(1)}, bf16[256,512]{1,0:T(8,128)(2,1)S(1)}, u32[]{:S(2)}, u32[]{:S(2)}) collective-permute-start(bf16[256,512]{1,0:T(8,128)(2,1)S(1)} %broadcast_select_fusion.5), channel_id=1, source_target_pairs={{4,0},{6,2},{8,4},{10,6},{12,8},{14,10},{20,16},{22,18},{24,20},{2... | collective-permute-start | bytes 786440 | tf_op jit(solution)/shard_map/ppermute | solution.py:54
  21.0 2.3 %collective-permute-done.1 = bf16[256,512]{1,0:T(8,128)(2,1)S(1)} collective-permute-done((bf16[256,512]{1,0:T(8,128)(2,1)}, bf16[256,512]{1,0:T(8,128)(2,1)S(1)}, u32[]{:S(2)}, u32[]{:S(2)}) %collective-permute-start.1) | collective-permute-done | bytes 262176 | tf_op jit(solution)/shard_map/ppermute | solution.py:54
  24.0 1.3 %fusion.43 = f32[512,512]{0,1:T(8,128)S(1)} fusion(bf16[512,256]{1,0:T(8,128)(2,1)S(1)} %copy-done.1, bf16[256,512]{1,0:T(8,128)(2,1)} %collective-permute-done, pred[]{:T(512)S(6)} %eq.29, bf16[256,2048]{1,0:T(8,128)(2,1)S(1)} %copy-done.5, s32[]{:T(128)S(6)} %select_n.143), kind=kOutput, calls=%fused_computation.80 | convolution fusion | flops 134348800 | bytes 1835013 | tf_op jit(solution)/shard_map/dot_general | solution.py:88
  27.2 1.3 %fusion.5 = f32[512,512]{1,0:T(8,128)S(1)} fusion(f32[512,512]{0,1:T(8,128)S(1)} %fusion.43, bf16[512,256]{1,0:T(8,128)(2,1)S(1)} %copy-done.2, bf16[256,512]{1,0:T(8,128)(2,1)} %collective-permute-done, pred[]{:T(512)S(6)} %eq.29, bf16[256,2048]{1,0:T(8,128)(2,1)S(1)} %copy-done.5, s32[]{:T(128)S(6)} %select_n.143), kind=kOutput, calls=%fused_computation.11 | convolution fusion | flops 134610944 | bytes 2883589 | tf_op jit(solution)/shard_map/dot_general | solution.py:87
  32.0 4.8 %collective-permute-start.11 = (bf16[64,512]{1,0:T(8,128)(2,1)S(1)}, bf16[64,512]{1,0:T(8,128)(2,1)S(1)}, u32[]{:S(2)}, u32[]{:S(2)}) collective-permute-start(bf16[64,512]{1,0:T(8,128)(2,1)S(1)} %get-tuple-element.22), channel_id=1, source_target_pairs={{0,28},{2,30},{4,16},{6,18},{8,20},{10,22},{12,24},{14,26},{16,12}... | collective-permute-start | bytes 196616 | tf_op jit(solution)/shard_map/ppermute | solution.py:54
  36.8 1.9 %collective-permute-start.9 = (bf16[64,512]{1,0:T(8,128)(2,1)S(1)}, bf16[64,512]{1,0:T(8,128)(2,1)S(1)}, u32[]{:S(2)}, u32[]{:S(2)}) collective-permute-start(bf16[64,512]{1,0:T(8,128)(2,1)S(1)} %get-tuple-element.24), channel_id=1, source_target_pairs={{0,20},{2,22},{4,24},{6,26},{8,28},{10,30},{12,16},{14,18},{16,4},... | collective-permute-start | bytes 196616 | tf_op jit(solution)/shard_map/ppermute | solution.py:54
  40.2 2.9 %collective-permute-start.5 = (bf16[64,512]{1,0:T(8,128)(2,1)S(1)}, bf16[64,512]{1,0:T(8,128)(2,1)S(1)}, u32[]{:S(2)}, u32[]{:S(2)}) collective-permute-start(bf16[64,512]{1,0:T(8,128)(2,1)S(1)} %get-tuple-element.19), channel_id=1, source_target_pairs={{0,12},{2,14},{4,0},{6,2},{8,4},{10,6},{12,8},{14,10},{16,28},{18,... | collective-permute-start | bytes 196616 | tf_op jit(solution)/shard_map/ppermute | solution.py:54
  43.1 1.1 %collective-permute-start.4 = (bf16[64,512]{1,0:T(8,128)(2,1)S(1)}, bf16[64,512]{1,0:T(8,128)(2,1)S(1)}, u32[]{:S(2)}, u32[]{:S(2)}) collective-permute-start(bf16[64,512]{1,0:T(8,128)(2,1)S(1)} %get-tuple-element.20), channel_id=1, source_target_pairs={{0,8},{2,10},{4,12},{6,14},{8,0},{10,2},{12,4},{14,6},{16,24},{18,... | collective-permute-start | bytes 196616 | tf_op jit(solution)/shard_map/ppermute | solution.py:54
  45.7 2.6 %collective-permute-done.4 = bf16[64,512]{1,0:T(8,128)(2,1)S(1)} collective-permute-done((bf16[64,512]{1,0:T(8,128)(2,1)S(1)}, bf16[64,512]{1,0:T(8,128)(2,1)S(1)}, u32[]{:S(2)}, u32[]{:S(2)}) %collective-permute-start.4) | collective-permute-done | bytes 65568 | tf_op jit(solution)/shard_map/ppermute | solution.py:54
  48.3 2.0 %collective-permute-done.3 = bf16[64,512]{1,0:T(8,128)(2,1)S(1)} collective-permute-done((bf16[64,512]{1,0:T(8,128)(2,1)S(1)}, bf16[64,512]{1,0:T(8,128)(2,1)S(1)}, u32[]{:S(2)}, u32[]{:S(2)}) %collective-permute-start.3) | collective-permute-done | bytes 65568 | tf_op jit(solution)/shard_map/ppermute | solution.py:54
  50.5 1.1 %collective-permute-start.14 = (bf16[64,1024]{1,0:T(8,128)(2,1)S(1)}, bf16[64,1024]{1,0:T(8,128)(2,1)S(1)}, u32[]{:S(2)}, u32[]{:S(2)}) collective-permute-start(bf16[64,1024]{1,0:T(8,128)(2,1)S(1)} %fusion.30), channel_id=1, source_target_pairs={{0,8},{2,10},{4,12},{6,14},{8,0},{10,2},{12,4},{14,6},{16,24},{18,... | collective-permute-start | bytes 393224 | tf_op jit(solution)/shard_map/ppermute | solution.py:54
  51.6 2.7 %collective-permute-start.13 = (bf16[64,1024]{1,0:T(8,128)(2,1)S(1)}, bf16[64,1024]{1,0:T(8,128)(2,1)S(1)}, u32[]{:S(2)}, u32[]{:S(2)}) collective-permute-start(bf16[64,1024]{1,0:T(8,128)(2,1)S(1)} %fusion.30), channel_id=1, source_target_pairs={{0,12},{2,14},{4,0},{6,2},{8,4},{10,6},{12,8},{14,10},{16,28},{18,... | collective-permute-start | bytes 393224 | tf_op jit(solution)/shard_map/ppermute | solution.py:54
  54.3 3.1 %collective-permute-done.15 = bf16[64,1024]{1,0:T(8,128)(2,1)S(1)} collective-permute-done((bf16[64,1024]{1,0:T(8,128)(2,1)S(1)}, bf16[64,1024]{1,0:T(8,128)(2,1)S(1)}, u32[]{:S(2)}, u32[]{:S(2)}) %collective-permute-start.15) | collective-permute-done | bytes 131104 | tf_op jit(solution)/shard_map/ppermute | solution.py:54
  57.4 2.7 %collective-permute-done.14 = bf16[64,1024]{1,0:T(8,128)(2,1)S(1)} collective-permute-done((bf16[64,1024]{1,0:T(8,128)(2,1)S(1)}, bf16[64,1024]{1,0:T(8,128)(2,1)S(1)}, u32[]{:S(2)}, u32[]{:S(2)}) %collective-permute-start.14) | collective-permute-done | bytes 131104 | tf_op jit(solution)/shard_map/ppermute | solution.py:54
  60.1 2.0 %collective-permute-start.17 = (bf16[64,1024]{1,0:T(8,128)(2,1)S(1)}, bf16[64,1024]{1,0:T(8,128)(2,1)S(1)}, u32[]{:S(2)}, u32[]{:S(2)}) collective-permute-start(bf16[64,1024]{1,0:T(8,128)(2,1)S(1)} %collective-permute-done.13), channel_id=1, source_target_pairs={{0,2},{2,0},{4,6},{6,4},{8,10},{10,8},{12,14},{14,12},{16,18},{18,... | collective-permute-start | bytes 393224 | tf_op jit(solution)/shard_map/ppermute | solution.py:54
  62.6 2.5 %collective-permute-done.18 = bf16[64,1024]{1,0:T(8,128)(2,1)S(1)} collective-permute-done((bf16[64,1024]{1,0:T(8,128)(2,1)S(1)}, bf16[64,1024]{1,0:T(8,128)(2,1)S(1)}, u32[]{:S(2)}, u32[]{:S(2)}) %collective-permute-start.18) | collective-permute-done | bytes 131104 | tf_op jit(solution)/shard_map/ppermute | solution.py:54
  65.1 1.4 %collective-permute-done.17 = bf16[64,1024]{1,0:T(8,128)(2,1)S(1)} collective-permute-done((bf16[64,1024]{1,0:T(8,128)(2,1)S(1)}, bf16[64,1024]{1,0:T(8,128)(2,1)S(1)}, u32[]{:S(2)}, u32[]{:S(2)}) %collective-permute-start.17) | collective-permute-done | bytes 131104 | tf_op jit(solution)/shard_map/ppermute | solution.py:54
  67.0 13.6 %all_to_all.9 = bf16[16,16,512]{2,1,0:T(8,128)(2,1)S(1)} all-to-all(bf16[16,16,512]{2,1,0:T(8,128)(2,1)S(1)} %bitcast.69), channel_id=1, replica_groups=mesh['seq'=2,'hist'=8,'chan'=2] {'hist','chan'}, dimensions={0} | all-to-all | bytes 524288 | tf_op jit(solution)/shard_map/all_to_all | solution.py:131
  (73 shorter events, 12.6 us)
Async XLA Ops:
  0.0 62.1 %copy-start = (bf16[2048,512]{1,0:T(8,128)(2,1)S(1)}, bf16[2048,512]{1,0:T(8,128)(2,1)}, u32[]{:S(2)}) copy-start(bf16[2048,512]{1,0:T(8,128)(2,1)} %param.13) | copy-start | bytes 6291460
  0.0 20.4 %copy-start.1 = (bf16[512,256]{1,0:T(8,128)(2,1)S(1)}, bf16[512,256]{1,0:T(8,128)(2,1)}, u32[]{:S(2)}) copy-start(bf16[512,256]{1,0:T(8,128)(2,1)} %constant.111.clone) | copy-start | bytes 786436
  0.0 10.4 %copy-start.7 = (bf16[32,2048]{1,0:T(8,128)(2,1)S(1)}, bf16[32,2048]{1,0:T(8,128)(2,1)}, u32[]{:S(2)}) copy-start(bf16[32,2048]{1,0:T(8,128)(2,1)} %param.12) | copy-start | bytes 393220
  1.8 16.1 %collective-permute-start = (bf16[256,512]{1,0:T(8,128)(2,1)}, bf16[256,512]{1,0:T(8,128)(2,1)}, u32[]{:S(2)}, u32[]{:S(2)}) collective-permute-start(bf16[256,512]{1,0:T(8,128)(2,1)} %constant_dynamic-slice_fusion.4), channel_id=1, source_target_pairs={{0,2},{2,0},{4,6},{6,4},{8,10},{10,8},{12,14},{14,12},{16,18},{18,... | collective-permute-start | bytes 786440 | tf_op jit(solution)/shard_map/ppermute | solution.py:54
  4.9 15.8 %copy-start.2 = (bf16[512,256]{1,0:T(8,128)(2,1)S(1)}, bf16[512,256]{1,0:T(8,128)(2,1)}, u32[]{:S(2)}) copy-start(bf16[512,256]{1,0:T(8,128)(2,1)} %constant.110.clone) | copy-start | bytes 786436
  6.9 16.4 %collective-permute-start.1 = (bf16[256,512]{1,0:T(8,128)(2,1)}, bf16[256,512]{1,0:T(8,128)(2,1)S(1)}, u32[]{:S(2)}, u32[]{:S(2)}) collective-permute-start(bf16[256,512]{1,0:T(8,128)(2,1)} %get-tuple-element.14), channel_id=1, source_target_pairs={{0,2},{2,0},{4,6},{6,4},{8,10},{10,8},{12,14},{14,12},{16,18},{18,... | collective-permute-start | bytes 786440 | tf_op jit(solution)/shard_map/ppermute | solution.py:54
  6.9 18.3 %collective-permute-start.7 = (bf16[256,512]{1,0:T(8,128)(2,1)}, bf16[256,512]{1,0:T(8,128)(2,1)S(1)}, u32[]{:S(2)}, u32[]{:S(2)}) collective-permute-start(bf16[256,512]{1,0:T(8,128)(2,1)} %get-tuple-element.15), channel_id=1, source_target_pairs={{0,18},{2,16},{4,22},{6,20},{8,26},{10,24},{12,30},{14,28},{16,2},... | collective-permute-start | bytes 786440 | tf_op jit(solution)/shard_map/ppermute | solution.py:54
  9.9 15.4 %collective-permute-start.6 = (bf16[256,512]{1,0:T(8,128)(2,1)}, bf16[256,512]{1,0:T(8,128)(2,1)S(1)}, u32[]{:S(2)}, u32[]{:S(2)}) collective-permute-start(bf16[256,512]{1,0:T(8,128)(2,1)} %get-tuple-element.13), channel_id=1, source_target_pairs={{0,16},{2,18},{4,20},{6,22},{8,24},{10,26},{12,28},{14,30},{16,0},... | collective-permute-start | bytes 786440 | tf_op jit(solution)/shard_map/ppermute | solution.py:54
  11.1 29.2 %collective-permute-start.12 = (bf16[32,1024]{1,0:T(8,128)(2,1)}, bf16[32,1024]{1,0:T(8,128)(2,1)}, u32[]{:S(2)}, u32[]{:S(2)}) collective-permute-start(bf16[32,1024]{1,0:T(8,128)(2,1)} %constant_dynamic-slice_fusion), channel_id=1, source_target_pairs={{0,2},{2,0},{4,6},{6,4},{8,10},{10,8},{12,14},{14,12},{16,18},{18,... | collective-permute-start | bytes 196616 | tf_op jit(solution)/shard_map/ppermute | solution.py:54
  19.0 9.5 %collective-permute-start.2 = (bf16[256,512]{1,0:T(8,128)(2,1)S(1)}, bf16[256,512]{1,0:T(8,128)(2,1)S(1)}, u32[]{:S(2)}, u32[]{:S(2)}) collective-permute-start(bf16[256,512]{1,0:T(8,128)(2,1)S(1)} %broadcast_select_fusion.5), channel_id=1, source_target_pairs={{4,0},{6,2},{8,4},{10,6},{12,8},{14,10},{20,16},{22,18},{24,20},{2... | collective-permute-start | bytes 786440 | tf_op jit(solution)/shard_map/ppermute | solution.py:54
  32.0 11.2 %collective-permute-start.11 = (bf16[64,512]{1,0:T(8,128)(2,1)S(1)}, bf16[64,512]{1,0:T(8,128)(2,1)S(1)}, u32[]{:S(2)}, u32[]{:S(2)}) collective-permute-start(bf16[64,512]{1,0:T(8,128)(2,1)S(1)} %get-tuple-element.22), channel_id=1, source_target_pairs={{0,28},{2,30},{4,16},{6,18},{8,20},{10,22},{12,24},{14,26},{16,12}... | collective-permute-start | bytes 196616 | tf_op jit(solution)/shard_map/ppermute | solution.py:54
  36.8 7.4 %collective-permute-start.10 = (bf16[64,512]{1,0:T(8,128)(2,1)S(1)}, bf16[64,512]{1,0:T(8,128)(2,1)S(1)}, u32[]{:S(2)}, u32[]{:S(2)}) collective-permute-start(bf16[64,512]{1,0:T(8,128)(2,1)S(1)} %get-tuple-element.23), channel_id=1, source_target_pairs={{0,24},{2,26},{4,28},{6,30},{8,16},{10,18},{12,20},{14,22},{16,8},... | collective-permute-start | bytes 196616 | tf_op jit(solution)/shard_map/ppermute | solution.py:54
  36.8 8.3 %collective-permute-start.9 = (bf16[64,512]{1,0:T(8,128)(2,1)S(1)}, bf16[64,512]{1,0:T(8,128)(2,1)S(1)}, u32[]{:S(2)}, u32[]{:S(2)}) collective-permute-start(bf16[64,512]{1,0:T(8,128)(2,1)S(1)} %get-tuple-element.24), channel_id=1, source_target_pairs={{0,20},{2,22},{4,24},{6,26},{8,28},{10,30},{12,16},{14,18},{16,4},... | collective-permute-start | bytes 196616 | tf_op jit(solution)/shard_map/ppermute | solution.py:54
  38.7 6.5 %collective-permute-start.8 = (bf16[64,512]{1,0:T(8,128)(2,1)S(1)}, bf16[64,512]{1,0:T(8,128)(2,1)S(1)}, u32[]{:S(2)}, u32[]{:S(2)}) collective-permute-start(bf16[64,512]{1,0:T(8,128)(2,1)S(1)} %get-tuple-element.21), channel_id=1, source_target_pairs={{0,16},{2,18},{4,20},{6,22},{8,24},{10,26},{12,28},{14,30},{16,0},... | collective-permute-start | bytes 196616 | tf_op jit(solution)/shard_map/ppermute | solution.py:54
  40.2 5.5 %collective-permute-start.5 = (bf16[64,512]{1,0:T(8,128)(2,1)S(1)}, bf16[64,512]{1,0:T(8,128)(2,1)S(1)}, u32[]{:S(2)}, u32[]{:S(2)}) collective-permute-start(bf16[64,512]{1,0:T(8,128)(2,1)S(1)} %get-tuple-element.19), channel_id=1, source_target_pairs={{0,12},{2,14},{4,0},{6,2},{8,4},{10,6},{12,8},{14,10},{16,28},{18,... | collective-permute-start | bytes 196616 | tf_op jit(solution)/shard_map/ppermute | solution.py:54
  43.1 5.2 %collective-permute-start.4 = (bf16[64,512]{1,0:T(8,128)(2,1)S(1)}, bf16[64,512]{1,0:T(8,128)(2,1)S(1)}, u32[]{:S(2)}, u32[]{:S(2)}) collective-permute-start(bf16[64,512]{1,0:T(8,128)(2,1)S(1)} %get-tuple-element.20), channel_id=1, source_target_pairs={{0,8},{2,10},{4,12},{6,14},{8,0},{10,2},{12,4},{14,6},{16,24},{18,... | collective-permute-start | bytes 196616 | tf_op jit(solution)/shard_map/ppermute | solution.py:54
  44.2 6.1 %collective-permute-start.3 = (bf16[64,512]{1,0:T(8,128)(2,1)S(1)}, bf16[64,512]{1,0:T(8,128)(2,1)S(1)}, u32[]{:S(2)}, u32[]{:S(2)}) collective-permute-start(bf16[64,512]{1,0:T(8,128)(2,1)S(1)} %get-tuple-element.18), channel_id=1, source_target_pairs={{0,4},{2,6},{4,8},{6,10},{8,12},{10,14},{12,0},{14,2},{16,20},{18,... | collective-permute-start | bytes 196616 | tf_op jit(solution)/shard_map/ppermute | solution.py:54
  50.4 7.0 %collective-permute-start.15 = (bf16[64,1024]{1,0:T(8,128)(2,1)S(1)}, bf16[64,1024]{1,0:T(8,128)(2,1)S(1)}, u32[]{:S(2)}, u32[]{:S(2)}) collective-permute-start(bf16[64,1024]{1,0:T(8,128)(2,1)S(1)} %fusion.30), channel_id=1, source_target_pairs={{0,4},{2,6},{4,8},{6,10},{8,12},{10,14},{12,0},{14,2},{16,20},{18,... | collective-permute-start | bytes 393224 | tf_op jit(solution)/shard_map/ppermute | solution.py:54
  50.5 9.6 %collective-permute-start.14 = (bf16[64,1024]{1,0:T(8,128)(2,1)S(1)}, bf16[64,1024]{1,0:T(8,128)(2,1)S(1)}, u32[]{:S(2)}, u32[]{:S(2)}) collective-permute-start(bf16[64,1024]{1,0:T(8,128)(2,1)S(1)} %fusion.30), channel_id=1, source_target_pairs={{0,8},{2,10},{4,12},{6,14},{8,0},{10,2},{12,4},{14,6},{16,24},{18,... | collective-permute-start | bytes 393224 | tf_op jit(solution)/shard_map/ppermute | solution.py:54
  51.6 8.6 %collective-permute-start.13 = (bf16[64,1024]{1,0:T(8,128)(2,1)S(1)}, bf16[64,1024]{1,0:T(8,128)(2,1)S(1)}, u32[]{:S(2)}, u32[]{:S(2)}) collective-permute-start(bf16[64,1024]{1,0:T(8,128)(2,1)S(1)} %fusion.30), channel_id=1, source_target_pairs={{0,12},{2,14},{4,0},{6,2},{8,4},{10,6},{12,8},{14,10},{16,28},{18,... | collective-permute-start | bytes 393224 | tf_op jit(solution)/shard_map/ppermute | solution.py:54
  54.3 8.3 %collective-permute-start.16 = (bf16[64,1024]{1,0:T(8,128)(2,1)S(1)}, bf16[64,1024]{1,0:T(8,128)(2,1)S(1)}, u32[]{:S(2)}, u32[]{:S(2)}) collective-permute-start(bf16[64,1024]{1,0:T(8,128)(2,1)S(1)} %fusion.30), channel_id=1, source_target_pairs={{0,2},{2,0},{4,6},{6,4},{8,10},{10,8},{12,14},{14,12},{16,18},{18,... | collective-permute-start | bytes 393224 | tf_op jit(solution)/shard_map/ppermute | solution.py:54
  57.4 5.2 %collective-permute-start.19 = (bf16[64,1024]{1,0:T(8,128)(2,1)S(1)}, bf16[64,1024]{1,0:T(8,128)(2,1)S(1)}, u32[]{:S(2)}, u32[]{:S(2)}) collective-permute-start(bf16[64,1024]{1,0:T(8,128)(2,1)S(1)} %collective-permute-done.15), channel_id=1, source_target_pairs={{0,2},{2,0},{4,6},{6,4},{8,10},{10,8},{12,14},{14,12},{16,18},{18,... | collective-permute-start | bytes 393224 | tf_op jit(solution)/shard_map/ppermute | solution.py:54
  60.1 5.0 %collective-permute-start.18 = (bf16[64,1024]{1,0:T(8,128)(2,1)S(1)}, bf16[64,1024]{1,0:T(8,128)(2,1)S(1)}, u32[]{:S(2)}, u32[]{:S(2)}) collective-permute-start(bf16[64,1024]{1,0:T(8,128)(2,1)S(1)} %collective-permute-done.14), channel_id=1, source_target_pairs={{0,2},{2,0},{4,6},{6,4},{8,10},{10,8},{12,14},{14,12},{16,18},{18,... | collective-permute-start | bytes 393224 | tf_op jit(solution)/shard_map/ppermute | solution.py:54
  60.1 6.4 %collective-permute-start.17 = (bf16[64,1024]{1,0:T(8,128)(2,1)S(1)}, bf16[64,1024]{1,0:T(8,128)(2,1)S(1)}, u32[]{:S(2)}, u32[]{:S(2)}) collective-permute-start(bf16[64,1024]{1,0:T(8,128)(2,1)S(1)} %collective-permute-done.13), channel_id=1, source_target_pairs={{0,2},{2,0},{4,6},{6,4},{8,10},{10,8},{12,14},{14,12},{16,18},{18,... | collective-permute-start | bytes 393224 | tf_op jit(solution)/shard_map/ppermute | solution.py:54
  (6 other events, 10.6 us)

commit v2 on v1

v2 whole, which is shorter than its diff:
```python
import functools

import numpy as np

import jax
import jax.numpy as jnp
from jax import lax
from jax.experimental import pallas as pl
from jax.experimental.pallas import tpu as pltpu
from jax.sharding import PartitionSpec as P

BF16 = jnp.bfloat16
F32 = jnp.float32
VMEM_BYTES = 16 * 1024 * 1024


def halves(values):
    high = values.astype(jnp.bfloat16)
    return high, (values - high.astype(np.float32)).astype(jnp.bfloat16)


def table_of(rows, tokens):
    period = rows + tokens
    orders = 2 * np.arange(period // 2)[:, None] + 1
    angles = (orders * np.arange(rows)[None, :] % (2 * period)) * (np.pi / period)
    forward = halves(np.concatenate([np.cos(angles), np.sin(angles)], 0).astype(np.float32))
    lags = tokens - 1 - np.arange(tokens)
    angles = (orders.T * lags[:, None] % (2 * period)) * (np.pi / period)
    inverse = np.concatenate([np.cos(angles), -np.sin(angles)], 1).astype(np.float32)
    inverse = halves(inverse * np.float32(2.0 / period))
    return np.concatenate([np.concatenate(forward, 1), np.concatenate(inverse, 0)], 0)


def places(px, py):
    sx = lax.rem(lax.axis_index("seq"), px)
    y = lax.rem(lax.axis_index("hist"), py)
    return sx, y, lax.div(lax.axis_index("hist"), py)


def pick_kernel(px, py, width, history, taps, gates, *refs):
    sx, y, _ = places(px, py)
    outs, sems = refs[:-1], refs[-1]
    rows, owned = history.shape[0], gates.shape[0]
    wide = px * width
    copies = []
    outs = list(outs)

    def copy(source, target):
        copies.append(pltpu.make_async_copy(source, target, sems.at[len(copies)]))
        copies[-1].start()

    def columns(dx, dy):
        start = (y ^ dy) * wide + (sx ^ dx) * width
        return pl.ds(pl.multiple_of(start, width), width)

    for dy in range(1, py):
        copy(taps.at[:, columns(0, dy)], outs.pop(0))
    copy(taps.at[:, columns(0, 0)], outs.pop(0))
    for dx in range(px):
        for dy in range(py):
            if dx or dy:
                copy(history.at[:, columns(dx, dy)], outs.pop(0))
    for dy in range(1, py):
        target = outs.pop(0)
        start = pl.multiple_of((y ^ dy) * wide, wide)
        copy(gates.at[:, pl.ds(start, wide)], target)
    for one in copies:
        one.wait()


def transform(table, values):
    period, rows = table.shape[1], values.shape[0]
    out = jnp.dot(table[:period, :rows], values, preferred_element_type=F32)
    return out + jnp.dot(table[:period, rows : 2 * rows], values, preferred_element_type=F32)


def early_kernel(px, py, tile, table, history, taps, *refs):
    peers, outs = refs[: py - 1], refs[py - 1 :]
    sx, y, _ = places(px, py)
    width = outs[0].shape[1]

    def step(number, _):
        cols = pl.ds(pl.multiple_of(number * tile, tile), tile)
        start = y * px * width + sx * width + number * tile
        own = pl.ds(pl.multiple_of(start, tile), tile)
        values = [history[:, own], taps[:, own]] + [r[:, cols] for r in peers]
        for out, value in zip(outs, values):
            out[:, cols] = transform(table, value)
        return 0

    lax.fori_loop(0, width // tile, step, 0)


def conv_kernel(px, py, nz, tile, table, *refs):
    refs = list(refs)
    own_input = refs.pop(0)
    spectra = [refs.pop(0) for _ in range(py)]
    following = [refs.pop(0) for _ in range(py)]
    inputs = [[None if dx == dy == 0 else refs.pop(0) for dy in range(py)] for dx in range(px)]
    outs = [[refs.pop(0) for _ in range(nz)] for _ in range(px)]
    (conv,) = refs
    _, y, z = places(px, py)
    width = own_input.shape[1]
    period = table.shape[1]
    modes = period // 2
    group = outs[0][0].shape[0]
    tokens = conv.shape[1]
    rows = following[0].shape[0]
    assert 2 * rows == period
    odd = lax.broadcasted_iota(jnp.int32, (modes, tile), 0) % 2
    sign = (1 - 2 * odd).astype(F32)

    def step(number, _):
        cols = pl.ds(pl.multiple_of(number * tile, tile), tile)
        after = following[0][:, cols]
        for d in range(1, py):
            after = jnp.where(y == d, following[d][:, cols], after)
        after = transform(table, after)
        held = [r[:, cols] for r in spectra]
        spec = []
        for dy in range(py):
            value = after if py == 1 else jnp.where(y ^ dy == 0, held[1 - dy], after)
            spec.append(
                (
                    held[dy][:modes] - sign * value[modes:],
                    held[dy][modes:] + sign * value[:modes],
                )
            )
        for dx in range(px):
            real, imag = None, None
            for dy in range(py):
                here = inputs[dx][dy]
                out = own_input[:, cols] if here is None else transform(table, here[:, cols])
                (tc, ts), ic, is_ = spec[dy], out[:modes], out[modes:]
                re, im = tc * ic + ts * is_, tc * is_ - ts * ic
                real, imag = (re, im) if dy == 0 else (real + re, imag + im)
            product = jnp.concatenate([real, imag], 0)
            high = product.astype(BF16)
            low = (product - high.astype(F32)).astype(BF16)
            i_high, i_low = table[period : period + tokens, :], table[period + tokens :, :]
            total = jnp.dot(i_high, high, preferred_element_type=F32)
            total = total + jnp.dot(i_high, low, preferred_element_type=F32)
            total = total + jnp.dot(i_low, high, preferred_element_type=F32)
            conv[dx, :, cols] = total
        return 0

    lax.fori_loop(0, width // tile, step, 0)
    for dx in range(px):
        for dz in range(nz):
            begin = pl.multiple_of(lax.rem(z + dz, nz) * group, group)
            out = outs[dx][dz]
            out[...] = conv[dx, pl.ds(begin, group), :].astype(out.dtype)


def local(history, filter_taps, gate_values, out_weight):
    rows, channels = history.shape
    owned = gate_values.shape[0]
    seqs, hists, chans = (lax.axis_size(a) for a in ("seq", "hist", "chan"))
    tokens = owned * hists
    px = 2 if seqs % 2 == 0 else 1
    py = 2 if hists % 2 == 0 else 1
    nz = hists // py
    wide = channels // py
    width = wide // px
    group = tokens // nz
    sx = lax.axis_index("seq") % px
    y = lax.axis_index("hist") % py
    z = lax.axis_index("hist") // py

    def move(value, dx=0, dz=0, dy=0, wrap=True, only=None):
        pairs = []
        for s in range(seqs):
            for h in range(hists):
                to_z = h // py + dz
                if (not wrap and not 0 <= to_z < nz) or only not in (None, h % py):
                    continue
                target = (s ^ dx) * hists + (to_z % nz) * py + ((h % py) ^ dy)
                pairs.append((s * hists + h, target))
        return lax.ppermute(value, ("seq", "hist"), pairs)

    def ordered(index, values):
        if len(values) == 1:
            return values
        first, second = values
        return [jnp.where(index == 0, first, second), jnp.where(index == 0, second, first)]

    hbm = pl.BlockSpec(memory_space=pltpu.HBM)
    vmem = pl.BlockSpec(memory_space=pltpu.VMEM)
    piece = jax.ShapeDtypeStruct((rows, width), BF16)
    shapes = [piece] * (py + px * py - 1) + [jax.ShapeDtypeStruct((owned, wide), BF16)] * (py - 1)
    picked = list(
        pl.pallas_call(
            functools.partial(pick_kernel, px, py, width),
            out_shape=shapes,
            in_specs=[hbm] * 3,
            out_specs=[vmem] * len(shapes),
            scratch_shapes=[pltpu.SemaphoreType.DMA((len(shapes),))],
        )(history, filter_taps, gate_values)
    )
    peers = [move(picked.pop(0), dy=dy) for dy in range(1, py)]
    following = [picked.pop(0)] + peers
    following = [move(v, dz=-1, wrap=False, only=d) for d, v in enumerate(following)]
    inputs = []
    for dx in range(px):
        for dy in range(py):
            if dx or dy:
                inputs.append(move(picked.pop(0), dx=dx, dy=dy))
    gates = [lax.dynamic_slice_in_dim(gate_values, y * wide, wide, 1)]
    gates = ordered(y, gates + [move(picked.pop(0), dy=dy) for dy in range(1, py)])
    gate = jnp.concatenate(gates, 0).astype(F32)

    table = table_of(rows, tokens)
    tile = 256 if width % 256 == 0 else width
    params = pltpu.CompilerParams(vmem_limit_bytes=VMEM_BYTES)
    flops = 4 * rows * 2 * rows * width
    early = pl.pallas_call(
        functools.partial(early_kernel, px, py, tile),
        out_shape=[jax.ShapeDtypeStruct((rows + tokens, width), F32)] * (py + 1),
        in_specs=[vmem] * (2 + py),
        out_specs=[vmem] * (py + 1),
        compiler_params=params,
        cost_estimate=pl.CostEstimate(flops=3 * flops, bytes_accessed=rows * width * 8, transcendentals=0),
    )(table, history, filter_taps, *peers)
    part = lambda own: jax.ShapeDtypeStruct((group, width), F32 if own else BF16)
    contributions = pl.pallas_call(
        functools.partial(conv_kernel, px, py, nz, tile),
        out_shape=[part(dx == dz == 0) for dx in range(px) for dz in range(nz)],
        in_specs=[vmem] * (1 + 1 + py + py + px * py - 1),
        out_specs=[vmem] * (px * nz),
        scratch_shapes=[pltpu.VMEM((px, tokens, width), F32)],
        compiler_params=params,
        cost_estimate=pl.CostEstimate(flops=7 * flops, bytes_accessed=rows * width * 8, transcendentals=0),
    )(table, *early, *following, *inputs)

    sums = []
    for dx in range(px):
        total = None
        for dz in range(nz):
            value = contributions[dx * nz + dz]
            if dx or dz:
                value = move(value, dx=dx, dz=dz).astype(F32)
            total = value if dz == 0 else total + value
        sums.append(total)
    conv = jnp.concatenate(ordered(sx, sums), 1)
    gated = (conv * gate).astype(BF16)

    along = [gated] + [move(gated, dz=-dz) for dz in range(1, nz)]
    total = 0.0
    for dy in range(py):
        across = [move(v, dy=dy) if dy else v for v in along]
        weight = lax.dynamic_slice_in_dim(out_weight, (y ^ dy) * wide, wide, 0)
        total = total + jnp.dot(jnp.concatenate(across, 0), weight, preferred_element_type=F32)
    total = total.astype(BF16).reshape(nz, group, -1)
    total = jnp.roll(total, z, axis=0).reshape(tokens, -1)
    final = lax.all_to_all(total, ("hist", "chan"), split_axis=0, concat_axis=0, tiled=True)
    share = owned // chans
    final = final.reshape(hists, chans, share, -1).astype(F32).sum(1).astype(BF16)
    return final.transpose(1, 0, 2).reshape(share, -1)


def solution(mesh):
    return jax.shard_map(
        local,
        mesh=mesh,
        in_specs=(
            P(("seq", "hist"), "chan"),
            P("hist", "chan"),
            P(("seq", "hist"), "chan"),
            P("chan", "hist"),
        ),
        out_specs=P(("seq", "hist", "chan"), None),
        check_vma=False,
    )
```

time: 81.8 us -> 77.6 us (0.949)
  matrix products: 8.94 us -> 0.87 us
  Pallas kernels: 0 us -> 7.63 us
  starting transfers between devices: 25.1 us -> 31.9 us
  waiting for transfers between devices: 24 us -> 20 us
  other arithmetic: 3.48 us -> 0.28 us
  local copies, waits for them, and re-layouts: 5.84 us -> 3.13 us
    dot_general x20 -> x0, matrix products: 8.07 us -> none  [the longest x7 3.13 us: transform(): out = jnp.dot(fwd_high, block, preferred_element_type=F32)]
    pallas_call x0 -> x3, Pallas kernels: none -> 7.63 us  [the longest x1 3.92 us: local(): pl.pallas_call(functools.partial(conv_kernel, px, py, nz, tile), out_shap...]
    ppermute x20 -> x21, starting transfers between devices: 25.1 us -> 31.9 us  [move(): return lax.ppermute(value, ('seq', 'hist'), pairs)]
    dynamic_slice x3 -> x0, local copies, waits for them, and re-layouts: 4.53 us -> none  [the longest x2 3.9 us: cut(): return lax.dynamic_slice_in_dim(value, start, quarter, 1)]
    ppermute x20 -> x21, waiting for transfers between devices: 24 us -> 20 us  [move(): return lax.ppermute(value, ('seq', 'hist'), pairs)]
    unnamed x20 -> x14, local copies, waits for them, and re-layouts: 0.58 us -> 2.47 us
    select_n x3 -> x2, other arithmetic: 1.95 us -> 0.1 us  [ordered(): jnp.where(index == 0, first, second)]
    add x2 -> x0, other arithmetic: 1.34 us -> none  [local(): real = real + tc * ic + ts * is_]
  transfers between devices with their start and end apart: 20 -> 21, of which waited for: 9 -> 10; matrix products, arithmetic and copies ran while one was open for 18% -> 1% of each run, Pallas kernels for 0% -> 7%
where the time goes in v2:
time: 77.6 us; the launch traced here: 77.4 us
  starting transfers between devices  31.9 us (41%)
  waiting for transfers between devices  20 us (26%)
  blocking collectives  13.4 us (17%)
  Pallas kernels  7.63 us (10%)
  local copies, waits for them, and re-layouts  3.13 us (4%)
  matrix products  0.87 us (1%)
    ppermute x21, starting transfers between devices, move(): return lax.ppermute(value, ('seq', 'hist'), pairs)  31.9 us
    ppermute x21, waiting for transfers between devices, move(): return lax.ppermute(value, ('seq', 'hist'), pairs)  20 us
    all_to_all x1, blocking collectives, local(): lax.all_to_all(total, ('hist', 'chan'), split_axis=0, concat_axis=0, tile...  13.4 us
    pallas_call x1, Pallas kernels, local(): pl.pallas_call(functools.partial(conv_kernel, px, py, nz, tile), out_shap...  3.92 us
    pallas_call x1, Pallas kernels, local(): pl.pallas_call(functools.partial(pick_kernel, px, py, width), out_shape=s...  2.56 us
    unnamed x14, local copies, waits for them, and re-layouts  2.47 us
  transfers between devices with their start and end apart: 21, of which 10 were waited for; matrix products, arithmetic and copies ran while one was open for 1% of the time, Pallas kernels for 7%

profile of v2, /device:TPU:0, one launch (start us, length us, event | category | flops | bytes accessed | tf_op | source)
XLA Modules:
  0.0 77.4 jit_solution(13930144500466697455)
XLA Ops:
  0.0 2.6 %shard_map.55 = (bf16[256,512]{1,0:T(8,128)(2,1)}, bf16[256,512]{1,0:T(8,128)(2,1)}, bf16[256,512]{1,0:T(8,128)(2,1)}, bf16[256,512]{1,0:T(8,128)(2,1)}, bf16[25...) custom-call(bf16[256,2048]{1,0:T(8,128)(2,1)} %history.3, bf16[256,2048]{1,0:T(8,128)(2,1)} %taps.3, bf16[32,2048]{1,0:T(8,128)(2,1)} %gates.1), custom_call_target="tpu_custom_call" | custom-call | tf_op jit(solution)/shard_map/pallas_call | solution.py:192
  2.6 3.1 %collective-permute-start = (bf16[256,512]{1,0:T(8,128)(2,1)}, bf16[256,512]{1,0:T(8,128)(2,1)S(1)}, u32[]{:S(2)}, u32[]{:S(2)}) collective-permute-start(bf16[256,512]{1,0:T(8,128)(2,1)} %get-tuple-element.22), channel_id=1, source_target_pairs={{0,2},{2,0},{4,6},{6,4},{8,10},{10,8},{12,14},{14,12},{16,18},{18,... | collective-permute-start | bytes 786440 | tf_op jit(solution)/shard_map/ppermute | solution.py:179
  5.6 1.3 %collective-permute-start.1 = (bf16[256,512]{1,0:T(8,128)(2,1)}, bf16[256,512]{1,0:T(8,128)(2,1)S(1)}, u32[]{:S(2)}, u32[]{:S(2)}) collective-permute-start(bf16[256,512]{1,0:T(8,128)(2,1)} %get-tuple-element.26), channel_id=1, source_target_pairs={{4,0},{8,4},{12,8},{20,16},{24,20},{28,24},{5,1},{9,5},{13,9},{21,... | collective-permute-start | bytes 786440 | tf_op jit(solution)/shard_map/ppermute | solution.py:179
  7.0 1.6 %collective-permute-start.4 = (bf16[256,512]{1,0:T(8,128)(2,1)}, bf16[256,512]{1,0:T(8,128)(2,1)S(1)}, u32[]{:S(2)}, u32[]{:S(2)}) collective-permute-start(bf16[256,512]{1,0:T(8,128)(2,1)} %get-tuple-element.28), channel_id=1, source_target_pairs={{0,16},{2,18},{4,20},{6,22},{8,24},{10,26},{12,28},{14,30},{16,0},... | collective-permute-start | bytes 786440 | tf_op jit(solution)/shard_map/ppermute | solution.py:179
  8.6 1.9 %collective-permute-start.5 = (bf16[256,512]{1,0:T(8,128)(2,1)}, bf16[256,512]{1,0:T(8,128)(2,1)S(1)}, u32[]{:S(2)}, u32[]{:S(2)}) collective-permute-start(bf16[256,512]{1,0:T(8,128)(2,1)} %get-tuple-element.29), channel_id=1, source_target_pairs={{0,18},{2,16},{4,22},{6,20},{8,26},{10,24},{12,30},{14,28},{16,2},... | collective-permute-start | bytes 786440 | tf_op jit(solution)/shard_map/ppermute | solution.py:179
  10.5 2.5 %collective-permute-done.refs_0_ = bf16[256,512]{1,0:T(8,128)(2,1)S(1)} collective-permute-done((bf16[256,512]{1,0:T(8,128)(2,1)}, bf16[256,512]{1,0:T(8,128)(2,1)S(1)}, u32[]{:S(2)}, u32[]{:S(2)}) %collective-permute-start) | collective-permute-done | bytes 262176 | tf_op jit(solution)/shard_map/ppermute | solution.py:179
  13.7 1.2 %copy-done.2 = bf16[256,2048]{1,0:T(8,128)(2,1)S(1)} copy-done((bf16[256,2048]{1,0:T(8,128)(2,1)S(1)}, bf16[256,2048]{1,0:T(8,128)(2,1)}, u32[]{:S(2)}) %copy-start.2) | copy-done | bytes 1048600
  14.9 1.2 %copy-done.3 = bf16[1024,512]{1,0:T(8,128)(2,1)S(1)} copy-done((bf16[1024,512]{1,0:T(8,128)(2,1)S(1)}, bf16[1024,512]{1,0:T(8,128)(2,1)}, u32[]{:S(2)}) %copy-start.3) | copy-done | bytes 1048600
  17.3 2.7 %collective-permute-start.13 = (bf16[32,1024]{1,0:T(8,128)(2,1)S(1)}, bf16[32,1024]{1,0:T(8,128)(2,1)S(1)}, u32[]{:S(2)}, u32[]{:S(2)}) collective-permute-start(bf16[32,1024]{1,0:T(8,128)(2,1)S(1)} %copy-done.6), channel_id=1, source_target_pairs={{0,2},{2,0},{4,6},{6,4},{8,10},{10,8},{12,14},{14,12},{16,18},{18,... | collective-permute-start | bytes 196616 | tf_op jit(solution)/shard_map/ppermute | solution.py:179
  20.0 4.1 %collective-permute-done.3.refs_5_ = bf16[256,512]{1,0:T(8,128)(2,1)S(1)} collective-permute-done((bf16[256,512]{1,0:T(8,128)(2,1)}, bf16[256,512]{1,0:T(8,128)(2,1)S(1)}, u32[]{:S(2)}, u32[]{:S(2)}) %collective-permute-start.3) | collective-permute-done | bytes 262176 | tf_op jit(solution)/shard_map/ppermute | solution.py:179
  24.1 3.9 %shard_map.57 = (f32[64,512]{1,0:T(8,128)S(1)}, bf16[64,512]{1,0:T(8,128)(2,1)S(1)}, bf16[64,512]{1,0:T(8,128)(2,1)S(1)}, bf16[64,512]{1,0:T(8,128)(2,1)S(1)}, b...) custom-call(bf16[1024,512]{1,0:T(8,128)(2,1)S(1)} %copy-done.4, ...), custom_call_target="tpu_custom_call" | custom-call | flops 1879048192 | bytes 1048576 | tf_op jit(solution)/shard_map/pallas_call | solution.py:225
  28.0 2.8 %collective-permute-start.10 = (bf16[64,512]{1,0:T(8,128)(2,1)S(1)}, bf16[64,512]{1,0:T(8,128)(2,1)S(1)}, u32[]{:S(2)}, u32[]{:S(2)}) collective-permute-start(bf16[64,512]{1,0:T(8,128)(2,1)S(1)} %get-tuple-element.35), channel_id=1, source_target_pairs={{0,20},{2,22},{4,24},{6,26},{8,28},{10,30},{12,16},{14,18},{16,4},... | collective-permute-start | bytes 196616 | tf_op jit(solution)/shard_map/ppermute | solution.py:179
  30.8 2.6 %collective-permute-start.11 = (bf16[64,512]{1,0:T(8,128)(2,1)S(1)}, bf16[64,512]{1,0:T(8,128)(2,1)S(1)}, u32[]{:S(2)}, u32[]{:S(2)}) collective-permute-start(bf16[64,512]{1,0:T(8,128)(2,1)S(1)} %get-tuple-element.36), channel_id=1, source_target_pairs={{0,24},{2,26},{4,28},{6,30},{8,16},{10,18},{12,20},{14,22},{16,8},... | collective-permute-start | bytes 196616 | tf_op jit(solution)/shard_map/ppermute | solution.py:179
  33.4 2.3 %collective-permute-start.12 = (bf16[64,512]{1,0:T(8,128)(2,1)S(1)}, bf16[64,512]{1,0:T(8,128)(2,1)S(1)}, u32[]{:S(2)}, u32[]{:S(2)}) collective-permute-start(bf16[64,512]{1,0:T(8,128)(2,1)S(1)} %get-tuple-element.37), channel_id=1, source_target_pairs={{0,28},{2,30},{4,16},{6,18},{8,20},{10,22},{12,24},{14,26},{16,12}... | collective-permute-start | bytes 196616 | tf_op jit(solution)/shard_map/ppermute | solution.py:179
  36.7 2.9 %collective-permute-start.8 = (bf16[64,512]{1,0:T(8,128)(2,1)S(1)}, bf16[64,512]{1,0:T(8,128)(2,1)S(1)}, u32[]{:S(2)}, u32[]{:S(2)}) collective-permute-start(bf16[64,512]{1,0:T(8,128)(2,1)S(1)} %get-tuple-element.33), channel_id=1, source_target_pairs={{0,12},{2,14},{4,0},{6,2},{8,4},{10,6},{12,8},{14,10},{16,28},{18,... | collective-permute-start | bytes 196616 | tf_op jit(solution)/shard_map/ppermute | solution.py:179
  40.1 1.7 %collective-permute-done.6 = bf16[64,512]{1,0:T(8,128)(2,1)S(1)} collective-permute-done((bf16[64,512]{1,0:T(8,128)(2,1)S(1)}, bf16[64,512]{1,0:T(8,128)(2,1)S(1)}, u32[]{:S(2)}, u32[]{:S(2)}) %collective-permute-start.6) | collective-permute-done | bytes 65568 | tf_op jit(solution)/shard_map/ppermute | solution.py:179
  44.1 4.0 %collective-permute-start.14 = (bf16[64,1024]{1,0:T(8,128)(2,1)S(1)}, bf16[64,1024]{1,0:T(8,128)(2,1)S(1)}, u32[]{:S(2)}, u32[]{:S(2)}) collective-permute-start(bf16[64,1024]{1,0:T(8,128)(2,1)S(1)} %fusion.19), channel_id=1, source_target_pairs={{0,12},{2,14},{4,0},{6,2},{8,4},{10,6},{12,8},{14,10},{16,28},{18,... | collective-permute-start | bytes 393224 | tf_op jit(solution)/shard_map/ppermute | solution.py:179
  49.5 2.1 %collective-permute-done.14 = bf16[64,1024]{1,0:T(8,128)(2,1)S(1)} collective-permute-done((bf16[64,1024]{1,0:T(8,128)(2,1)S(1)}, bf16[64,1024]{1,0:T(8,128)(2,1)S(1)}, u32[]{:S(2)}, u32[]{:S(2)}) %collective-permute-start.14) | collective-permute-done | bytes 131104 | tf_op jit(solution)/shard_map/ppermute | solution.py:179
  51.6 1.3 %collective-permute-start.18 = (bf16[64,1024]{1,0:T(8,128)(2,1)S(1)}, bf16[64,1024]{1,0:T(8,128)(2,1)S(1)}, u32[]{:S(2)}, u32[]{:S(2)}) collective-permute-start(bf16[64,1024]{1,0:T(8,128)(2,1)S(1)} %collective-permute-done.14), channel_id=1, source_target_pairs={{0,2},{2,0},{4,6},{6,4},{8,10},{10,8},{12,14},{14,12},{16,18},{18,... | collective-permute-start | bytes 393224 | tf_op jit(solution)/shard_map/ppermute | solution.py:179
  52.9 3.1 %collective-permute-done.15 = bf16[64,1024]{1,0:T(8,128)(2,1)S(1)} collective-permute-done((bf16[64,1024]{1,0:T(8,128)(2,1)S(1)}, bf16[64,1024]{1,0:T(8,128)(2,1)S(1)}, u32[]{:S(2)}, u32[]{:S(2)}) %collective-permute-start.15) | collective-permute-done | bytes 131104 | tf_op jit(solution)/shard_map/ppermute | solution.py:179
  56.0 1.7 %collective-permute-start.19 = (bf16[64,1024]{1,0:T(8,128)(2,1)S(1)}, bf16[64,1024]{1,0:T(8,128)(2,1)S(1)}, u32[]{:S(2)}, u32[]{:S(2)}) collective-permute-start(bf16[64,1024]{1,0:T(8,128)(2,1)S(1)} %collective-permute-done.15), channel_id=1, source_target_pairs={{0,2},{2,0},{4,6},{6,4},{8,10},{10,8},{12,14},{14,12},{16,18},{18,... | collective-permute-start | bytes 393224 | tf_op jit(solution)/shard_map/ppermute | solution.py:179
  58.5 2.7 %collective-permute-done.19 = bf16[64,1024]{1,0:T(8,128)(2,1)S(1)} collective-permute-done((bf16[64,1024]{1,0:T(8,128)(2,1)S(1)}, bf16[64,1024]{1,0:T(8,128)(2,1)S(1)}, u32[]{:S(2)}, u32[]{:S(2)}) %collective-permute-start.19) | collective-permute-done | bytes 131104 | tf_op jit(solution)/shard_map/ppermute | solution.py:179
  61.2 1.5 %collective-permute-done.20 = bf16[64,1024]{1,0:T(8,128)(2,1)S(1)} collective-permute-done((bf16[64,1024]{1,0:T(8,128)(2,1)S(1)}, bf16[64,1024]{1,0:T(8,128)(2,1)S(1)}, u32[]{:S(2)}, u32[]{:S(2)}) %collective-permute-start.20) | collective-permute-done | bytes 131104 | tf_op jit(solution)/shard_map/ppermute | solution.py:179
  63.3 13.4 %all_to_all.9 = bf16[16,16,512]{2,1,0:T(8,128)(2,1)S(1)} all-to-all(bf16[16,16,512]{2,1,0:T(8,128)(2,1)S(1)} %bitcast.7), channel_id=1, replica_groups=mesh['seq'=2,'hist'=8,'chan'=2] {'hist','chan'}, dimensions={0} | all-to-all | bytes 524288 | tf_op jit(solution)/shard_map/all_to_all | solution.py:255
  (44 shorter events, 9.1 us)
Async XLA Ops:
  0.0 58.0 %copy-start = (bf16[2048,512]{1,0:T(8,128)(2,1)S(1)}, bf16[2048,512]{1,0:T(8,128)(2,1)}, u32[]{:S(2)}) copy-start(bf16[2048,512]{1,0:T(8,128)(2,1)} %param.8) | copy-start | bytes 6291460
  0.0 13.6 %copy-start.1 = (bf16[256,2048]{1,0:T(8,128)(2,1)S(1)}, bf16[256,2048]{1,0:T(8,128)(2,1)}, u32[]{:S(2)}) copy-start(bf16[256,2048]{1,0:T(8,128)(2,1)} %history.3) | copy-start | bytes 3145732
  2.6 10.4 %collective-permute-start = (bf16[256,512]{1,0:T(8,128)(2,1)}, bf16[256,512]{1,0:T(8,128)(2,1)S(1)}, u32[]{:S(2)}, u32[]{:S(2)}) collective-permute-start(bf16[256,512]{1,0:T(8,128)(2,1)} %get-tuple-element.22), channel_id=1, source_target_pairs={{0,2},{2,0},{4,6},{6,4},{8,10},{10,8},{12,14},{14,12},{16,18},{18,... | collective-permute-start | bytes 786440 | tf_op jit(solution)/shard_map/ppermute | solution.py:179
  5.6 11.6 %collective-permute-start.1 = (bf16[256,512]{1,0:T(8,128)(2,1)}, bf16[256,512]{1,0:T(8,128)(2,1)S(1)}, u32[]{:S(2)}, u32[]{:S(2)}) collective-permute-start(bf16[256,512]{1,0:T(8,128)(2,1)} %get-tuple-element.26), channel_id=1, source_target_pairs={{4,0},{8,4},{12,8},{20,16},{24,20},{28,24},{5,1},{9,5},{13,9},{21,... | collective-permute-start | bytes 786440 | tf_op jit(solution)/shard_map/ppermute | solution.py:179
  6.9 17.2 %collective-permute-start.3 = (bf16[256,512]{1,0:T(8,128)(2,1)}, bf16[256,512]{1,0:T(8,128)(2,1)S(1)}, u32[]{:S(2)}, u32[]{:S(2)}) collective-permute-start(bf16[256,512]{1,0:T(8,128)(2,1)} %get-tuple-element.27), channel_id=1, source_target_pairs={{0,2},{2,0},{4,6},{6,4},{8,10},{10,8},{12,14},{14,12},{16,18},{18,... | collective-permute-start | bytes 786440 | tf_op jit(solution)/shard_map/ppermute | solution.py:179
  7.0 17.1 %collective-permute-start.4 = (bf16[256,512]{1,0:T(8,128)(2,1)}, bf16[256,512]{1,0:T(8,128)(2,1)S(1)}, u32[]{:S(2)}, u32[]{:S(2)}) collective-permute-start(bf16[256,512]{1,0:T(8,128)(2,1)} %get-tuple-element.28), channel_id=1, source_target_pairs={{0,16},{2,18},{4,20},{6,22},{8,24},{10,26},{12,28},{14,30},{16,0},... | collective-permute-start | bytes 786440 | tf_op jit(solution)/shard_map/ppermute | solution.py:179
  8.6 15.5 %collective-permute-start.5 = (bf16[256,512]{1,0:T(8,128)(2,1)}, bf16[256,512]{1,0:T(8,128)(2,1)S(1)}, u32[]{:S(2)}, u32[]{:S(2)}) collective-permute-start(bf16[256,512]{1,0:T(8,128)(2,1)} %get-tuple-element.29), channel_id=1, source_target_pairs={{0,18},{2,16},{4,22},{6,20},{8,26},{10,24},{12,30},{14,28},{16,2},... | collective-permute-start | bytes 786440 | tf_op jit(solution)/shard_map/ppermute | solution.py:179
  13.0 11.1 %collective-permute-start.2 = (bf16[256,512]{1,0:T(8,128)(2,1)S(1)}, bf16[256,512]{1,0:T(8,128)(2,1)S(1)}, u32[]{:S(2)}, u32[]{:S(2)}) collective-permute-start(bf16[256,512]{1,0:T(8,128)(2,1)S(1)} %collective-permute-done.refs_0_), channel_id=1, source_target_pairs={{6,2},{10,6},{14,10},{22,18},{26,22},{30,26},{7,3},{11,7},{15,11},... | collective-permute-start | bytes 786440 | tf_op jit(solution)/shard_map/ppermute | solution.py:179
  17.3 19.0 %collective-permute-start.13 = (bf16[32,1024]{1,0:T(8,128)(2,1)S(1)}, bf16[32,1024]{1,0:T(8,128)(2,1)S(1)}, u32[]{:S(2)}, u32[]{:S(2)}) collective-permute-start(bf16[32,1024]{1,0:T(8,128)(2,1)S(1)} %copy-done.6), channel_id=1, source_target_pairs={{0,2},{2,0},{4,6},{6,4},{8,10},{10,8},{12,14},{14,12},{16,18},{18,... | collective-permute-start | bytes 196616 | tf_op jit(solution)/shard_map/ppermute | solution.py:179
  24.1 16.0 %copy-start.5 = (bf16[32,2048]{1,0:T(8,128)(2,1)S(1)}, bf16[32,2048]{1,0:T(8,128)(2,1)}, u32[]{:S(2)}) copy-start(bf16[32,2048]{1,0:T(8,128)(2,1)} %gates.1) | copy-start | bytes 393220
  28.0 8.6 %collective-permute-start.10 = (bf16[64,512]{1,0:T(8,128)(2,1)S(1)}, bf16[64,512]{1,0:T(8,128)(2,1)S(1)}, u32[]{:S(2)}, u32[]{:S(2)}) collective-permute-start(bf16[64,512]{1,0:T(8,128)(2,1)S(1)} %get-tuple-element.35), channel_id=1, source_target_pairs={{0,20},{2,22},{4,24},{6,26},{8,28},{10,30},{12,16},{14,18},{16,4},... | collective-permute-start | bytes 196616 | tf_op jit(solution)/shard_map/ppermute | solution.py:179
  30.8 8.9 %collective-permute-start.11 = (bf16[64,512]{1,0:T(8,128)(2,1)S(1)}, bf16[64,512]{1,0:T(8,128)(2,1)S(1)}, u32[]{:S(2)}, u32[]{:S(2)}) collective-permute-start(bf16[64,512]{1,0:T(8,128)(2,1)S(1)} %get-tuple-element.36), channel_id=1, source_target_pairs={{0,24},{2,26},{4,28},{6,30},{8,16},{10,18},{12,20},{14,22},{16,8},... | collective-permute-start | bytes 196616 | tf_op jit(solution)/shard_map/ppermute | solution.py:179
  33.4 6.7 %collective-permute-start.12 = (bf16[64,512]{1,0:T(8,128)(2,1)S(1)}, bf16[64,512]{1,0:T(8,128)(2,1)S(1)}, u32[]{:S(2)}, u32[]{:S(2)}) collective-permute-start(bf16[64,512]{1,0:T(8,128)(2,1)S(1)} %get-tuple-element.37), channel_id=1, source_target_pairs={{0,28},{2,30},{4,16},{6,18},{8,20},{10,22},{12,24},{14,26},{16,12}... | collective-permute-start | bytes 196616 | tf_op jit(solution)/shard_map/ppermute | solution.py:179
  35.7 6.2 %collective-permute-start.6 = (bf16[64,512]{1,0:T(8,128)(2,1)S(1)}, bf16[64,512]{1,0:T(8,128)(2,1)S(1)}, u32[]{:S(2)}, u32[]{:S(2)}) collective-permute-start(bf16[64,512]{1,0:T(8,128)(2,1)S(1)} %get-tuple-element.31), channel_id=1, source_target_pairs={{0,4},{2,6},{4,8},{6,10},{8,12},{10,14},{12,0},{14,2},{16,20},{18,... | collective-permute-start | bytes 196616 | tf_op jit(solution)/shard_map/ppermute | solution.py:179
  36.3 6.6 %collective-permute-start.7 = (bf16[64,512]{1,0:T(8,128)(2,1)S(1)}, bf16[64,512]{1,0:T(8,128)(2,1)S(1)}, u32[]{:S(2)}, u32[]{:S(2)}) collective-permute-start(bf16[64,512]{1,0:T(8,128)(2,1)S(1)} %get-tuple-element.32), channel_id=1, source_target_pairs={{0,8},{2,10},{4,12},{6,14},{8,0},{10,2},{12,4},{14,6},{16,24},{18,... | collective-permute-start | bytes 196616 | tf_op jit(solution)/shard_map/ppermute | solution.py:179
  36.7 6.3 %collective-permute-start.8 = (bf16[64,512]{1,0:T(8,128)(2,1)S(1)}, bf16[64,512]{1,0:T(8,128)(2,1)S(1)}, u32[]{:S(2)}, u32[]{:S(2)}) collective-permute-start(bf16[64,512]{1,0:T(8,128)(2,1)S(1)} %get-tuple-element.33), channel_id=1, source_target_pairs={{0,12},{2,14},{4,0},{6,2},{8,4},{10,6},{12,8},{14,10},{16,28},{18,... | collective-permute-start | bytes 196616 | tf_op jit(solution)/shard_map/ppermute | solution.py:179
  39.7 4.3 %collective-permute-start.9 = (bf16[64,512]{1,0:T(8,128)(2,1)S(1)}, bf16[64,512]{1,0:T(8,128)(2,1)S(1)}, u32[]{:S(2)}, u32[]{:S(2)}) collective-permute-start(bf16[64,512]{1,0:T(8,128)(2,1)S(1)} %get-tuple-element.34), channel_id=1, source_target_pairs={{0,16},{2,18},{4,20},{6,22},{8,24},{10,26},{12,28},{14,30},{16,0},... | collective-permute-start | bytes 196616 | tf_op jit(solution)/shard_map/ppermute | solution.py:179
  44.1 7.5 %collective-permute-start.14 = (bf16[64,1024]{1,0:T(8,128)(2,1)S(1)}, bf16[64,1024]{1,0:T(8,128)(2,1)S(1)}, u32[]{:S(2)}, u32[]{:S(2)}) collective-permute-start(bf16[64,1024]{1,0:T(8,128)(2,1)S(1)} %fusion.19), channel_id=1, source_target_pairs={{0,12},{2,14},{4,0},{6,2},{8,4},{10,6},{12,8},{14,10},{16,28},{18,... | collective-permute-start | bytes 393224 | tf_op jit(solution)/shard_map/ppermute | solution.py:179
  48.1 7.9 %collective-permute-start.15 = (bf16[64,1024]{1,0:T(8,128)(2,1)S(1)}, bf16[64,1024]{1,0:T(8,128)(2,1)S(1)}, u32[]{:S(2)}, u32[]{:S(2)}) collective-permute-start(bf16[64,1024]{1,0:T(8,128)(2,1)S(1)} %fusion.19), channel_id=1, source_target_pairs={{0,8},{2,10},{4,12},{6,14},{8,0},{10,2},{12,4},{14,6},{16,24},{18,... | collective-permute-start | bytes 393224 | tf_op jit(solution)/shard_map/ppermute | solution.py:179
  48.1 9.7 %collective-permute-start.16 = (bf16[64,1024]{1,0:T(8,128)(2,1)S(1)}, bf16[64,1024]{1,0:T(8,128)(2,1)S(1)}, u32[]{:S(2)}, u32[]{:S(2)}) collective-permute-start(bf16[64,1024]{1,0:T(8,128)(2,1)S(1)} %fusion.19), channel_id=1, source_target_pairs={{0,4},{2,6},{4,8},{6,10},{8,12},{10,14},{12,0},{14,2},{16,20},{18,... | collective-permute-start | bytes 393224 | tf_op jit(solution)/shard_map/ppermute | solution.py:179
  48.7 9.8 %collective-permute-start.17 = (bf16[64,1024]{1,0:T(8,128)(2,1)S(1)}, bf16[64,1024]{1,0:T(8,128)(2,1)S(1)}, u32[]{:S(2)}, u32[]{:S(2)}) collective-permute-start(bf16[64,1024]{1,0:T(8,128)(2,1)S(1)} %fusion.19), channel_id=1, source_target_pairs={{0,2},{2,0},{4,6},{6,4},{8,10},{10,8},{12,14},{14,12},{16,18},{18,... | collective-permute-start | bytes 393224 | tf_op jit(solution)/shard_map/ppermute | solution.py:179
  51.6 6.9 %collective-permute-start.18 = (bf16[64,1024]{1,0:T(8,128)(2,1)S(1)}, bf16[64,1024]{1,0:T(8,128)(2,1)S(1)}, u32[]{:S(2)}, u32[]{:S(2)}) collective-permute-start(bf16[64,1024]{1,0:T(8,128)(2,1)S(1)} %collective-permute-done.14), channel_id=1, source_target_pairs={{0,2},{2,0},{4,6},{6,4},{8,10},{10,8},{12,14},{14,12},{16,18},{18,... | collective-permute-start | bytes 393224 | tf_op jit(solution)/shard_map/ppermute | solution.py:179
  56.0 5.2 %collective-permute-start.19 = (bf16[64,1024]{1,0:T(8,128)(2,1)S(1)}, bf16[64,1024]{1,0:T(8,128)(2,1)S(1)}, u32[]{:S(2)}, u32[]{:S(2)}) collective-permute-start(bf16[64,1024]{1,0:T(8,128)(2,1)S(1)} %collective-permute-done.15), channel_id=1, source_target_pairs={{0,2},{2,0},{4,6},{6,4},{8,10},{10,8},{12,14},{14,12},{16,18},{18,... | collective-permute-start | bytes 393224 | tf_op jit(solution)/shard_map/ppermute | solution.py:179
  57.7 5.0 %collective-permute-start.20 = (bf16[64,1024]{1,0:T(8,128)(2,1)S(1)}, bf16[64,1024]{1,0:T(8,128)(2,1)S(1)}, u32[]{:S(2)}, u32[]{:S(2)}) collective-permute-start(bf16[64,1024]{1,0:T(8,128)(2,1)S(1)} %collective-permute-done.16), channel_id=1, source_target_pairs={{0,2},{2,0},{4,6},{6,4},{8,10},{10,8},{12,14},{14,12},{16,18},{18,... | collective-permute-start | bytes 393224 | tf_op jit(solution)/shard_map/ppermute | solution.py:179
  (4 other events, 11.6 us)

commit v3 on v2

--- a/solution.py
+++ b/solution.py
@@ -70,8 +70,8 @@
 
 def transform(table, values):
     period, rows = table.shape[1], values.shape[0]
-    out = jnp.dot(table[:period, :rows], values, preferred_element_type=F32)
-    return out + jnp.dot(table[:period, rows : 2 * rows], values, preferred_element_type=F32)
+    twice = jnp.concatenate([values, values], 0)
+    return jnp.dot(table[:period, : 2 * rows], twice, preferred_element_type=F32)
 
 
 def early_kernel(px, py, tile, table, history, taps, *refs):
@@ -138,10 +138,9 @@
             high = product.astype(BF16)
             low = (product - high.astype(F32)).astype(BF16)
             i_high, i_low = table[period : period + tokens, :], table[period + tokens :, :]
-            total = jnp.dot(i_high, high, preferred_element_type=F32)
-            total = total + jnp.dot(i_high, low, preferred_element_type=F32)
-            total = total + jnp.dot(i_low, high, preferred_element_type=F32)
-            conv[dx, :, cols] = total
+            wide_table = jnp.concatenate([i_high, i_high, i_low], 1)
+            stacked = jnp.concatenate([high, low, high], 0)
+            conv[dx, :, cols] = jnp.dot(wide_table, stacked, preferred_element_type=F32)
         return 0
 
     lax.fori_loop(0, width // tile, step, 0)
@@ -252,10 +251,19 @@
         total = total + jnp.dot(jnp.concatenate(across, 0), weight, preferred_element_type=F32)
     total = total.astype(BF16).reshape(nz, group, -1)
     total = jnp.roll(total, z, axis=0).reshape(tokens, -1)
-    final = lax.all_to_all(total, ("hist", "chan"), split_axis=0, concat_axis=0, tiled=True)
     share = owned // chans
-    final = final.reshape(hists, chans, share, -1).astype(F32).sum(1).astype(BF16)
-    return final.transpose(1, 0, 2).reshape(share, -1)
+    total = total.reshape(hists, chans, share, -1)
+    if chans == 2:
+        c = lax.axis_index("chan")
+        sent = lax.dynamic_index_in_dim(total, 1 - c, 1, keepdims=False)
+        kept = lax.dynamic_index_in_dim(total, c, 1, keepdims=False)
+        sent = lax.ppermute(sent, "chan", [(0, 1), (1, 0)])
+        total = kept.astype(F32) + sent.astype(F32)
+    else:
+        total = lax.psum_scatter(total.astype(F32), "chan", scatter_dimension=1)
+    total = total.astype(BF16).reshape(hists * share, -1)
+    final = lax.all_to_all(total, "hist", split_axis=0, concat_axis=0, tiled=True)
+    return final.reshape(hists, share, -1).transpose(1, 0, 2).reshape(share, -1)
 
 
 def solution(mesh):

time: 77.6 us -> 76.1 us (0.981)
  blocking collectives: 13.4 us -> 10.6 us
  waiting for transfers between devices: 20 us -> 21.3 us
    all_to_all x1, blocking collectives: 13.4 us -> 10.6 us  [local(): lax.all_to_all(total, 'hist', split_axis=0, concat_axis=0, tiled=True)]
    ppermute x0 -> x1, waiting for transfers between devices: none -> 1.33 us  [local(): sent = lax.ppermute(sent, 'chan', [(0, 1), (1, 0)])]
  transfers between devices with their start and end apart: 21 -> 22, of which waited for: 10 -> 11; matrix products, arithmetic and copies ran while one was open for 1% -> 1% of each run, Pallas kernels for 7% -> 7%
where the time goes in v3:
time: 76.1 us; the launch traced here: 75.9 us
  starting transfers between devices  32 us (42%)
  waiting for transfers between devices  21.3 us (28%)
  blocking collectives  10.6 us (14%)
  Pallas kernels  7.51 us (10%)
  local copies, waits for them, and re-layouts  3.15 us (4%)
  matrix products  0.87 us (1%)
    ppermute x21, starting transfers between devices, move(): return lax.ppermute(value, ('seq', 'hist'), pairs)  31.9 us
    ppermute x21, waiting for transfers between devices, move(): return lax.ppermute(value, ('seq', 'hist'), pairs)  20 us
    all_to_all x1, blocking collectives, local(): lax.all_to_all(total, 'hist', split_axis=0, concat_axis=0, tiled=True)  10.6 us
    pallas_call x1, Pallas kernels, local(): pl.pallas_call(functools.partial(conv_kernel, px, py, nz, tile), out_shap...  3.81 us
    pallas_call x1, Pallas kernels, local(): pl.pallas_call(functools.partial(pick_kernel, px, py, width), out_shape=s...  2.56 us
    unnamed x14, local copies, waits for them, and re-layouts  2.47 us
  transfers between devices with their start and end apart: 22, of which 11 were waited for; matrix products, arithmetic and copies ran while one was open for 1% of the time, Pallas kernels for 7%

profile of v3, /device:TPU:0, one launch (start us, length us, event | category | flops | bytes accessed | tf_op | source)
XLA Modules:
  0.0 75.9 jit_solution(5359472281862260548)
XLA Ops:
  0.0 2.6 %shard_map.55 = (bf16[256,512]{1,0:T(8,128)(2,1)}, bf16[256,512]{1,0:T(8,128)(2,1)}, bf16[256,512]{1,0:T(8,128)(2,1)}, bf16[256,512]{1,0:T(8,128)(2,1)}, bf16[25...) custom-call(bf16[256,2048]{1,0:T(8,128)(2,1)} %history.3, bf16[256,2048]{1,0:T(8,128)(2,1)} %taps.3, bf16[32,2048]{1,0:T(8,128)(2,1)} %gates.1), custom_call_target="tpu_custom_call" | custom-call | tf_op jit(solution)/shard_map/pallas_call | solution.py:191
  2.6 3.1 %collective-permute-start = (bf16[256,512]{1,0:T(8,128)(2,1)}, bf16[256,512]{1,0:T(8,128)(2,1)S(1)}, u32[]{:S(2)}, u32[]{:S(2)}) collective-permute-start(bf16[256,512]{1,0:T(8,128)(2,1)} %get-tuple-element.22), channel_id=1, source_target_pairs={{0,2},{2,0},{4,6},{6,4},{8,10},{10,8},{12,14},{14,12},{16,18},{18,... | collective-permute-start | bytes 786440 | tf_op jit(solution)/shard_map/ppermute | solution.py:178
  5.6 1.3 %collective-permute-start.1 = (bf16[256,512]{1,0:T(8,128)(2,1)}, bf16[256,512]{1,0:T(8,128)(2,1)S(1)}, u32[]{:S(2)}, u32[]{:S(2)}) collective-permute-start(bf16[256,512]{1,0:T(8,128)(2,1)} %get-tuple-element.26), channel_id=1, source_target_pairs={{4,0},{8,4},{12,8},{20,16},{24,20},{28,24},{5,1},{9,5},{13,9},{21,... | collective-permute-start | bytes 786440 | tf_op jit(solution)/shard_map/ppermute | solution.py:178
  7.0 1.6 %collective-permute-start.4 = (bf16[256,512]{1,0:T(8,128)(2,1)}, bf16[256,512]{1,0:T(8,128)(2,1)S(1)}, u32[]{:S(2)}, u32[]{:S(2)}) collective-permute-start(bf16[256,512]{1,0:T(8,128)(2,1)} %get-tuple-element.28), channel_id=1, source_target_pairs={{0,16},{2,18},{4,20},{6,22},{8,24},{10,26},{12,28},{14,30},{16,0},... | collective-permute-start | bytes 786440 | tf_op jit(solution)/shard_map/ppermute | solution.py:178
  8.5 1.9 %collective-permute-start.5 = (bf16[256,512]{1,0:T(8,128)(2,1)}, bf16[256,512]{1,0:T(8,128)(2,1)S(1)}, u32[]{:S(2)}, u32[]{:S(2)}) collective-permute-start(bf16[256,512]{1,0:T(8,128)(2,1)} %get-tuple-element.29), channel_id=1, source_target_pairs={{0,18},{2,16},{4,22},{6,20},{8,26},{10,24},{12,30},{14,28},{16,2},... | collective-permute-start | bytes 786440 | tf_op jit(solution)/shard_map/ppermute | solution.py:178
  10.5 2.5 %collective-permute-done.refs_0_ = bf16[256,512]{1,0:T(8,128)(2,1)S(1)} collective-permute-done((bf16[256,512]{1,0:T(8,128)(2,1)}, bf16[256,512]{1,0:T(8,128)(2,1)S(1)}, u32[]{:S(2)}, u32[]{:S(2)}) %collective-permute-start) | collective-permute-done | bytes 262176 | tf_op jit(solution)/shard_map/ppermute | solution.py:178
  14.9 1.2 %copy-done.3 = bf16[1024,512]{1,0:T(8,128)(2,1)S(1)} copy-done((bf16[1024,512]{1,0:T(8,128)(2,1)S(1)}, bf16[1024,512]{1,0:T(8,128)(2,1)}, u32[]{:S(2)}) %copy-start.3) | copy-done | bytes 1048600
  17.3 2.7 %collective-permute-start.13 = (bf16[32,1024]{1,0:T(8,128)(2,1)S(1)}, bf16[32,1024]{1,0:T(8,128)(2,1)S(1)}, u32[]{:S(2)}, u32[]{:S(2)}) collective-permute-start(bf16[32,1024]{1,0:T(8,128)(2,1)S(1)} %copy-done.6), channel_id=1, source_target_pairs={{0,2},{2,0},{4,6},{6,4},{8,10},{10,8},{12,14},{14,12},{16,18},{18,... | collective-permute-start | bytes 196616 | tf_op jit(solution)/shard_map/ppermute | solution.py:178
  20.0 4.1 %collective-permute-done.3.refs_5_ = bf16[256,512]{1,0:T(8,128)(2,1)S(1)} collective-permute-done((bf16[256,512]{1,0:T(8,128)(2,1)}, bf16[256,512]{1,0:T(8,128)(2,1)S(1)}, u32[]{:S(2)}, u32[]{:S(2)}) %collective-permute-start.3) | collective-permute-done | bytes 262176 | tf_op jit(solution)/shard_map/ppermute | solution.py:178
  24.1 3.8 %shard_map.57 = (f32[64,512]{1,0:T(8,128)S(1)}, bf16[64,512]{1,0:T(8,128)(2,1)S(1)}, bf16[64,512]{1,0:T(8,128)(2,1)S(1)}, bf16[64,512]{1,0:T(8,128)(2,1)S(1)}, b...) custom-call(bf16[1024,512]{1,0:T(8,128)(2,1)S(1)} %copy-done.4, ...), custom_call_target="tpu_custom_call" | custom-call | flops 1879048192 | bytes 1048576 | tf_op jit(solution)/shard_map/pallas_call | solution.py:224
  27.9 2.8 %collective-permute-start.10 = (bf16[64,512]{1,0:T(8,128)(2,1)S(1)}, bf16[64,512]{1,0:T(8,128)(2,1)S(1)}, u32[]{:S(2)}, u32[]{:S(2)}) collective-permute-start(bf16[64,512]{1,0:T(8,128)(2,1)S(1)} %get-tuple-element.35), channel_id=1, source_target_pairs={{0,20},{2,22},{4,24},{6,26},{8,28},{10,30},{12,16},{14,18},{16,4},... | collective-permute-start | bytes 196616 | tf_op jit(solution)/shard_map/ppermute | solution.py:178
  30.7 2.6 %collective-permute-start.11 = (bf16[64,512]{1,0:T(8,128)(2,1)S(1)}, bf16[64,512]{1,0:T(8,128)(2,1)S(1)}, u32[]{:S(2)}, u32[]{:S(2)}) collective-permute-start(bf16[64,512]{1,0:T(8,128)(2,1)S(1)} %get-tuple-element.36), channel_id=1, source_target_pairs={{0,24},{2,26},{4,28},{6,30},{8,16},{10,18},{12,20},{14,22},{16,8},... | collective-permute-start | bytes 196616 | tf_op jit(solution)/shard_map/ppermute | solution.py:178
  33.3 2.3 %collective-permute-start.12 = (bf16[64,512]{1,0:T(8,128)(2,1)S(1)}, bf16[64,512]{1,0:T(8,128)(2,1)S(1)}, u32[]{:S(2)}, u32[]{:S(2)}) collective-permute-start(bf16[64,512]{1,0:T(8,128)(2,1)S(1)} %get-tuple-element.37), channel_id=1, source_target_pairs={{0,28},{2,30},{4,16},{6,18},{8,20},{10,22},{12,24},{14,26},{16,12}... | collective-permute-start | bytes 196616 | tf_op jit(solution)/shard_map/ppermute | solution.py:178
  36.6 2.9 %collective-permute-start.8 = (bf16[64,512]{1,0:T(8,128)(2,1)S(1)}, bf16[64,512]{1,0:T(8,128)(2,1)S(1)}, u32[]{:S(2)}, u32[]{:S(2)}) collective-permute-start(bf16[64,512]{1,0:T(8,128)(2,1)S(1)} %get-tuple-element.33), channel_id=1, source_target_pairs={{0,12},{2,14},{4,0},{6,2},{8,4},{10,6},{12,8},{14,10},{16,28},{18,... | collective-permute-start | bytes 196616 | tf_op jit(solution)/shard_map/ppermute | solution.py:178
  40.0 1.7 %collective-permute-done.6 = bf16[64,512]{1,0:T(8,128)(2,1)S(1)} collective-permute-done((bf16[64,512]{1,0:T(8,128)(2,1)S(1)}, bf16[64,512]{1,0:T(8,128)(2,1)S(1)}, u32[]{:S(2)}, u32[]{:S(2)}) %collective-permute-start.6) | collective-permute-done | bytes 65568 | tf_op jit(solution)/shard_map/ppermute | solution.py:178
  44.0 4.0 %collective-permute-start.14 = (bf16[64,1024]{1,0:T(8,128)(2,1)S(1)}, bf16[64,1024]{1,0:T(8,128)(2,1)S(1)}, u32[]{:S(2)}, u32[]{:S(2)}) collective-permute-start(bf16[64,1024]{1,0:T(8,128)(2,1)S(1)} %fusion.19), channel_id=1, source_target_pairs={{0,12},{2,14},{4,0},{6,2},{8,4},{10,6},{12,8},{14,10},{16,28},{18,... | collective-permute-start | bytes 393224 | tf_op jit(solution)/shard_map/ppermute | solution.py:178
  49.4 2.1 %collective-permute-done.14 = bf16[64,1024]{1,0:T(8,128)(2,1)S(1)} collective-permute-done((bf16[64,1024]{1,0:T(8,128)(2,1)S(1)}, bf16[64,1024]{1,0:T(8,128)(2,1)S(1)}, u32[]{:S(2)}, u32[]{:S(2)}) %collective-permute-start.14) | collective-permute-done | bytes 131104 | tf_op jit(solution)/shard_map/ppermute | solution.py:178
  51.5 1.3 %collective-permute-start.18 = (bf16[64,1024]{1,0:T(8,128)(2,1)S(1)}, bf16[64,1024]{1,0:T(8,128)(2,1)S(1)}, u32[]{:S(2)}, u32[]{:S(2)}) collective-permute-start(bf16[64,1024]{1,0:T(8,128)(2,1)S(1)} %collective-permute-done.14), channel_id=1, source_target_pairs={{0,2},{2,0},{4,6},{6,4},{8,10},{10,8},{12,14},{14,12},{16,18},{18,... | collective-permute-start | bytes 393224 | tf_op jit(solution)/shard_map/ppermute | solution.py:178
  52.8 3.1 %collective-permute-done.15 = bf16[64,1024]{1,0:T(8,128)(2,1)S(1)} collective-permute-done((bf16[64,1024]{1,0:T(8,128)(2,1)S(1)}, bf16[64,1024]{1,0:T(8,128)(2,1)S(1)}, u32[]{:S(2)}, u32[]{:S(2)}) %collective-permute-start.15) | collective-permute-done | bytes 131104 | tf_op jit(solution)/shard_map/ppermute | solution.py:178
  55.9 1.7 %collective-permute-start.19 = (bf16[64,1024]{1,0:T(8,128)(2,1)S(1)}, bf16[64,1024]{1,0:T(8,128)(2,1)S(1)}, u32[]{:S(2)}, u32[]{:S(2)}) collective-permute-start(bf16[64,1024]{1,0:T(8,128)(2,1)S(1)} %collective-permute-done.15), channel_id=1, source_target_pairs={{0,2},{2,0},{4,6},{6,4},{8,10},{10,8},{12,14},{14,12},{16,18},{18,... | collective-permute-start | bytes 393224 | tf_op jit(solution)/shard_map/ppermute | solution.py:178
  58.4 2.7 %collective-permute-done.19 = bf16[64,1024]{1,0:T(8,128)(2,1)S(1)} collective-permute-done((bf16[64,1024]{1,0:T(8,128)(2,1)S(1)}, bf16[64,1024]{1,0:T(8,128)(2,1)S(1)}, u32[]{:S(2)}, u32[]{:S(2)}) %collective-permute-start.19) | collective-permute-done | bytes 131104 | tf_op jit(solution)/shard_map/ppermute | solution.py:178
  61.1 1.5 %collective-permute-done.20 = bf16[64,1024]{1,0:T(8,128)(2,1)S(1)} collective-permute-done((bf16[64,1024]{1,0:T(8,128)(2,1)S(1)}, bf16[64,1024]{1,0:T(8,128)(2,1)S(1)}, u32[]{:S(2)}, u32[]{:S(2)}) %collective-permute-start.20) | collective-permute-done | bytes 131104 | tf_op jit(solution)/shard_map/ppermute | solution.py:178
  63.3 1.3 %collective-permute-done.21 = bf16[8,16,512]{2,1,0:T(8,128)(2,1)S(1)} collective-permute-done((bf16[8,16,512]{2,1,0:T(8,128)(2,1)S(1)}, bf16[8,16,512]{2,1,0:T(8,128)(2,1)S(1)}, u32[]{:S(2)}, u32[]{:S(2)}) %collective-permute-start.21) | collective-permute-done | bytes 131104 | tf_op jit(solution)/shard_map/ppermute | solution.py:260
  64.6 10.6 %all_to_all.6 = bf16[8,16,512]{2,1,0:T(8,128)(2,1)S(1)} all-to-all(bf16[8,16,512]{2,1,0:T(8,128)(2,1)S(1)} %fusion.20), channel_id=1, replica_groups=mesh['seq'=2,'hist'=8,'chan'=2] {'hist'}, dimensions={0} | all-to-all | bytes 262144 | tf_op jit(solution)/shard_map/all_to_all | solution.py:265
  (47 shorter events, 10.5 us)
Async XLA Ops:
  0.0 57.9 %copy-start = (bf16[2048,512]{1,0:T(8,128)(2,1)S(1)}, bf16[2048,512]{1,0:T(8,128)(2,1)}, u32[]{:S(2)}) copy-start(bf16[2048,512]{1,0:T(8,128)(2,1)} %param.8) | copy-start | bytes 6291460
  2.6 10.4 %collective-permute-start = (bf16[256,512]{1,0:T(8,128)(2,1)}, bf16[256,512]{1,0:T(8,128)(2,1)S(1)}, u32[]{:S(2)}, u32[]{:S(2)}) collective-permute-start(bf16[256,512]{1,0:T(8,128)(2,1)} %get-tuple-element.22), channel_id=1, source_target_pairs={{0,2},{2,0},{4,6},{6,4},{8,10},{10,8},{12,14},{14,12},{16,18},{18,... | collective-permute-start | bytes 786440 | tf_op jit(solution)/shard_map/ppermute | solution.py:178
  5.6 11.6 %collective-permute-start.1 = (bf16[256,512]{1,0:T(8,128)(2,1)}, bf16[256,512]{1,0:T(8,128)(2,1)S(1)}, u32[]{:S(2)}, u32[]{:S(2)}) collective-permute-start(bf16[256,512]{1,0:T(8,128)(2,1)} %get-tuple-element.26), channel_id=1, source_target_pairs={{4,0},{8,4},{12,8},{20,16},{24,20},{28,24},{5,1},{9,5},{13,9},{21,... | collective-permute-start | bytes 786440 | tf_op jit(solution)/shard_map/ppermute | solution.py:178
  6.9 17.2 %collective-permute-start.3 = (bf16[256,512]{1,0:T(8,128)(2,1)}, bf16[256,512]{1,0:T(8,128)(2,1)S(1)}, u32[]{:S(2)}, u32[]{:S(2)}) collective-permute-start(bf16[256,512]{1,0:T(8,128)(2,1)} %get-tuple-element.27), channel_id=1, source_target_pairs={{0,2},{2,0},{4,6},{6,4},{8,10},{10,8},{12,14},{14,12},{16,18},{18,... | collective-permute-start | bytes 786440 | tf_op jit(solution)/shard_map/ppermute | solution.py:178
  7.0 17.1 %collective-permute-start.4 = (bf16[256,512]{1,0:T(8,128)(2,1)}, bf16[256,512]{1,0:T(8,128)(2,1)S(1)}, u32[]{:S(2)}, u32[]{:S(2)}) collective-permute-start(bf16[256,512]{1,0:T(8,128)(2,1)} %get-tuple-element.28), channel_id=1, source_target_pairs={{0,16},{2,18},{4,20},{6,22},{8,24},{10,26},{12,28},{14,30},{16,0},... | collective-permute-start | bytes 786440 | tf_op jit(solution)/shard_map/ppermute | solution.py:178
  8.5 15.5 %collective-permute-start.5 = (bf16[256,512]{1,0:T(8,128)(2,1)}, bf16[256,512]{1,0:T(8,128)(2,1)S(1)}, u32[]{:S(2)}, u32[]{:S(2)}) collective-permute-start(bf16[256,512]{1,0:T(8,128)(2,1)} %get-tuple-element.29), channel_id=1, source_target_pairs={{0,18},{2,16},{4,22},{6,20},{8,26},{10,24},{12,30},{14,28},{16,2},... | collective-permute-start | bytes 786440 | tf_op jit(solution)/shard_map/ppermute | solution.py:178
  13.0 11.1 %collective-permute-start.2 = (bf16[256,512]{1,0:T(8,128)(2,1)S(1)}, bf16[256,512]{1,0:T(8,128)(2,1)S(1)}, u32[]{:S(2)}, u32[]{:S(2)}) collective-permute-start(bf16[256,512]{1,0:T(8,128)(2,1)S(1)} %collective-permute-done.refs_0_), channel_id=1, source_target_pairs={{6,2},{10,6},{14,10},{22,18},{26,22},{30,26},{7,3},{11,7},{15,11},... | collective-permute-start | bytes 786440 | tf_op jit(solution)/shard_map/ppermute | solution.py:178
  17.3 18.9 %collective-permute-start.13 = (bf16[32,1024]{1,0:T(8,128)(2,1)S(1)}, bf16[32,1024]{1,0:T(8,128)(2,1)S(1)}, u32[]{:S(2)}, u32[]{:S(2)}) collective-permute-start(bf16[32,1024]{1,0:T(8,128)(2,1)S(1)} %copy-done.6), channel_id=1, source_target_pairs={{0,2},{2,0},{4,6},{6,4},{8,10},{10,8},{12,14},{14,12},{16,18},{18,... | collective-permute-start | bytes 196616 | tf_op jit(solution)/shard_map/ppermute | solution.py:178
  24.1 15.9 %copy-start.5 = (bf16[32,2048]{1,0:T(8,128)(2,1)S(1)}, bf16[32,2048]{1,0:T(8,128)(2,1)}, u32[]{:S(2)}) copy-start(bf16[32,2048]{1,0:T(8,128)(2,1)} %gates.1) | copy-start | bytes 393220
  27.9 8.6 %collective-permute-start.10 = (bf16[64,512]{1,0:T(8,128)(2,1)S(1)}, bf16[64,512]{1,0:T(8,128)(2,1)S(1)}, u32[]{:S(2)}, u32[]{:S(2)}) collective-permute-start(bf16[64,512]{1,0:T(8,128)(2,1)S(1)} %get-tuple-element.35), channel_id=1, source_target_pairs={{0,20},{2,22},{4,24},{6,26},{8,28},{10,30},{12,16},{14,18},{16,4},... | collective-permute-start | bytes 196616 | tf_op jit(solution)/shard_map/ppermute | solution.py:178
  30.7 8.9 %collective-permute-start.11 = (bf16[64,512]{1,0:T(8,128)(2,1)S(1)}, bf16[64,512]{1,0:T(8,128)(2,1)S(1)}, u32[]{:S(2)}, u32[]{:S(2)}) collective-permute-start(bf16[64,512]{1,0:T(8,128)(2,1)S(1)} %get-tuple-element.36), channel_id=1, source_target_pairs={{0,24},{2,26},{4,28},{6,30},{8,16},{10,18},{12,20},{14,22},{16,8},... | collective-permute-start | bytes 196616 | tf_op jit(solution)/shard_map/ppermute | solution.py:178
  33.3 6.7 %collective-permute-start.12 = (bf16[64,512]{1,0:T(8,128)(2,1)S(1)}, bf16[64,512]{1,0:T(8,128)(2,1)S(1)}, u32[]{:S(2)}, u32[]{:S(2)}) collective-permute-start(bf16[64,512]{1,0:T(8,128)(2,1)S(1)} %get-tuple-element.37), channel_id=1, source_target_pairs={{0,28},{2,30},{4,16},{6,18},{8,20},{10,22},{12,24},{14,26},{16,12}... | collective-permute-start | bytes 196616 | tf_op jit(solution)/shard_map/ppermute | solution.py:178
  35.5 6.2 %collective-permute-start.6 = (bf16[64,512]{1,0:T(8,128)(2,1)S(1)}, bf16[64,512]{1,0:T(8,128)(2,1)S(1)}, u32[]{:S(2)}, u32[]{:S(2)}) collective-permute-start(bf16[64,512]{1,0:T(8,128)(2,1)S(1)} %get-tuple-element.31), channel_id=1, source_target_pairs={{0,4},{2,6},{4,8},{6,10},{8,12},{10,14},{12,0},{14,2},{16,20},{18,... | collective-permute-start | bytes 196616 | tf_op jit(solution)/shard_map/ppermute | solution.py:178
  36.2 6.6 %collective-permute-start.7 = (bf16[64,512]{1,0:T(8,128)(2,1)S(1)}, bf16[64,512]{1,0:T(8,128)(2,1)S(1)}, u32[]{:S(2)}, u32[]{:S(2)}) collective-permute-start(bf16[64,512]{1,0:T(8,128)(2,1)S(1)} %get-tuple-element.32), channel_id=1, source_target_pairs={{0,8},{2,10},{4,12},{6,14},{8,0},{10,2},{12,4},{14,6},{16,24},{18,... | collective-permute-start | bytes 196616 | tf_op jit(solution)/shard_map/ppermute | solution.py:178
  36.6 6.3 %collective-permute-start.8 = (bf16[64,512]{1,0:T(8,128)(2,1)S(1)}, bf16[64,512]{1,0:T(8,128)(2,1)S(1)}, u32[]{:S(2)}, u32[]{:S(2)}) collective-permute-start(bf16[64,512]{1,0:T(8,128)(2,1)S(1)} %get-tuple-element.33), channel_id=1, source_target_pairs={{0,12},{2,14},{4,0},{6,2},{8,4},{10,6},{12,8},{14,10},{16,28},{18,... | collective-permute-start | bytes 196616 | tf_op jit(solution)/shard_map/ppermute | solution.py:178
  39.6 4.3 %collective-permute-start.9 = (bf16[64,512]{1,0:T(8,128)(2,1)S(1)}, bf16[64,512]{1,0:T(8,128)(2,1)S(1)}, u32[]{:S(2)}, u32[]{:S(2)}) collective-permute-start(bf16[64,512]{1,0:T(8,128)(2,1)S(1)} %get-tuple-element.34), channel_id=1, source_target_pairs={{0,16},{2,18},{4,20},{6,22},{8,24},{10,26},{12,28},{14,30},{16,0},... | collective-permute-start | bytes 196616 | tf_op jit(solution)/shard_map/ppermute | solution.py:178
  44.0 7.5 %collective-permute-start.14 = (bf16[64,1024]{1,0:T(8,128)(2,1)S(1)}, bf16[64,1024]{1,0:T(8,128)(2,1)S(1)}, u32[]{:S(2)}, u32[]{:S(2)}) collective-permute-start(bf16[64,1024]{1,0:T(8,128)(2,1)S(1)} %fusion.19), channel_id=1, source_target_pairs={{0,12},{2,14},{4,0},{6,2},{8,4},{10,6},{12,8},{14,10},{16,28},{18,... | collective-permute-start | bytes 393224 | tf_op jit(solution)/shard_map/ppermute | solution.py:178
  47.9 7.9 %collective-permute-start.15 = (bf16[64,1024]{1,0:T(8,128)(2,1)S(1)}, bf16[64,1024]{1,0:T(8,128)(2,1)S(1)}, u32[]{:S(2)}, u32[]{:S(2)}) collective-permute-start(bf16[64,1024]{1,0:T(8,128)(2,1)S(1)} %fusion.19), channel_id=1, source_target_pairs={{0,8},{2,10},{4,12},{6,14},{8,0},{10,2},{12,4},{14,6},{16,24},{18,... | collective-permute-start | bytes 393224 | tf_op jit(solution)/shard_map/ppermute | solution.py:178
  47.9 9.7 %collective-permute-start.16 = (bf16[64,1024]{1,0:T(8,128)(2,1)S(1)}, bf16[64,1024]{1,0:T(8,128)(2,1)S(1)}, u32[]{:S(2)}, u32[]{:S(2)}) collective-permute-start(bf16[64,1024]{1,0:T(8,128)(2,1)S(1)} %fusion.19), channel_id=1, source_target_pairs={{0,4},{2,6},{4,8},{6,10},{8,12},{10,14},{12,0},{14,2},{16,20},{18,... | collective-permute-start | bytes 393224 | tf_op jit(solution)/shard_map/ppermute | solution.py:178
  48.6 9.8 %collective-permute-start.17 = (bf16[64,1024]{1,0:T(8,128)(2,1)S(1)}, bf16[64,1024]{1,0:T(8,128)(2,1)S(1)}, u32[]{:S(2)}, u32[]{:S(2)}) collective-permute-start(bf16[64,1024]{1,0:T(8,128)(2,1)S(1)} %fusion.19), channel_id=1, source_target_pairs={{0,2},{2,0},{4,6},{6,4},{8,10},{10,8},{12,14},{14,12},{16,18},{18,... | collective-permute-start | bytes 393224 | tf_op jit(solution)/shard_map/ppermute | solution.py:178
  51.5 6.9 %collective-permute-start.18 = (bf16[64,1024]{1,0:T(8,128)(2,1)S(1)}, bf16[64,1024]{1,0:T(8,128)(2,1)S(1)}, u32[]{:S(2)}, u32[]{:S(2)}) collective-permute-start(bf16[64,1024]{1,0:T(8,128)(2,1)S(1)} %collective-permute-done.14), channel_id=1, source_target_pairs={{0,2},{2,0},{4,6},{6,4},{8,10},{10,8},{12,14},{14,12},{16,18},{18,... | collective-permute-start | bytes 393224 | tf_op jit(solution)/shard_map/ppermute | solution.py:178
  55.9 5.2 %collective-permute-start.19 = (bf16[64,1024]{1,0:T(8,128)(2,1)S(1)}, bf16[64,1024]{1,0:T(8,128)(2,1)S(1)}, u32[]{:S(2)}, u32[]{:S(2)}) collective-permute-start(bf16[64,1024]{1,0:T(8,128)(2,1)S(1)} %collective-permute-done.15), channel_id=1, source_target_pairs={{0,2},{2,0},{4,6},{6,4},{8,10},{10,8},{12,14},{14,12},{16,18},{18,... | collective-permute-start | bytes 393224 | tf_op jit(solution)/shard_map/ppermute | solution.py:178
  57.6 5.0 %collective-permute-start.20 = (bf16[64,1024]{1,0:T(8,128)(2,1)S(1)}, bf16[64,1024]{1,0:T(8,128)(2,1)S(1)}, u32[]{:S(2)}, u32[]{:S(2)}) collective-permute-start(bf16[64,1024]{1,0:T(8,128)(2,1)S(1)} %collective-permute-done.16), channel_id=1, source_target_pairs={{0,2},{2,0},{4,6},{6,4},{8,10},{10,8},{12,14},{14,12},{16,18},{18,... | collective-permute-start | bytes 393224 | tf_op jit(solution)/shard_map/ppermute | solution.py:178
  63.2 1.4 %collective-permute-start.21 = (bf16[8,16,512]{2,1,0:T(8,128)(2,1)S(1)}, bf16[8,16,512]{2,1,0:T(8,128)(2,1)S(1)}, u32[]{:S(2)}, u32[]{:S(2)}) collective-permute-start(bf16[8,16,512]{2,1,0:T(8,128)(2,1)S(1)} %dynamic-slice_bitcast_fusion), channel_id=1, source_target_pairs={{0,1},{1,0},{2,3},{3,2},{4,5},{5,4},{6,7},{7,6},{8,9},{9,8},{10,11... | collective-permute-start | bytes 393224 | tf_op jit(solution)/shard_map/ppermute | solution.py:260
  (5 other events, 25.2 us)

commit v4 on v3

--- a/solution.py
+++ b/solution.py
@@ -89,6 +89,18 @@
         return 0
 
     lax.fori_loop(0, width // tile, step, 0)
+
+
+def more_kernel(tile, table, *refs):
+    values, outs = refs[: len(refs) // 2], refs[len(refs) // 2 :]
+
+    def step(number, _):
+        cols = pl.ds(pl.multiple_of(number * tile, tile), tile)
+        for out, value in zip(outs, values):
+            out[:, cols] = transform(table, value[:, cols])
+        return 0
+
+    lax.fori_loop(0, outs[0].shape[1] // tile, step, 0)
 
 
 def conv_kernel(px, py, nz, tile, table, *refs):
@@ -130,7 +142,12 @@
             real, imag = None, None
             for dy in range(py):
                 here = inputs[dx][dy]
-                out = own_input[:, cols] if here is None else transform(table, here[:, cols])
+                if here is None:
+                    out = own_input[:, cols]
+                elif dy == 0:
+                    out = here[:, cols]
+                else:
+                    out = transform(table, here[:, cols])
                 (tc, ts), ic, is_ = spec[dy], out[:modes], out[modes:]
                 re, im = tc * ic + ts * is_, tc * is_ - ts * ic
                 real, imag = (re, im) if dy == 0 else (real + re, imag + im)
@@ -220,6 +237,17 @@
         compiler_params=params,
         cost_estimate=pl.CostEstimate(flops=3 * flops, bytes_accessed=rows * width * 8, transcendentals=0),
     )(table, history, filter_taps, *peers)
+    for dx in range(1, px):
+        whole = jax.ShapeDtypeStruct((rows + tokens, width), F32)
+        n = dx * py - 1
+        inputs[n] = pl.pallas_call(
+            functools.partial(more_kernel, tile),
+            out_shape=[whole],
+            in_specs=[vmem] * 2,
+            out_specs=[vmem],
+            compiler_params=params,
+            cost_estimate=pl.CostEstimate(flops=flops, bytes_accessed=rows * width * 8, transcendentals=0),
+        )(table, inputs[n])[0]
     part = lambda own: jax.ShapeDtypeStruct((group, width), F32 if own else BF16)
     contributions = pl.pallas_call(
         functools.partial(conv_kernel, px, py, nz, tile),

time: 76.1 us -> 75.1 us (0.987)
  local copies, waits for them, and re-layouts: 3.15 us -> 1.92 us
    unnamed x14 -> x10, local copies, waits for them, and re-layouts: 2.47 us -> 1.24 us
    pallas_call x1, Pallas kernels: 3.81 us -> 2.87 us  [local(): pl.pallas_call(functools.partial(conv_kernel, px, py, nz, tile), out_shap...]
  transfers between devices with their start and end apart: 22 -> 22, of which waited for: 11 -> 12; matrix products, arithmetic and copies ran while one was open for 1% -> 1% of each run, Pallas kernels for 7% -> 6%
where the time goes in v4:
time: 75.1 us; the launch traced here: 74.9 us
  starting transfers between devices  32.5 us (43%)
  waiting for transfers between devices  21.5 us (29%)
  blocking collectives  10.5 us (14%)
  Pallas kernels  7.19 us (10%)
  local copies, waits for them, and re-layouts  1.92 us (3%)
  matrix products  0.87 us (1%)
    ppermute x21, starting transfers between devices, move(): return lax.ppermute(value, ('seq', 'hist'), pairs)  32.4 us
    ppermute x21, waiting for transfers between devices, move(): return lax.ppermute(value, ('seq', 'hist'), pairs)  20.1 us
    all_to_all x1, blocking collectives, local(): lax.all_to_all(total, 'hist', split_axis=0, concat_axis=0, tiled=True)  10.5 us
    pallas_call x1, Pallas kernels, local(): pl.pallas_call(functools.partial(conv_kernel, px, py, nz, tile), out_shap...  2.87 us
    pallas_call x1, Pallas kernels, local(): pl.pallas_call(functools.partial(pick_kernel, px, py, width), out_shape=s...  2.56 us
  transfers between devices with their start and end apart: 22, of which 12 were waited for; matrix products, arithmetic and copies ran while one was open for 1% of the time, Pallas kernels for 6%

profile of v4, /device:TPU:0, one launch (start us, length us, event | category | flops | bytes accessed | tf_op | source)
XLA Modules:
  0.0 74.9 jit_solution(15455984497298090189)
XLA Ops:
  0.0 2.6 %shard_map.55 = (bf16[256,512]{1,0:T(8,128)(2,1)}, bf16[256,512]{1,0:T(8,128)(2,1)}, bf16[256,512]{1,0:T(8,128)(2,1)}, bf16[256,512]{1,0:T(8,128)(2,1)}, bf16[25...) custom-call(bf16[256,2048]{1,0:T(8,128)(2,1)} %history.3, bf16[256,2048]{1,0:T(8,128)(2,1)} %taps.3, bf16[32,2048]{1,0:T(8,128)(2,1)} %gates.1), custom_call_target="tpu_custom_call" | custom-call | tf_op jit(solution)/shard_map/pallas_call | solution.py:208
  2.6 3.1 %collective-permute-start = (bf16[256,512]{1,0:T(8,128)(2,1)}, bf16[256,512]{1,0:T(8,128)(2,1)S(1)}, u32[]{:S(2)}, u32[]{:S(2)}) collective-permute-start(bf16[256,512]{1,0:T(8,128)(2,1)} %get-tuple-element.22), channel_id=1, source_target_pairs={{0,2},{2,0},{4,6},{6,4},{8,10},{10,8},{12,14},{14,12},{16,18},{18,... | collective-permute-start | bytes 786440 | tf_op jit(solution)/shard_map/ppermute | solution.py:195
  5.6 1.5 %collective-permute-start.4 = (bf16[256,512]{1,0:T(8,128)(2,1)}, bf16[256,512]{1,0:T(8,128)(2,1)S(1)}, u32[]{:S(2)}, u32[]{:S(2)}) collective-permute-start(bf16[256,512]{1,0:T(8,128)(2,1)} %get-tuple-element.28), channel_id=1, source_target_pairs={{0,16},{2,18},{4,20},{6,22},{8,24},{10,26},{12,28},{14,30},{16,0},... | collective-permute-start | bytes 786440 | tf_op jit(solution)/shard_map/ppermute | solution.py:195
  7.1 1.3 %collective-permute-start.1 = (bf16[256,512]{1,0:T(8,128)(2,1)}, bf16[256,512]{1,0:T(8,128)(2,1)S(1)}, u32[]{:S(2)}, u32[]{:S(2)}) collective-permute-start(bf16[256,512]{1,0:T(8,128)(2,1)} %get-tuple-element.26), channel_id=1, source_target_pairs={{4,0},{8,4},{12,8},{20,16},{24,20},{28,24},{5,1},{9,5},{13,9},{21,... | collective-permute-start | bytes 786440 | tf_op jit(solution)/shard_map/ppermute | solution.py:195
  8.5 2.0 %collective-permute-start.5 = (bf16[256,512]{1,0:T(8,128)(2,1)}, bf16[256,512]{1,0:T(8,128)(2,1)S(1)}, u32[]{:S(2)}, u32[]{:S(2)}) collective-permute-start(bf16[256,512]{1,0:T(8,128)(2,1)} %get-tuple-element.29), channel_id=1, source_target_pairs={{0,18},{2,16},{4,22},{6,20},{8,26},{10,24},{12,30},{14,28},{16,2},... | collective-permute-start | bytes 786440 | tf_op jit(solution)/shard_map/ppermute | solution.py:195
  10.5 3.2 %collective-permute-done.refs_0_ = bf16[256,512]{1,0:T(8,128)(2,1)S(1)} collective-permute-done((bf16[256,512]{1,0:T(8,128)(2,1)}, bf16[256,512]{1,0:T(8,128)(2,1)S(1)}, u32[]{:S(2)}, u32[]{:S(2)}) %collective-permute-start) | collective-permute-done | bytes 262176 | tf_op jit(solution)/shard_map/ppermute | solution.py:195
  15.1 2.8 %collective-permute-start.13 = (bf16[32,1024]{1,0:T(8,128)(2,1)}, bf16[32,1024]{1,0:T(8,128)(2,1)S(1)}, u32[]{:S(2)}, u32[]{:S(2)}) collective-permute-start(bf16[32,1024]{1,0:T(8,128)(2,1)} %get-tuple-element.38), channel_id=1, source_target_pairs={{0,2},{2,0},{4,6},{6,4},{8,10},{10,8},{12,14},{14,12},{16,18},{18,... | collective-permute-start | bytes 196616 | tf_op jit(solution)/shard_map/ppermute | solution.py:195
  20.9 3.2 %collective-permute-done.3.refs_5_ = bf16[256,512]{1,0:T(8,128)(2,1)S(1)} collective-permute-done((bf16[256,512]{1,0:T(8,128)(2,1)}, bf16[256,512]{1,0:T(8,128)(2,1)S(1)}, u32[]{:S(2)}, u32[]{:S(2)}) %collective-permute-start.3) | collective-permute-done | bytes 262176 | tf_op jit(solution)/shard_map/ppermute | solution.py:195
  24.1 2.9 %shard_map.58 = (f32[64,512]{1,0:T(8,128)S(1)}, bf16[64,512]{1,0:T(8,128)(2,1)S(1)}, bf16[64,512]{1,0:T(8,128)(2,1)S(1)}, bf16[64,512]{1,0:T(8,128)(2,1)S(1)}, b...) custom-call(bf16[1024,512]{1,0:T(8,128)(2,1)S(1)} %copy-done.3, ...), custom_call_target="tpu_custom_call" | custom-call | flops 1879048192 | bytes 1048576 | tf_op jit(solution)/shard_map/pallas_call | solution.py:252
  27.0 2.8 %collective-permute-start.10 = (bf16[64,512]{1,0:T(8,128)(2,1)S(1)}, bf16[64,512]{1,0:T(8,128)(2,1)S(1)}, u32[]{:S(2)}, u32[]{:S(2)}) collective-permute-start(bf16[64,512]{1,0:T(8,128)(2,1)S(1)} %get-tuple-element.35), channel_id=1, source_target_pairs={{0,20},{2,22},{4,24},{6,26},{8,28},{10,30},{12,16},{14,18},{16,4},... | collective-permute-start | bytes 196616 | tf_op jit(solution)/shard_map/ppermute | solution.py:195
  29.8 2.6 %collective-permute-start.11 = (bf16[64,512]{1,0:T(8,128)(2,1)S(1)}, bf16[64,512]{1,0:T(8,128)(2,1)S(1)}, u32[]{:S(2)}, u32[]{:S(2)}) collective-permute-start(bf16[64,512]{1,0:T(8,128)(2,1)S(1)} %get-tuple-element.36), channel_id=1, source_target_pairs={{0,24},{2,26},{4,28},{6,30},{8,16},{10,18},{12,20},{14,22},{16,8},... | collective-permute-start | bytes 196616 | tf_op jit(solution)/shard_map/ppermute | solution.py:195
  32.3 2.3 %collective-permute-start.12 = (bf16[64,512]{1,0:T(8,128)(2,1)S(1)}, bf16[64,512]{1,0:T(8,128)(2,1)S(1)}, u32[]{:S(2)}, u32[]{:S(2)}) collective-permute-start(bf16[64,512]{1,0:T(8,128)(2,1)S(1)} %get-tuple-element.37), channel_id=1, source_target_pairs={{0,28},{2,30},{4,16},{6,18},{8,20},{10,22},{12,24},{14,26},{16,12}... | collective-permute-start | bytes 196616 | tf_op jit(solution)/shard_map/ppermute | solution.py:195
  35.6 2.9 %collective-permute-start.8 = (bf16[64,512]{1,0:T(8,128)(2,1)S(1)}, bf16[64,512]{1,0:T(8,128)(2,1)S(1)}, u32[]{:S(2)}, u32[]{:S(2)}) collective-permute-start(bf16[64,512]{1,0:T(8,128)(2,1)S(1)} %get-tuple-element.33), channel_id=1, source_target_pairs={{0,12},{2,14},{4,0},{6,2},{8,4},{10,6},{12,8},{14,10},{16,28},{18,... | collective-permute-start | bytes 196616 | tf_op jit(solution)/shard_map/ppermute | solution.py:195
  39.2 1.6 %collective-permute-done.6 = bf16[64,512]{1,0:T(8,128)(2,1)S(1)} collective-permute-done((bf16[64,512]{1,0:T(8,128)(2,1)S(1)}, bf16[64,512]{1,0:T(8,128)(2,1)S(1)}, u32[]{:S(2)}, u32[]{:S(2)}) %collective-permute-start.6) | collective-permute-done | bytes 65568 | tf_op jit(solution)/shard_map/ppermute | solution.py:195
  42.9 3.4 %collective-permute-start.14 = (bf16[64,1024]{1,0:T(8,128)(2,1)S(1)}, bf16[64,1024]{1,0:T(8,128)(2,1)S(1)}, u32[]{:S(2)}, u32[]{:S(2)}) collective-permute-start(bf16[64,1024]{1,0:T(8,128)(2,1)S(1)} %fusion.19), channel_id=1, source_target_pairs={{0,12},{2,14},{4,0},{6,2},{8,4},{10,6},{12,8},{14,10},{16,28},{18,... | collective-permute-start | bytes 393224 | tf_op jit(solution)/shard_map/ppermute | solution.py:195
  46.9 1.5 %collective-permute-start.17 = (bf16[64,1024]{1,0:T(8,128)(2,1)S(1)}, bf16[64,1024]{1,0:T(8,128)(2,1)S(1)}, u32[]{:S(2)}, u32[]{:S(2)}) collective-permute-start(bf16[64,1024]{1,0:T(8,128)(2,1)S(1)} %fusion.19), channel_id=1, source_target_pairs={{0,2},{2,0},{4,6},{6,4},{8,10},{10,8},{12,14},{14,12},{16,18},{18,... | collective-permute-start | bytes 393224 | tf_op jit(solution)/shard_map/ppermute | solution.py:195
  48.4 1.9 %collective-permute-done.14 = bf16[64,1024]{1,0:T(8,128)(2,1)S(1)} collective-permute-done((bf16[64,1024]{1,0:T(8,128)(2,1)S(1)}, bf16[64,1024]{1,0:T(8,128)(2,1)S(1)}, u32[]{:S(2)}, u32[]{:S(2)}) %collective-permute-start.14) | collective-permute-done | bytes 131104 | tf_op jit(solution)/shard_map/ppermute | solution.py:195
  50.3 1.5 %collective-permute-start.18 = (bf16[64,1024]{1,0:T(8,128)(2,1)S(1)}, bf16[64,1024]{1,0:T(8,128)(2,1)S(1)}, u32[]{:S(2)}, u32[]{:S(2)}) collective-permute-start(bf16[64,1024]{1,0:T(8,128)(2,1)S(1)} %collective-permute-done.14), channel_id=1, source_target_pairs={{0,2},{2,0},{4,6},{6,4},{8,10},{10,8},{12,14},{14,12},{16,18},{18,... | collective-permute-start | bytes 393224 | tf_op jit(solution)/shard_map/ppermute | solution.py:195
  51.8 3.3 %collective-permute-done.15 = bf16[64,1024]{1,0:T(8,128)(2,1)S(1)} collective-permute-done((bf16[64,1024]{1,0:T(8,128)(2,1)S(1)}, bf16[64,1024]{1,0:T(8,128)(2,1)S(1)}, u32[]{:S(2)}, u32[]{:S(2)}) %collective-permute-start.15) | collective-permute-done | bytes 131104 | tf_op jit(solution)/shard_map/ppermute | solution.py:195
  55.2 1.5 %collective-permute-start.19 = (bf16[64,1024]{1,0:T(8,128)(2,1)S(1)}, bf16[64,1024]{1,0:T(8,128)(2,1)S(1)}, u32[]{:S(2)}, u32[]{:S(2)}) collective-permute-start(bf16[64,1024]{1,0:T(8,128)(2,1)S(1)} %collective-permute-done.15), channel_id=1, source_target_pairs={{0,2},{2,0},{4,6},{6,4},{8,10},{10,8},{12,14},{14,12},{16,18},{18,... | collective-permute-start | bytes 393224 | tf_op jit(solution)/shard_map/ppermute | solution.py:195
  57.6 2.7 %collective-permute-done.19 = bf16[64,1024]{1,0:T(8,128)(2,1)S(1)} collective-permute-done((bf16[64,1024]{1,0:T(8,128)(2,1)S(1)}, bf16[64,1024]{1,0:T(8,128)(2,1)S(1)}, u32[]{:S(2)}, u32[]{:S(2)}) %collective-permute-start.19) | collective-permute-done | bytes 131104 | tf_op jit(solution)/shard_map/ppermute | solution.py:195
  60.3 1.4 %collective-permute-done.20 = bf16[64,1024]{1,0:T(8,128)(2,1)S(1)} collective-permute-done((bf16[64,1024]{1,0:T(8,128)(2,1)S(1)}, bf16[64,1024]{1,0:T(8,128)(2,1)S(1)}, u32[]{:S(2)}, u32[]{:S(2)}) %collective-permute-start.20) | collective-permute-done | bytes 131104 | tf_op jit(solution)/shard_map/ppermute | solution.py:195
  62.4 1.3 %collective-permute-done.21 = bf16[8,16,512]{2,1,0:T(8,128)(2,1)S(1)} collective-permute-done((bf16[8,16,512]{2,1,0:T(8,128)(2,1)S(1)}, bf16[8,16,512]{2,1,0:T(8,128)(2,1)S(1)}, u32[]{:S(2)}, u32[]{:S(2)}) %collective-permute-start.21) | collective-permute-done | bytes 131104 | tf_op jit(solution)/shard_map/ppermute | solution.py:288
  63.8 10.5 %all_to_all.6 = bf16[8,16,512]{2,1,0:T(8,128)(2,1)S(1)} all-to-all(bf16[8,16,512]{2,1,0:T(8,128)(2,1)S(1)} %fusion.20), channel_id=1, replica_groups=mesh['seq'=2,'hist'=8,'chan'=2] {'hist'}, dimensions={0} | all-to-all | bytes 262144 | tf_op jit(solution)/shard_map/all_to_all | solution.py:293
  (44 shorter events, 11.2 us)
Async XLA Ops:
  0.0 57.2 %copy-start = (bf16[2048,512]{1,0:T(8,128)(2,1)S(1)}, bf16[2048,512]{1,0:T(8,128)(2,1)}, u32[]{:S(2)}) copy-start(bf16[2048,512]{1,0:T(8,128)(2,1)} %param.8) | copy-start | bytes 6291460
  0.0 19.7 %copy-start.1 = (bf16[256,2048]{1,0:T(8,128)(2,1)S(1)}, bf16[256,2048]{1,0:T(8,128)(2,1)}, u32[]{:S(2)}) copy-start(bf16[256,2048]{1,0:T(8,128)(2,1)} %history.3) | copy-start | bytes 3145732
  2.6 11.1 %collective-permute-start = (bf16[256,512]{1,0:T(8,128)(2,1)}, bf16[256,512]{1,0:T(8,128)(2,1)S(1)}, u32[]{:S(2)}, u32[]{:S(2)}) collective-permute-start(bf16[256,512]{1,0:T(8,128)(2,1)} %get-tuple-element.22), channel_id=1, source_target_pairs={{0,2},{2,0},{4,6},{6,4},{8,10},{10,8},{12,14},{14,12},{16,18},{18,... | collective-permute-start | bytes 786440 | tf_op jit(solution)/shard_map/ppermute | solution.py:195
  5.6 9.4 %collective-permute-start.4 = (bf16[256,512]{1,0:T(8,128)(2,1)}, bf16[256,512]{1,0:T(8,128)(2,1)S(1)}, u32[]{:S(2)}, u32[]{:S(2)}) collective-permute-start(bf16[256,512]{1,0:T(8,128)(2,1)} %get-tuple-element.28), channel_id=1, source_target_pairs={{0,16},{2,18},{4,20},{6,22},{8,24},{10,26},{12,28},{14,30},{16,0},... | collective-permute-start | bytes 786440 | tf_op jit(solution)/shard_map/ppermute | solution.py:195
  7.1 13.7 %collective-permute-start.1 = (bf16[256,512]{1,0:T(8,128)(2,1)}, bf16[256,512]{1,0:T(8,128)(2,1)S(1)}, u32[]{:S(2)}, u32[]{:S(2)}) collective-permute-start(bf16[256,512]{1,0:T(8,128)(2,1)} %get-tuple-element.26), channel_id=1, source_target_pairs={{4,0},{8,4},{12,8},{20,16},{24,20},{28,24},{5,1},{9,5},{13,9},{21,... | collective-permute-start | bytes 786440 | tf_op jit(solution)/shard_map/ppermute | solution.py:195
  8.4 15.7 %collective-permute-start.3 = (bf16[256,512]{1,0:T(8,128)(2,1)}, bf16[256,512]{1,0:T(8,128)(2,1)S(1)}, u32[]{:S(2)}, u32[]{:S(2)}) collective-permute-start(bf16[256,512]{1,0:T(8,128)(2,1)} %get-tuple-element.27), channel_id=1, source_target_pairs={{0,2},{2,0},{4,6},{6,4},{8,10},{10,8},{12,14},{14,12},{16,18},{18,... | collective-permute-start | bytes 786440 | tf_op jit(solution)/shard_map/ppermute | solution.py:195
  8.5 15.6 %collective-permute-start.5 = (bf16[256,512]{1,0:T(8,128)(2,1)}, bf16[256,512]{1,0:T(8,128)(2,1)S(1)}, u32[]{:S(2)}, u32[]{:S(2)}) collective-permute-start(bf16[256,512]{1,0:T(8,128)(2,1)} %get-tuple-element.29), channel_id=1, source_target_pairs={{0,18},{2,16},{4,22},{6,20},{8,26},{10,24},{12,30},{14,28},{16,2},... | collective-permute-start | bytes 786440 | tf_op jit(solution)/shard_map/ppermute | solution.py:195
  13.7 10.4 %collective-permute-start.2 = (bf16[256,512]{1,0:T(8,128)(2,1)S(1)}, bf16[256,512]{1,0:T(8,128)(2,1)S(1)}, u32[]{:S(2)}, u32[]{:S(2)}) collective-permute-start(bf16[256,512]{1,0:T(8,128)(2,1)S(1)} %collective-permute-done.refs_0_), channel_id=1, source_target_pairs={{6,2},{10,6},{14,10},{22,18},{26,22},{30,26},{7,3},{11,7},{15,11},... | collective-permute-start | bytes 786440 | tf_op jit(solution)/shard_map/ppermute | solution.py:195
  15.1 20.2 %collective-permute-start.13 = (bf16[32,1024]{1,0:T(8,128)(2,1)}, bf16[32,1024]{1,0:T(8,128)(2,1)S(1)}, u32[]{:S(2)}, u32[]{:S(2)}) collective-permute-start(bf16[32,1024]{1,0:T(8,128)(2,1)} %get-tuple-element.38), channel_id=1, source_target_pairs={{0,2},{2,0},{4,6},{6,4},{8,10},{10,8},{12,14},{14,12},{16,18},{18,... | collective-permute-start | bytes 196616 | tf_op jit(solution)/shard_map/ppermute | solution.py:195
  27.0 8.6 %collective-permute-start.10 = (bf16[64,512]{1,0:T(8,128)(2,1)S(1)}, bf16[64,512]{1,0:T(8,128)(2,1)S(1)}, u32[]{:S(2)}, u32[]{:S(2)}) collective-permute-start(bf16[64,512]{1,0:T(8,128)(2,1)S(1)} %get-tuple-element.35), channel_id=1, source_target_pairs={{0,20},{2,22},{4,24},{6,26},{8,28},{10,30},{12,16},{14,18},{16,4},... | collective-permute-start | bytes 196616 | tf_op jit(solution)/shard_map/ppermute | solution.py:195
  29.8 8.7 %collective-permute-start.11 = (bf16[64,512]{1,0:T(8,128)(2,1)S(1)}, bf16[64,512]{1,0:T(8,128)(2,1)S(1)}, u32[]{:S(2)}, u32[]{:S(2)}) collective-permute-start(bf16[64,512]{1,0:T(8,128)(2,1)S(1)} %get-tuple-element.36), channel_id=1, source_target_pairs={{0,24},{2,26},{4,28},{6,30},{8,16},{10,18},{12,20},{14,22},{16,8},... | collective-permute-start | bytes 196616 | tf_op jit(solution)/shard_map/ppermute | solution.py:195
  32.3 6.8 %collective-permute-start.12 = (bf16[64,512]{1,0:T(8,128)(2,1)S(1)}, bf16[64,512]{1,0:T(8,128)(2,1)S(1)}, u32[]{:S(2)}, u32[]{:S(2)}) collective-permute-start(bf16[64,512]{1,0:T(8,128)(2,1)S(1)} %get-tuple-element.37), channel_id=1, source_target_pairs={{0,28},{2,30},{4,16},{6,18},{8,20},{10,22},{12,24},{14,26},{16,12}... | collective-permute-start | bytes 196616 | tf_op jit(solution)/shard_map/ppermute | solution.py:195
  34.6 6.2 %collective-permute-start.6 = (bf16[64,512]{1,0:T(8,128)(2,1)S(1)}, bf16[64,512]{1,0:T(8,128)(2,1)S(1)}, u32[]{:S(2)}, u32[]{:S(2)}) collective-permute-start(bf16[64,512]{1,0:T(8,128)(2,1)S(1)} %get-tuple-element.31), channel_id=1, source_target_pairs={{0,4},{2,6},{4,8},{6,10},{8,12},{10,14},{12,0},{14,2},{16,20},{18,... | collective-permute-start | bytes 196616 | tf_op jit(solution)/shard_map/ppermute | solution.py:195
  35.3 6.6 %collective-permute-start.7 = (bf16[64,512]{1,0:T(8,128)(2,1)S(1)}, bf16[64,512]{1,0:T(8,128)(2,1)S(1)}, u32[]{:S(2)}, u32[]{:S(2)}) collective-permute-start(bf16[64,512]{1,0:T(8,128)(2,1)S(1)} %get-tuple-element.32), channel_id=1, source_target_pairs={{0,8},{2,10},{4,12},{6,14},{8,0},{10,2},{12,4},{14,6},{16,24},{18,... | collective-permute-start | bytes 196616 | tf_op jit(solution)/shard_map/ppermute | solution.py:195
  35.6 6.2 %collective-permute-start.8 = (bf16[64,512]{1,0:T(8,128)(2,1)S(1)}, bf16[64,512]{1,0:T(8,128)(2,1)S(1)}, u32[]{:S(2)}, u32[]{:S(2)}) collective-permute-start(bf16[64,512]{1,0:T(8,128)(2,1)S(1)} %get-tuple-element.33), channel_id=1, source_target_pairs={{0,12},{2,14},{4,0},{6,2},{8,4},{10,6},{12,8},{14,10},{16,28},{18,... | collective-permute-start | bytes 196616 | tf_op jit(solution)/shard_map/ppermute | solution.py:195
  38.5 4.3 %collective-permute-start.9 = (bf16[64,512]{1,0:T(8,128)(2,1)S(1)}, bf16[64,512]{1,0:T(8,128)(2,1)S(1)}, u32[]{:S(2)}, u32[]{:S(2)}) collective-permute-start(bf16[64,512]{1,0:T(8,128)(2,1)S(1)} %get-tuple-element.34), channel_id=1, source_target_pairs={{0,16},{2,18},{4,20},{6,22},{8,24},{10,26},{12,28},{14,30},{16,0},... | collective-permute-start | bytes 196616 | tf_op jit(solution)/shard_map/ppermute | solution.py:195
  42.9 7.4 %collective-permute-start.14 = (bf16[64,1024]{1,0:T(8,128)(2,1)S(1)}, bf16[64,1024]{1,0:T(8,128)(2,1)S(1)}, u32[]{:S(2)}, u32[]{:S(2)}) collective-permute-start(bf16[64,1024]{1,0:T(8,128)(2,1)S(1)} %fusion.19), channel_id=1, source_target_pairs={{0,12},{2,14},{4,0},{6,2},{8,4},{10,6},{12,8},{14,10},{16,28},{18,... | collective-permute-start | bytes 393224 | tf_op jit(solution)/shard_map/ppermute | solution.py:195
  46.2 8.9 %collective-permute-start.15 = (bf16[64,1024]{1,0:T(8,128)(2,1)S(1)}, bf16[64,1024]{1,0:T(8,128)(2,1)S(1)}, u32[]{:S(2)}, u32[]{:S(2)}) collective-permute-start(bf16[64,1024]{1,0:T(8,128)(2,1)S(1)} %fusion.19), channel_id=1, source_target_pairs={{0,8},{2,10},{4,12},{6,14},{8,0},{10,2},{12,4},{14,6},{16,24},{18,... | collective-permute-start | bytes 393224 | tf_op jit(solution)/shard_map/ppermute | solution.py:195
  46.2 10.4 %collective-permute-start.16 = (bf16[64,1024]{1,0:T(8,128)(2,1)S(1)}, bf16[64,1024]{1,0:T(8,128)(2,1)S(1)}, u32[]{:S(2)}, u32[]{:S(2)}) collective-permute-start(bf16[64,1024]{1,0:T(8,128)(2,1)S(1)} %fusion.19), channel_id=1, source_target_pairs={{0,4},{2,6},{4,8},{6,10},{8,12},{10,14},{12,0},{14,2},{16,20},{18,... | collective-permute-start | bytes 393224 | tf_op jit(solution)/shard_map/ppermute | solution.py:195
  46.9 10.7 %collective-permute-start.17 = (bf16[64,1024]{1,0:T(8,128)(2,1)S(1)}, bf16[64,1024]{1,0:T(8,128)(2,1)S(1)}, u32[]{:S(2)}, u32[]{:S(2)}) collective-permute-start(bf16[64,1024]{1,0:T(8,128)(2,1)S(1)} %fusion.19), channel_id=1, source_target_pairs={{0,2},{2,0},{4,6},{6,4},{8,10},{10,8},{12,14},{14,12},{16,18},{18,... | collective-permute-start | bytes 393224 | tf_op jit(solution)/shard_map/ppermute | solution.py:195
  50.3 7.3 %collective-permute-start.18 = (bf16[64,1024]{1,0:T(8,128)(2,1)S(1)}, bf16[64,1024]{1,0:T(8,128)(2,1)S(1)}, u32[]{:S(2)}, u32[]{:S(2)}) collective-permute-start(bf16[64,1024]{1,0:T(8,128)(2,1)S(1)} %collective-permute-done.14), channel_id=1, source_target_pairs={{0,2},{2,0},{4,6},{6,4},{8,10},{10,8},{12,14},{14,12},{16,18},{18,... | collective-permute-start | bytes 393224 | tf_op jit(solution)/shard_map/ppermute | solution.py:195
  55.2 5.2 %collective-permute-start.19 = (bf16[64,1024]{1,0:T(8,128)(2,1)S(1)}, bf16[64,1024]{1,0:T(8,128)(2,1)S(1)}, u32[]{:S(2)}, u32[]{:S(2)}) collective-permute-start(bf16[64,1024]{1,0:T(8,128)(2,1)S(1)} %collective-permute-done.15), channel_id=1, source_target_pairs={{0,2},{2,0},{4,6},{6,4},{8,10},{10,8},{12,14},{14,12},{16,18},{18,... | collective-permute-start | bytes 393224 | tf_op jit(solution)/shard_map/ppermute | solution.py:195
  56.7 5.0 %collective-permute-start.20 = (bf16[64,1024]{1,0:T(8,128)(2,1)S(1)}, bf16[64,1024]{1,0:T(8,128)(2,1)S(1)}, u32[]{:S(2)}, u32[]{:S(2)}) collective-permute-start(bf16[64,1024]{1,0:T(8,128)(2,1)S(1)} %collective-permute-done.16), channel_id=1, source_target_pairs={{0,2},{2,0},{4,6},{6,4},{8,10},{10,8},{12,14},{14,12},{16,18},{18,... | collective-permute-start | bytes 393224 | tf_op jit(solution)/shard_map/ppermute | solution.py:195
  62.3 1.4 %collective-permute-start.21 = (bf16[8,16,512]{2,1,0:T(8,128)(2,1)S(1)}, bf16[8,16,512]{2,1,0:T(8,128)(2,1)S(1)}, u32[]{:S(2)}, u32[]{:S(2)}) collective-permute-start(bf16[8,16,512]{2,1,0:T(8,128)(2,1)S(1)} %dynamic-slice_bitcast_fusion), channel_id=1, source_target_pairs={{0,1},{1,0},{2,3},{3,2},{4,5},{5,4},{6,7},{7,6},{8,9},{9,8},{10,11... | collective-permute-start | bytes 393224 | tf_op jit(solution)/shard_map/ppermute | solution.py:288
  (3 other events, 33.3 us)

commit v5 on v4

--- a/solution.py
+++ b/solution.py
@@ -12,6 +12,7 @@
 BF16 = jnp.bfloat16
 F32 = jnp.float32
 VMEM_BYTES = 16 * 1024 * 1024
+CUT_BYTES = 52 * 1024 * 1024
 
 
 def halves(values):
@@ -37,10 +38,9 @@
     return sx, y, lax.div(lax.axis_index("hist"), py)
 
 
-def pick_kernel(px, py, width, history, taps, gates, *refs):
+def pick_kernel(px, py, width, history, taps, *refs):
     sx, y, _ = places(px, py)
     outs, sems = refs[:-1], refs[-1]
-    rows, owned = history.shape[0], gates.shape[0]
     wide = px * width
     copies = []
     outs = list(outs)
@@ -60,10 +60,6 @@
         for dy in range(py):
             if dx or dy:
                 copy(history.at[:, columns(dx, dy)], outs.pop(0))
-    for dy in range(1, py):
-        target = outs.pop(0)
-        start = pl.multiple_of((y ^ dy) * wide, wide)
-        copy(gates.at[:, pl.ds(start, wide)], target)
     for one in copies:
         one.wait()
 
@@ -74,10 +70,13 @@
     return jnp.dot(table[:period, : 2 * rows], twice, preferred_element_type=F32)
 
 
-def early_kernel(px, py, tile, table, history, taps, *refs):
+def early_kernel(px, py, tile, table, history, taps, gates, *refs):
     peers, outs = refs[: py - 1], refs[py - 1 :]
     sx, y, _ = places(px, py)
     width = outs[0].shape[1]
+    for dy in range(1, py):
+        start = pl.multiple_of((y ^ dy) * px * width, px * width)
+        outs[py + dy][...] = gates[:, pl.ds(start, px * width)]
 
     def step(number, _):
         cols = pl.ds(pl.multiple_of(number * tile, tile), tile)
@@ -110,13 +109,12 @@
     following = [refs.pop(0) for _ in range(py)]
     inputs = [[None if dx == dy == 0 else refs.pop(0) for dy in range(py)] for dx in range(px)]
     outs = [[refs.pop(0) for _ in range(nz)] for _ in range(px)]
-    (conv,) = refs
     _, y, z = places(px, py)
     width = own_input.shape[1]
     period = table.shape[1]
     modes = period // 2
     group = outs[0][0].shape[0]
-    tokens = conv.shape[1]
+    tokens = group * nz
     rows = following[0].shape[0]
     assert 2 * rows == period
     odd = lax.broadcasted_iota(jnp.int32, (modes, tile), 0) % 2
@@ -154,18 +152,19 @@
             product = jnp.concatenate([real, imag], 0)
             high = product.astype(BF16)
             low = (product - high.astype(F32)).astype(BF16)
-            i_high, i_low = table[period : period + tokens, :], table[period + tokens :, :]
-            wide_table = jnp.concatenate([i_high, i_high, i_low], 1)
+            rows_of = []
+            for dz in range(nz):
+                begin = pl.multiple_of(period + lax.rem(z + dz, nz) * group, group)
+                i_high, i_low = table[pl.ds(begin, group), :], table[pl.ds(begin + tokens, group), :]
+                rows_of.append(jnp.concatenate([i_high, i_high, i_low], 1))
             stacked = jnp.concatenate([high, low, high], 0)
-            conv[dx, :, cols] = jnp.dot(wide_table, stacked, preferred_element_type=F32)
+            total = jnp.dot(jnp.concatenate(rows_of, 0), stacked, preferred_element_type=F32)
+            for dz in range(nz):
+                out = outs[dx][dz]
+                out[:, cols] = total[dz * group : (dz + 1) * group].astype(out.dtype)
         return 0
 
     lax.fori_loop(0, width // tile, step, 0)
-    for dx in range(px):
-        for dz in range(nz):
-            begin = pl.multiple_of(lax.rem(z + dz, nz) * group, group)
-            out = outs[dx][dz]
-            out[...] = conv[dx, pl.ds(begin, group), :].astype(out.dtype)
 
 
 def local(history, filter_taps, gate_values, out_weight):
@@ -203,15 +202,16 @@
     hbm = pl.BlockSpec(memory_space=pltpu.HBM)
     vmem = pl.BlockSpec(memory_space=pltpu.VMEM)
     piece = jax.ShapeDtypeStruct((rows, width), BF16)
-    shapes = [piece] * (py + px * py - 1) + [jax.ShapeDtypeStruct((owned, wide), BF16)] * (py - 1)
+    shapes = [piece] * (py + px * py - 1)
     picked = list(
         pl.pallas_call(
             functools.partial(pick_kernel, px, py, width),
             out_shape=shapes,
-            in_specs=[hbm] * 3,
+            in_specs=[hbm] * 2,
             out_specs=[vmem] * len(shapes),
             scratch_shapes=[pltpu.SemaphoreType.DMA((len(shapes),))],
-        )(history, filter_taps, gate_values)
+            compiler_params=pltpu.CompilerParams(vmem_limit_bytes=CUT_BYTES),
+        )(history, filter_taps)
     )
     peers = [move(picked.pop(0), dy=dy) for dy in range(1, py)]
     following = [picked.pop(0)] + peers
@@ -221,22 +221,24 @@
         for dy in range(py):
             if dx or dy:
                 inputs.append(move(picked.pop(0), dx=dx, dy=dy))
-    gates = [lax.dynamic_slice_in_dim(gate_values, y * wide, wide, 1)]
-    gates = ordered(y, gates + [move(picked.pop(0), dy=dy) for dy in range(1, py)])
-    gate = jnp.concatenate(gates, 0).astype(F32)
-
     table = table_of(rows, tokens)
     tile = 256 if width % 256 == 0 else width
     params = pltpu.CompilerParams(vmem_limit_bytes=VMEM_BYTES)
     flops = 4 * rows * 2 * rows * width
     early = pl.pallas_call(
         functools.partial(early_kernel, px, py, tile),
-        out_shape=[jax.ShapeDtypeStruct((rows + tokens, width), F32)] * (py + 1),
-        in_specs=[vmem] * (2 + py),
-        out_specs=[vmem] * (py + 1),
+        out_shape=[jax.ShapeDtypeStruct((rows + tokens, width), F32)] * (py + 1)
+        + [jax.ShapeDtypeStruct((owned, wide), BF16)] * (py - 1),
+        in_specs=[vmem] * (3 + py),
+        out_specs=[vmem] * (2 * py),
         compiler_params=params,
         cost_estimate=pl.CostEstimate(flops=3 * flops, bytes_accessed=rows * width * 8, transcendentals=0),
-    )(table, history, filter_taps, *peers)
+    )(table, history, filter_taps, gate_values, *peers)
+    gates = [lax.dynamic_slice_in_dim(gate_values, y * wide, wide, 1)]
+    gates = ordered(y, gates + [move(v, dy=dy) for dy, v in enumerate(early[py + 1 :], 1)])
+    gate = jnp.concatenate(gates, 0).astype(F32)
+
+    early = early[: py + 1]
     for dx in range(1, px):
         whole = jax.ShapeDtypeStruct((rows + tokens, width), F32)
         n = dx * py - 1
@@ -254,7 +256,6 @@
         out_shape=[part(dx == dz == 0) for dx in range(px) for dz in range(nz)],
         in_specs=[vmem] * (1 + 1 + py + py + px * py - 1),
         out_specs=[vmem] * (px * nz),
-        scratch_shapes=[pltpu.VMEM((px, tokens, width), F32)],
         compiler_params=params,
         cost_estimate=pl.CostEstimate(flops=7 * flops, bytes_accessed=rows * width * 8, transcendentals=0),
     )(table, *early, *following, *inputs)

time: 75.1 us -> 73.8 us (0.983)
  waiting for transfers between devices: 21.5 us -> 19.7 us
  Pallas kernels: 7.19 us -> 6.03 us
  local copies, waits for them, and re-layouts: 1.92 us -> 2.82 us
    ppermute x21, waiting for transfers between devices: 20.1 us -> 18.3 us  [move(): return lax.ppermute(value, ('seq', 'hist'), pairs)]
    pallas_call x1, Pallas kernels: 2.56 us -> 1.47 us  [local(): pl.pallas_call(functools.partial(pick_kernel, px, py, width), out_shape=s...]
    unnamed x10 -> x12, local copies, waits for them, and re-layouts: 1.24 us -> 2.14 us
  transfers between devices with their start and end apart: 22 -> 22, of which waited for: 12 -> 11; matrix products, arithmetic and copies ran while one was open for 1% -> 1% of each run, Pallas kernels for 6% -> 6%
where the time goes in v5:
time: 73.8 us; the launch traced here: 73.5 us
  starting transfers between devices  33.2 us (45%)
  waiting for transfers between devices  19.7 us (27%)
  blocking collectives  10.5 us (14%)
  Pallas kernels  6.03 us (8%)
  local copies, waits for them, and re-layouts  2.82 us (4%)
  matrix products  0.87 us (1%)
    ppermute x21, starting transfers between devices, move(): return lax.ppermute(value, ('seq', 'hist'), pairs)  33.2 us
    ppermute x21, waiting for transfers between devices, move(): return lax.ppermute(value, ('seq', 'hist'), pairs)  18.3 us
    all_to_all x1, blocking collectives, local(): lax.all_to_all(total, 'hist', split_axis=0, concat_axis=0, tiled=True)  10.5 us
    pallas_call x1, Pallas kernels, local(): pl.pallas_call(functools.partial(conv_kernel, px, py, nz, tile), out_shap...  2.81 us
    unnamed x12, local copies, waits for them, and re-layouts  2.14 us
  transfers between devices with their start and end apart: 22, of which 11 were waited for; matrix products, arithmetic and copies ran while one was open for 1% of the time, Pallas kernels for 6%

profile of v5, /device:TPU:0, one launch (start us, length us, event | category | flops | bytes accessed | tf_op | source)
XLA Modules:
  0.0 73.5 jit_solution(2457983606331059430)
XLA Ops:
  0.0 1.5 %shard_map.55 = (bf16[256,512]{1,0:T(8,128)(2,1)S(1)}, bf16[256,512]{1,0:T(8,128)(2,1)S(1)}, bf16[256,512]{1,0:T(8,128)(2,1)S(1)}, bf16[256,512]{1,0:T(8,128)(2,1)S(1)}, bf16[256,512]{1,0:T(8,128)(2,1)S(1)}) custom-call(bf16[256,2048]{1,0:T(8,128)(2,1)} %history.3, bf16[256,2048]{1,0:T(8,128)(2,1)} %taps.3), custom_call_target="tpu_custom_call" | custom-call | tf_op jit(solution)/shard_map/pallas_call | solution.py:207
  1.5 3.1 %collective-permute-start = (bf16[256,512]{1,0:T(8,128)(2,1)S(1)}, bf16[256,512]{1,0:T(8,128)(2,1)S(1)}, u32[]{:S(2)}, u32[]{:S(2)}) collective-permute-start(bf16[256,512]{1,0:T(8,128)(2,1)S(1)} %get-tuple-element.22), channel_id=1, source_target_pairs={{0,2},{2,0},{4,6},{6,4},{8,10},{10,8},{12,14},{14,12},{16,18},{18,... | collective-permute-start | bytes 786440 | tf_op jit(solution)/shard_map/ppermute | solution.py:194
  4.5 1.5 %collective-permute-start.4 = (bf16[256,512]{1,0:T(8,128)(2,1)S(1)}, bf16[256,512]{1,0:T(8,128)(2,1)S(1)}, u32[]{:S(2)}, u32[]{:S(2)}) collective-permute-start(bf16[256,512]{1,0:T(8,128)(2,1)S(1)} %get-tuple-element.28), channel_id=1, source_target_pairs={{0,16},{2,18},{4,20},{6,22},{8,24},{10,26},{12,28},{14,30},{16,0},... | collective-permute-start | bytes 786440 | tf_op jit(solution)/shard_map/ppermute | solution.py:194
  6.0 1.3 %collective-permute-start.1 = (bf16[256,512]{1,0:T(8,128)(2,1)S(1)}, bf16[256,512]{1,0:T(8,128)(2,1)S(1)}, u32[]{:S(2)}, u32[]{:S(2)}) collective-permute-start(bf16[256,512]{1,0:T(8,128)(2,1)S(1)} %get-tuple-element.26), channel_id=1, source_target_pairs={{4,0},{8,4},{12,8},{20,16},{24,20},{28,24},{5,1},{9,5},{13,9},{21,... | collective-permute-start | bytes 786440 | tf_op jit(solution)/shard_map/ppermute | solution.py:194
  7.4 2.0 %collective-permute-start.5 = (bf16[256,512]{1,0:T(8,128)(2,1)S(1)}, bf16[256,512]{1,0:T(8,128)(2,1)S(1)}, u32[]{:S(2)}, u32[]{:S(2)}) collective-permute-start(bf16[256,512]{1,0:T(8,128)(2,1)S(1)} %get-tuple-element.29), channel_id=1, source_target_pairs={{0,18},{2,16},{4,22},{6,20},{8,26},{10,24},{12,30},{14,28},{16,2},... | collective-permute-start | bytes 786440 | tf_op jit(solution)/shard_map/ppermute | solution.py:194
  9.4 3.0 %collective-permute-done.refs_0_ = bf16[256,512]{1,0:T(8,128)(2,1)S(1)} collective-permute-done((bf16[256,512]{1,0:T(8,128)(2,1)S(1)}, bf16[256,512]{1,0:T(8,128)(2,1)S(1)}, u32[]{:S(2)}, u32[]{:S(2)}) %collective-permute-start) | collective-permute-done | bytes 262176 | tf_op jit(solution)/shard_map/ppermute | solution.py:194
  16.4 3.4 %collective-permute-start.13 = (bf16[32,1024]{1,0:T(8,128)(2,1)S(1)}, bf16[32,1024]{1,0:T(8,128)(2,1)S(1)}, u32[]{:S(2)}, u32[]{:S(2)}) collective-permute-start(bf16[32,1024]{1,0:T(8,128)(2,1)S(1)} %get-tuple-element.38), channel_id=1, source_target_pairs={{0,2},{2,0},{4,6},{6,4},{8,10},{10,8},{12,14},{14,12},{16,18},{18,... | collective-permute-start | bytes 196616 | tf_op jit(solution)/shard_map/ppermute | solution.py:194
  20.4 2.3 %collective-permute-done.3.refs_5_ = bf16[256,512]{1,0:T(8,128)(2,1)S(1)} collective-permute-done((bf16[256,512]{1,0:T(8,128)(2,1)S(1)}, bf16[256,512]{1,0:T(8,128)(2,1)S(1)}, u32[]{:S(2)}, u32[]{:S(2)}) %collective-permute-start.3) | collective-permute-done | bytes 262176 | tf_op jit(solution)/shard_map/ppermute | solution.py:194
  22.8 2.8 %shard_map.58 = (f32[64,512]{1,0:T(8,128)S(1)}, bf16[64,512]{1,0:T(8,128)(2,1)S(1)}, bf16[64,512]{1,0:T(8,128)(2,1)S(1)}, bf16[64,512]{1,0:T(8,128)(2,1)S(1)}, b...) custom-call(bf16[1024,512]{1,0:T(8,128)(2,1)S(1)} %copy-done.3, ...), custom_call_target="tpu_custom_call" | custom-call | flops 1879048192 | bytes 1048576 | tf_op jit(solution)/shard_map/pallas_call | solution.py:254
  25.6 2.8 %collective-permute-start.10 = (bf16[64,512]{1,0:T(8,128)(2,1)S(1)}, bf16[64,512]{1,0:T(8,128)(2,1)S(1)}, u32[]{:S(2)}, u32[]{:S(2)}) collective-permute-start(bf16[64,512]{1,0:T(8,128)(2,1)S(1)} %get-tuple-element.35), channel_id=1, source_target_pairs={{0,20},{2,22},{4,24},{6,26},{8,28},{10,30},{12,16},{14,18},{16,4},... | collective-permute-start | bytes 196616 | tf_op jit(solution)/shard_map/ppermute | solution.py:194
  28.4 2.6 %collective-permute-start.11 = (bf16[64,512]{1,0:T(8,128)(2,1)S(1)}, bf16[64,512]{1,0:T(8,128)(2,1)S(1)}, u32[]{:S(2)}, u32[]{:S(2)}) collective-permute-start(bf16[64,512]{1,0:T(8,128)(2,1)S(1)} %get-tuple-element.36), channel_id=1, source_target_pairs={{0,24},{2,26},{4,28},{6,30},{8,16},{10,18},{12,20},{14,22},{16,8},... | collective-permute-start | bytes 196616 | tf_op jit(solution)/shard_map/ppermute | solution.py:194
  31.0 2.3 %collective-permute-start.12 = (bf16[64,512]{1,0:T(8,128)(2,1)S(1)}, bf16[64,512]{1,0:T(8,128)(2,1)S(1)}, u32[]{:S(2)}, u32[]{:S(2)}) collective-permute-start(bf16[64,512]{1,0:T(8,128)(2,1)S(1)} %get-tuple-element.37), channel_id=1, source_target_pairs={{0,28},{2,30},{4,16},{6,18},{8,20},{10,22},{12,24},{14,26},{16,12}... | collective-permute-start | bytes 196616 | tf_op jit(solution)/shard_map/ppermute | solution.py:194
  34.2 2.9 %collective-permute-start.8 = (bf16[64,512]{1,0:T(8,128)(2,1)S(1)}, bf16[64,512]{1,0:T(8,128)(2,1)S(1)}, u32[]{:S(2)}, u32[]{:S(2)}) collective-permute-start(bf16[64,512]{1,0:T(8,128)(2,1)S(1)} %get-tuple-element.33), channel_id=1, source_target_pairs={{0,12},{2,14},{4,0},{6,2},{8,4},{10,6},{12,8},{14,10},{16,28},{18,... | collective-permute-start | bytes 196616 | tf_op jit(solution)/shard_map/ppermute | solution.py:194
  37.8 1.6 %collective-permute-done.6 = bf16[64,512]{1,0:T(8,128)(2,1)S(1)} collective-permute-done((bf16[64,512]{1,0:T(8,128)(2,1)S(1)}, bf16[64,512]{1,0:T(8,128)(2,1)S(1)}, u32[]{:S(2)}, u32[]{:S(2)}) %collective-permute-start.6) | collective-permute-done | bytes 65568 | tf_op jit(solution)/shard_map/ppermute | solution.py:194
  41.5 3.4 %collective-permute-start.14 = (bf16[64,1024]{1,0:T(8,128)(2,1)S(1)}, bf16[64,1024]{1,0:T(8,128)(2,1)S(1)}, u32[]{:S(2)}, u32[]{:S(2)}) collective-permute-start(bf16[64,1024]{1,0:T(8,128)(2,1)S(1)} %fusion.19), channel_id=1, source_target_pairs={{0,12},{2,14},{4,0},{6,2},{8,4},{10,6},{12,8},{14,10},{16,28},{18,... | collective-permute-start | bytes 393224 | tf_op jit(solution)/shard_map/ppermute | solution.py:194
  45.5 1.5 %collective-permute-start.17 = (bf16[64,1024]{1,0:T(8,128)(2,1)S(1)}, bf16[64,1024]{1,0:T(8,128)(2,1)S(1)}, u32[]{:S(2)}, u32[]{:S(2)}) collective-permute-start(bf16[64,1024]{1,0:T(8,128)(2,1)S(1)} %fusion.19), channel_id=1, source_target_pairs={{0,2},{2,0},{4,6},{6,4},{8,10},{10,8},{12,14},{14,12},{16,18},{18,... | collective-permute-start | bytes 393224 | tf_op jit(solution)/shard_map/ppermute | solution.py:194
  47.1 1.8 %collective-permute-done.14 = bf16[64,1024]{1,0:T(8,128)(2,1)S(1)} collective-permute-done((bf16[64,1024]{1,0:T(8,128)(2,1)S(1)}, bf16[64,1024]{1,0:T(8,128)(2,1)S(1)}, u32[]{:S(2)}, u32[]{:S(2)}) %collective-permute-start.14) | collective-permute-done | bytes 131104 | tf_op jit(solution)/shard_map/ppermute | solution.py:194
  48.9 1.5 %collective-permute-start.18 = (bf16[64,1024]{1,0:T(8,128)(2,1)S(1)}, bf16[64,1024]{1,0:T(8,128)(2,1)S(1)}, u32[]{:S(2)}, u32[]{:S(2)}) collective-permute-start(bf16[64,1024]{1,0:T(8,128)(2,1)S(1)} %collective-permute-done.14), channel_id=1, source_target_pairs={{0,2},{2,0},{4,6},{6,4},{8,10},{10,8},{12,14},{14,12},{16,18},{18,... | collective-permute-start | bytes 393224 | tf_op jit(solution)/shard_map/ppermute | solution.py:194
  50.4 3.4 %collective-permute-done.15 = bf16[64,1024]{1,0:T(8,128)(2,1)S(1)} collective-permute-done((bf16[64,1024]{1,0:T(8,128)(2,1)S(1)}, bf16[64,1024]{1,0:T(8,128)(2,1)S(1)}, u32[]{:S(2)}, u32[]{:S(2)}) %collective-permute-start.15) | collective-permute-done | bytes 131104 | tf_op jit(solution)/shard_map/ppermute | solution.py:194
  53.8 1.5 %collective-permute-start.19 = (bf16[64,1024]{1,0:T(8,128)(2,1)S(1)}, bf16[64,1024]{1,0:T(8,128)(2,1)S(1)}, u32[]{:S(2)}, u32[]{:S(2)}) collective-permute-start(bf16[64,1024]{1,0:T(8,128)(2,1)S(1)} %collective-permute-done.15), channel_id=1, source_target_pairs={{0,2},{2,0},{4,6},{6,4},{8,10},{10,8},{12,14},{14,12},{16,18},{18,... | collective-permute-start | bytes 393224 | tf_op jit(solution)/shard_map/ppermute | solution.py:194
  56.3 2.7 %collective-permute-done.19 = bf16[64,1024]{1,0:T(8,128)(2,1)S(1)} collective-permute-done((bf16[64,1024]{1,0:T(8,128)(2,1)S(1)}, bf16[64,1024]{1,0:T(8,128)(2,1)S(1)}, u32[]{:S(2)}, u32[]{:S(2)}) %collective-permute-start.19) | collective-permute-done | bytes 131104 | tf_op jit(solution)/shard_map/ppermute | solution.py:194
  59.0 1.4 %collective-permute-done.20 = bf16[64,1024]{1,0:T(8,128)(2,1)S(1)} collective-permute-done((bf16[64,1024]{1,0:T(8,128)(2,1)S(1)}, bf16[64,1024]{1,0:T(8,128)(2,1)S(1)}, u32[]{:S(2)}, u32[]{:S(2)}) %collective-permute-start.20) | collective-permute-done | bytes 131104 | tf_op jit(solution)/shard_map/ppermute | solution.py:194
  61.0 1.3 %collective-permute-done.21 = bf16[8,16,512]{2,1,0:T(8,128)(2,1)S(1)} collective-permute-done((bf16[8,16,512]{2,1,0:T(8,128)(2,1)S(1)}, bf16[8,16,512]{2,1,0:T(8,128)(2,1)S(1)}, u32[]{:S(2)}, u32[]{:S(2)}) %collective-permute-start.21) | collective-permute-done | bytes 131104 | tf_op jit(solution)/shard_map/ppermute | solution.py:289
  62.4 10.5 %all_to_all.6 = bf16[8,16,512]{2,1,0:T(8,128)(2,1)S(1)} all-to-all(bf16[8,16,512]{2,1,0:T(8,128)(2,1)S(1)} %fusion.20), channel_id=1, replica_groups=mesh['seq'=2,'hist'=8,'chan'=2] {'hist'}, dimensions={0} | all-to-all | bytes 262144 | tf_op jit(solution)/shard_map/all_to_all | solution.py:294
  (46 shorter events, 11.4 us)
Async XLA Ops:
  0.0 55.8 %copy-start = (bf16[2048,512]{1,0:T(8,128)(2,1)S(1)}, bf16[2048,512]{1,0:T(8,128)(2,1)}, u32[]{:S(2)}) copy-start(bf16[2048,512]{1,0:T(8,128)(2,1)} %param.8) | copy-start | bytes 6291460
  1.5 10.9 %collective-permute-start = (bf16[256,512]{1,0:T(8,128)(2,1)S(1)}, bf16[256,512]{1,0:T(8,128)(2,1)S(1)}, u32[]{:S(2)}, u32[]{:S(2)}) collective-permute-start(bf16[256,512]{1,0:T(8,128)(2,1)S(1)} %get-tuple-element.22), channel_id=1, source_target_pairs={{0,2},{2,0},{4,6},{6,4},{8,10},{10,8},{12,14},{14,12},{16,18},{18,... | collective-permute-start | bytes 786440 | tf_op jit(solution)/shard_map/ppermute | solution.py:194
  4.5 11.8 %collective-permute-start.4 = (bf16[256,512]{1,0:T(8,128)(2,1)S(1)}, bf16[256,512]{1,0:T(8,128)(2,1)S(1)}, u32[]{:S(2)}, u32[]{:S(2)}) collective-permute-start(bf16[256,512]{1,0:T(8,128)(2,1)S(1)} %get-tuple-element.28), channel_id=1, source_target_pairs={{0,16},{2,18},{4,20},{6,22},{8,24},{10,26},{12,28},{14,30},{16,0},... | collective-permute-start | bytes 786440 | tf_op jit(solution)/shard_map/ppermute | solution.py:194
  6.0 14.4 %collective-permute-start.1 = (bf16[256,512]{1,0:T(8,128)(2,1)S(1)}, bf16[256,512]{1,0:T(8,128)(2,1)S(1)}, u32[]{:S(2)}, u32[]{:S(2)}) collective-permute-start(bf16[256,512]{1,0:T(8,128)(2,1)S(1)} %get-tuple-element.26), channel_id=1, source_target_pairs={{4,0},{8,4},{12,8},{20,16},{24,20},{28,24},{5,1},{9,5},{13,9},{21,... | collective-permute-start | bytes 786440 | tf_op jit(solution)/shard_map/ppermute | solution.py:194
  7.3 15.5 %collective-permute-start.3 = (bf16[256,512]{1,0:T(8,128)(2,1)S(1)}, bf16[256,512]{1,0:T(8,128)(2,1)S(1)}, u32[]{:S(2)}, u32[]{:S(2)}) collective-permute-start(bf16[256,512]{1,0:T(8,128)(2,1)S(1)} %get-tuple-element.27), channel_id=1, source_target_pairs={{0,2},{2,0},{4,6},{6,4},{8,10},{10,8},{12,14},{14,12},{16,18},{18,... | collective-permute-start | bytes 786440 | tf_op jit(solution)/shard_map/ppermute | solution.py:194
  7.4 15.4 %collective-permute-start.5 = (bf16[256,512]{1,0:T(8,128)(2,1)S(1)}, bf16[256,512]{1,0:T(8,128)(2,1)S(1)}, u32[]{:S(2)}, u32[]{:S(2)}) collective-permute-start(bf16[256,512]{1,0:T(8,128)(2,1)S(1)} %get-tuple-element.29), channel_id=1, source_target_pairs={{0,18},{2,16},{4,22},{6,20},{8,26},{10,24},{12,30},{14,28},{16,2},... | collective-permute-start | bytes 786440 | tf_op jit(solution)/shard_map/ppermute | solution.py:194
  12.4 10.4 %collective-permute-start.2 = (bf16[256,512]{1,0:T(8,128)(2,1)S(1)}, bf16[256,512]{1,0:T(8,128)(2,1)S(1)}, u32[]{:S(2)}, u32[]{:S(2)}) collective-permute-start(bf16[256,512]{1,0:T(8,128)(2,1)S(1)} %collective-permute-done.refs_0_), channel_id=1, source_target_pairs={{6,2},{10,6},{14,10},{22,18},{26,22},{30,26},{7,3},{11,7},{15,11},... | collective-permute-start | bytes 786440 | tf_op jit(solution)/shard_map/ppermute | solution.py:194
  16.4 17.5 %collective-permute-start.13 = (bf16[32,1024]{1,0:T(8,128)(2,1)S(1)}, bf16[32,1024]{1,0:T(8,128)(2,1)S(1)}, u32[]{:S(2)}, u32[]{:S(2)}) collective-permute-start(bf16[32,1024]{1,0:T(8,128)(2,1)S(1)} %get-tuple-element.38), channel_id=1, source_target_pairs={{0,2},{2,0},{4,6},{6,4},{8,10},{10,8},{12,14},{14,12},{16,18},{18,... | collective-permute-start | bytes 196616 | tf_op jit(solution)/shard_map/ppermute | solution.py:194
  22.8 14.9 %copy-start.5 = (bf16[32,2048]{1,0:T(8,128)(2,1)S(1)}, bf16[32,2048]{1,0:T(8,128)(2,1)}, u32[]{:S(2)}) copy-start(bf16[32,2048]{1,0:T(8,128)(2,1)} %gates.1) | copy-start | bytes 393220
  25.6 8.6 %collective-permute-start.10 = (bf16[64,512]{1,0:T(8,128)(2,1)S(1)}, bf16[64,512]{1,0:T(8,128)(2,1)S(1)}, u32[]{:S(2)}, u32[]{:S(2)}) collective-permute-start(bf16[64,512]{1,0:T(8,128)(2,1)S(1)} %get-tuple-element.35), channel_id=1, source_target_pairs={{0,20},{2,22},{4,24},{6,26},{8,28},{10,30},{12,16},{14,18},{16,4},... | collective-permute-start | bytes 196616 | tf_op jit(solution)/shard_map/ppermute | solution.py:194
  28.4 8.7 %collective-permute-start.11 = (bf16[64,512]{1,0:T(8,128)(2,1)S(1)}, bf16[64,512]{1,0:T(8,128)(2,1)S(1)}, u32[]{:S(2)}, u32[]{:S(2)}) collective-permute-start(bf16[64,512]{1,0:T(8,128)(2,1)S(1)} %get-tuple-element.36), channel_id=1, source_target_pairs={{0,24},{2,26},{4,28},{6,30},{8,16},{10,18},{12,20},{14,22},{16,8},... | collective-permute-start | bytes 196616 | tf_op jit(solution)/shard_map/ppermute | solution.py:194
  31.0 6.8 %collective-permute-start.12 = (bf16[64,512]{1,0:T(8,128)(2,1)S(1)}, bf16[64,512]{1,0:T(8,128)(2,1)S(1)}, u32[]{:S(2)}, u32[]{:S(2)}) collective-permute-start(bf16[64,512]{1,0:T(8,128)(2,1)S(1)} %get-tuple-element.37), channel_id=1, source_target_pairs={{0,28},{2,30},{4,16},{6,18},{8,20},{10,22},{12,24},{14,26},{16,12}... | collective-permute-start | bytes 196616 | tf_op jit(solution)/shard_map/ppermute | solution.py:194
  33.2 6.2 %collective-permute-start.6 = (bf16[64,512]{1,0:T(8,128)(2,1)S(1)}, bf16[64,512]{1,0:T(8,128)(2,1)S(1)}, u32[]{:S(2)}, u32[]{:S(2)}) collective-permute-start(bf16[64,512]{1,0:T(8,128)(2,1)S(1)} %get-tuple-element.31), channel_id=1, source_target_pairs={{0,4},{2,6},{4,8},{6,10},{8,12},{10,14},{12,0},{14,2},{16,20},{18,... | collective-permute-start | bytes 196616 | tf_op jit(solution)/shard_map/ppermute | solution.py:194
  33.9 6.6 %collective-permute-start.7 = (bf16[64,512]{1,0:T(8,128)(2,1)S(1)}, bf16[64,512]{1,0:T(8,128)(2,1)S(1)}, u32[]{:S(2)}, u32[]{:S(2)}) collective-permute-start(bf16[64,512]{1,0:T(8,128)(2,1)S(1)} %get-tuple-element.32), channel_id=1, source_target_pairs={{0,8},{2,10},{4,12},{6,14},{8,0},{10,2},{12,4},{14,6},{16,24},{18,... | collective-permute-start | bytes 196616 | tf_op jit(solution)/shard_map/ppermute | solution.py:194
  34.2 6.2 %collective-permute-start.8 = (bf16[64,512]{1,0:T(8,128)(2,1)S(1)}, bf16[64,512]{1,0:T(8,128)(2,1)S(1)}, u32[]{:S(2)}, u32[]{:S(2)}) collective-permute-start(bf16[64,512]{1,0:T(8,128)(2,1)S(1)} %get-tuple-element.33), channel_id=1, source_target_pairs={{0,12},{2,14},{4,0},{6,2},{8,4},{10,6},{12,8},{14,10},{16,28},{18,... | collective-permute-start | bytes 196616 | tf_op jit(solution)/shard_map/ppermute | solution.py:194
  37.1 4.3 %collective-permute-start.9 = (bf16[64,512]{1,0:T(8,128)(2,1)S(1)}, bf16[64,512]{1,0:T(8,128)(2,1)S(1)}, u32[]{:S(2)}, u32[]{:S(2)}) collective-permute-start(bf16[64,512]{1,0:T(8,128)(2,1)S(1)} %get-tuple-element.34), channel_id=1, source_target_pairs={{0,16},{2,18},{4,20},{6,22},{8,24},{10,26},{12,28},{14,30},{16,0},... | collective-permute-start | bytes 196616 | tf_op jit(solution)/shard_map/ppermute | solution.py:194
  41.5 7.4 %collective-permute-start.14 = (bf16[64,1024]{1,0:T(8,128)(2,1)S(1)}, bf16[64,1024]{1,0:T(8,128)(2,1)S(1)}, u32[]{:S(2)}, u32[]{:S(2)}) collective-permute-start(bf16[64,1024]{1,0:T(8,128)(2,1)S(1)} %fusion.19), channel_id=1, source_target_pairs={{0,12},{2,14},{4,0},{6,2},{8,4},{10,6},{12,8},{14,10},{16,28},{18,... | collective-permute-start | bytes 393224 | tf_op jit(solution)/shard_map/ppermute | solution.py:194
  44.9 8.9 %collective-permute-start.15 = (bf16[64,1024]{1,0:T(8,128)(2,1)S(1)}, bf16[64,1024]{1,0:T(8,128)(2,1)S(1)}, u32[]{:S(2)}, u32[]{:S(2)}) collective-permute-start(bf16[64,1024]{1,0:T(8,128)(2,1)S(1)} %fusion.19), channel_id=1, source_target_pairs={{0,8},{2,10},{4,12},{6,14},{8,0},{10,2},{12,4},{14,6},{16,24},{18,... | collective-permute-start | bytes 393224 | tf_op jit(solution)/shard_map/ppermute | solution.py:194
  44.9 10.4 %collective-permute-start.16 = (bf16[64,1024]{1,0:T(8,128)(2,1)S(1)}, bf16[64,1024]{1,0:T(8,128)(2,1)S(1)}, u32[]{:S(2)}, u32[]{:S(2)}) collective-permute-start(bf16[64,1024]{1,0:T(8,128)(2,1)S(1)} %fusion.19), channel_id=1, source_target_pairs={{0,4},{2,6},{4,8},{6,10},{8,12},{10,14},{12,0},{14,2},{16,20},{18,... | collective-permute-start | bytes 393224 | tf_op jit(solution)/shard_map/ppermute | solution.py:194
  45.5 10.7 %collective-permute-start.17 = (bf16[64,1024]{1,0:T(8,128)(2,1)S(1)}, bf16[64,1024]{1,0:T(8,128)(2,1)S(1)}, u32[]{:S(2)}, u32[]{:S(2)}) collective-permute-start(bf16[64,1024]{1,0:T(8,128)(2,1)S(1)} %fusion.19), channel_id=1, source_target_pairs={{0,2},{2,0},{4,6},{6,4},{8,10},{10,8},{12,14},{14,12},{16,18},{18,... | collective-permute-start | bytes 393224 | tf_op jit(solution)/shard_map/ppermute | solution.py:194
  48.9 7.4 %collective-permute-start.18 = (bf16[64,1024]{1,0:T(8,128)(2,1)S(1)}, bf16[64,1024]{1,0:T(8,128)(2,1)S(1)}, u32[]{:S(2)}, u32[]{:S(2)}) collective-permute-start(bf16[64,1024]{1,0:T(8,128)(2,1)S(1)} %collective-permute-done.14), channel_id=1, source_target_pairs={{0,2},{2,0},{4,6},{6,4},{8,10},{10,8},{12,14},{14,12},{16,18},{18,... | collective-permute-start | bytes 393224 | tf_op jit(solution)/shard_map/ppermute | solution.py:194
  53.8 5.2 %collective-permute-start.19 = (bf16[64,1024]{1,0:T(8,128)(2,1)S(1)}, bf16[64,1024]{1,0:T(8,128)(2,1)S(1)}, u32[]{:S(2)}, u32[]{:S(2)}) collective-permute-start(bf16[64,1024]{1,0:T(8,128)(2,1)S(1)} %collective-permute-done.15), channel_id=1, source_target_pairs={{0,2},{2,0},{4,6},{6,4},{8,10},{10,8},{12,14},{14,12},{16,18},{18,... | collective-permute-start | bytes 393224 | tf_op jit(solution)/shard_map/ppermute | solution.py:194
  55.3 5.1 %collective-permute-start.20 = (bf16[64,1024]{1,0:T(8,128)(2,1)S(1)}, bf16[64,1024]{1,0:T(8,128)(2,1)S(1)}, u32[]{:S(2)}, u32[]{:S(2)}) collective-permute-start(bf16[64,1024]{1,0:T(8,128)(2,1)S(1)} %collective-permute-done.16), channel_id=1, source_target_pairs={{0,2},{2,0},{4,6},{6,4},{8,10},{10,8},{12,14},{14,12},{16,18},{18,... | collective-permute-start | bytes 393224 | tf_op jit(solution)/shard_map/ppermute | solution.py:194
  61.0 1.4 %collective-permute-start.21 = (bf16[8,16,512]{2,1,0:T(8,128)(2,1)S(1)}, bf16[8,16,512]{2,1,0:T(8,128)(2,1)S(1)}, u32[]{:S(2)}, u32[]{:S(2)}) collective-permute-start(bf16[8,16,512]{2,1,0:T(8,128)(2,1)S(1)} %dynamic-slice_bitcast_fusion), channel_id=1, source_target_pairs={{0,1},{1,0},{2,3},{3,2},{4,5},{5,4},{6,7},{7,6},{8,9},{9,8},{10,11... | collective-permute-start | bytes 393224 | tf_op jit(solution)/shard_map/ppermute | solution.py:289
  (4 other events, 28.3 us)

commit v6 on v5

--- a/solution.py
+++ b/solution.py
@@ -142,7 +142,7 @@
                 here = inputs[dx][dy]
                 if here is None:
                     out = own_input[:, cols]
-                elif dy == 0:
+                elif dx:
                     out = here[:, cols]
                 else:
                     out = transform(table, here[:, cols])
@@ -222,7 +222,7 @@
             if dx or dy:
                 inputs.append(move(picked.pop(0), dx=dx, dy=dy))
     table = table_of(rows, tokens)
-    tile = 256 if width % 256 == 0 else width
+    tile = width
     params = pltpu.CompilerParams(vmem_limit_bytes=VMEM_BYTES)
     flops = 4 * rows * 2 * rows * width
     early = pl.pallas_call(
@@ -239,17 +239,17 @@
     gate = jnp.concatenate(gates, 0).astype(F32)
 
     early = early[: py + 1]
-    for dx in range(1, px):
+    first, count = py - 1, (px - 1) * py
+    if count:
         whole = jax.ShapeDtypeStruct((rows + tokens, width), F32)
-        n = dx * py - 1
-        inputs[n] = pl.pallas_call(
+        inputs[first:] = pl.pallas_call(
             functools.partial(more_kernel, tile),
-            out_shape=[whole],
-            in_specs=[vmem] * 2,
-            out_specs=[vmem],
+            out_shape=[whole] * count,
+            in_specs=[vmem] * (1 + count),
+            out_specs=[vmem] * count,
             compiler_params=params,
             cost_estimate=pl.CostEstimate(flops=flops, bytes_accessed=rows * width * 8, transcendentals=0),
-        )(table, inputs[n])[0]
+        )(table, *inputs[first:])
     part = lambda own: jax.ShapeDtypeStruct((group, width), F32 if own else BF16)
     contributions = pl.pallas_call(
         functools.partial(conv_kernel, px, py, nz, tile),

time: 73.8 us -> 73.2 us (level)
  waiting for transfers between devices: 19.7 us -> 20.9 us
  Pallas kernels: 6.03 us -> 5.23 us
    ppermute x21, waiting for transfers between devices: 18.3 us -> 19.5 us  [move(): return lax.ppermute(value, ('seq', 'hist'), pairs)]
  transfers between devices with their start and end apart: 22 -> 22, of which waited for: 11 -> 11; matrix products, arithmetic and copies ran while one was open for 1% -> 1% of each run, Pallas kernels for 6% -> 5%
where the time goes in v6:
time: 73.2 us; the launch traced here: 73 us
  starting transfers between devices  32.8 us (45%)
  waiting for transfers between devices  20.9 us (29%)
  blocking collectives  9.97 us (14%)
  Pallas kernels  5.23 us (7%)
  local copies, waits for them, and re-layouts  2.82 us (4%)
  matrix products  0.87 us (1%)
    ppermute x21, starting transfers between devices, move(): return lax.ppermute(value, ('seq', 'hist'), pairs)  32.7 us
    ppermute x21, waiting for transfers between devices, move(): return lax.ppermute(value, ('seq', 'hist'), pairs)  19.5 us
    all_to_all x1, blocking collectives, local(): lax.all_to_all(total, 'hist', split_axis=0, concat_axis=0, tiled=True)  9.97 us
    unnamed x12, local copies, waits for them, and re-layouts  2.14 us
    pallas_call x1, Pallas kernels, local(): pl.pallas_call(functools.partial(conv_kernel, px, py, nz, tile), out_shap...  2.08 us
    pallas_call x1, Pallas kernels, local(): pl.pallas_call(functools.partial(pick_kernel, px, py, width), out_shape=s...  1.47 us
  transfers between devices with their start and end apart: 22, of which 11 were waited for; matrix products, arithmetic and copies ran while one was open for 1% of the time, Pallas kernels for 5%

profile of v6, /device:TPU:0, one launch (start us, length us, event | category | flops | bytes accessed | tf_op | source)
XLA Modules:
  0.0 73.0 jit_solution(13600134457833154306)
XLA Ops:
  0.0 1.5 %shard_map.55 = (bf16[256,512]{1,0:T(8,128)(2,1)S(1)}, bf16[256,512]{1,0:T(8,128)(2,1)S(1)}, bf16[256,512]{1,0:T(8,128)(2,1)S(1)}, bf16[256,512]{1,0:T(8,128)(2,1)S(1)}, bf16[256,512]{1,0:T(8,128)(2,1)S(1)}) custom-call(bf16[256,2048]{1,0:T(8,128)(2,1)} %history.3, bf16[256,2048]{1,0:T(8,128)(2,1)} %taps.3), custom_call_target="tpu_custom_call" | custom-call | tf_op jit(solution)/shard_map/pallas_call | solution.py:207
  1.5 3.1 %collective-permute-start = (bf16[256,512]{1,0:T(8,128)(2,1)S(1)}, bf16[256,512]{1,0:T(8,128)(2,1)S(1)}, u32[]{:S(2)}, u32[]{:S(2)}) collective-permute-start(bf16[256,512]{1,0:T(8,128)(2,1)S(1)} %get-tuple-element.24), channel_id=1, source_target_pairs={{0,2},{2,0},{4,6},{6,4},{8,10},{10,8},{12,14},{14,12},{16,18},{18,... | collective-permute-start | bytes 786440 | tf_op jit(solution)/shard_map/ppermute | solution.py:194
  4.5 1.5 %collective-permute-start.4 = (bf16[256,512]{1,0:T(8,128)(2,1)S(1)}, bf16[256,512]{1,0:T(8,128)(2,1)S(1)}, u32[]{:S(2)}, u32[]{:S(2)}) collective-permute-start(bf16[256,512]{1,0:T(8,128)(2,1)S(1)} %get-tuple-element.30), channel_id=1, source_target_pairs={{0,16},{2,18},{4,20},{6,22},{8,24},{10,26},{12,28},{14,30},{16,0},... | collective-permute-start | bytes 786440 | tf_op jit(solution)/shard_map/ppermute | solution.py:194
  6.1 1.3 %collective-permute-start.1 = (bf16[256,512]{1,0:T(8,128)(2,1)S(1)}, bf16[256,512]{1,0:T(8,128)(2,1)S(1)}, u32[]{:S(2)}, u32[]{:S(2)}) collective-permute-start(bf16[256,512]{1,0:T(8,128)(2,1)S(1)} %get-tuple-element.28), channel_id=1, source_target_pairs={{4,0},{8,4},{12,8},{20,16},{24,20},{28,24},{5,1},{9,5},{13,9},{21,... | collective-permute-start | bytes 786440 | tf_op jit(solution)/shard_map/ppermute | solution.py:194
  7.4 1.4 %collective-permute-start.3 = (bf16[256,512]{1,0:T(8,128)(2,1)S(1)}, bf16[256,512]{1,0:T(8,128)(2,1)S(1)}, u32[]{:S(2)}, u32[]{:S(2)}) collective-permute-start(bf16[256,512]{1,0:T(8,128)(2,1)S(1)} %get-tuple-element.29), channel_id=1, source_target_pairs={{0,2},{2,0},{4,6},{6,4},{8,10},{10,8},{12,14},{14,12},{16,18},{18,... | collective-permute-start | bytes 786440 | tf_op jit(solution)/shard_map/ppermute | solution.py:194
  8.8 3.6 %collective-permute-done.refs_0_ = bf16[256,512]{1,0:T(8,128)(2,1)S(1)} collective-permute-done((bf16[256,512]{1,0:T(8,128)(2,1)S(1)}, bf16[256,512]{1,0:T(8,128)(2,1)S(1)}, u32[]{:S(2)}, u32[]{:S(2)}) %collective-permute-start) | collective-permute-done | bytes 262176 | tf_op jit(solution)/shard_map/ppermute | solution.py:194
  13.1 1.2 %copy-done.3 = bf16[256,2048]{1,0:T(8,128)(2,1)S(1)} copy-done((bf16[256,2048]{1,0:T(8,128)(2,1)S(1)}, bf16[256,2048]{1,0:T(8,128)(2,1)}, u32[]{:S(2)}) %copy-start.3) | copy-done | bytes 1048600
  16.2 3.4 %collective-permute-start.13 = (bf16[32,1024]{1,0:T(8,128)(2,1)S(1)}, bf16[32,1024]{1,0:T(8,128)(2,1)S(1)}, u32[]{:S(2)}, u32[]{:S(2)}) collective-permute-start(bf16[32,1024]{1,0:T(8,128)(2,1)S(1)} %get-tuple-element.42), channel_id=1, source_target_pairs={{0,2},{2,0},{4,6},{6,4},{8,10},{10,8},{12,14},{14,12},{16,18},{18,... | collective-permute-start | bytes 196616 | tf_op jit(solution)/shard_map/ppermute | solution.py:194
  20.4 2.4 %collective-permute-done.3.refs_5_ = bf16[256,512]{1,0:T(8,128)(2,1)S(1)} collective-permute-done((bf16[256,512]{1,0:T(8,128)(2,1)S(1)}, bf16[256,512]{1,0:T(8,128)(2,1)S(1)}, u32[]{:S(2)}, u32[]{:S(2)}) %collective-permute-start.3) | collective-permute-done | bytes 262176 | tf_op jit(solution)/shard_map/ppermute | solution.py:194
  22.8 2.1 %shard_map.58 = (f32[64,512]{1,0:T(8,128)S(1)}, bf16[64,512]{1,0:T(8,128)(2,1)S(1)}, bf16[64,512]{1,0:T(8,128)(2,1)S(1)}, bf16[64,512]{1,0:T(8,128)(2,1)S(1)}, b...) custom-call(bf16[1024,512]{1,0:T(8,128)(2,1)S(1)} %copy-done.1, ...), custom_call_target="tpu_custom_call" | custom-call | flops 1879048192 | bytes 1048576 | tf_op jit(solution)/shard_map/pallas_call | solution.py:254
  24.9 2.8 %collective-permute-start.10 = (bf16[64,512]{1,0:T(8,128)(2,1)S(1)}, bf16[64,512]{1,0:T(8,128)(2,1)S(1)}, u32[]{:S(2)}, u32[]{:S(2)}) collective-permute-start(bf16[64,512]{1,0:T(8,128)(2,1)S(1)} %get-tuple-element.39), channel_id=1, source_target_pairs={{0,20},{2,22},{4,24},{6,26},{8,28},{10,30},{12,16},{14,18},{16,4},... | collective-permute-start | bytes 196616 | tf_op jit(solution)/shard_map/ppermute | solution.py:194
  27.6 2.6 %collective-permute-start.11 = (bf16[64,512]{1,0:T(8,128)(2,1)S(1)}, bf16[64,512]{1,0:T(8,128)(2,1)S(1)}, u32[]{:S(2)}, u32[]{:S(2)}) collective-permute-start(bf16[64,512]{1,0:T(8,128)(2,1)S(1)} %get-tuple-element.40), channel_id=1, source_target_pairs={{0,24},{2,26},{4,28},{6,30},{8,16},{10,18},{12,20},{14,22},{16,8},... | collective-permute-start | bytes 196616 | tf_op jit(solution)/shard_map/ppermute | solution.py:194
  30.2 2.3 %collective-permute-start.12 = (bf16[64,512]{1,0:T(8,128)(2,1)S(1)}, bf16[64,512]{1,0:T(8,128)(2,1)S(1)}, u32[]{:S(2)}, u32[]{:S(2)}) collective-permute-start(bf16[64,512]{1,0:T(8,128)(2,1)S(1)} %get-tuple-element.41), channel_id=1, source_target_pairs={{0,28},{2,30},{4,16},{6,18},{8,20},{10,22},{12,24},{14,26},{16,12}... | collective-permute-start | bytes 196616 | tf_op jit(solution)/shard_map/ppermute | solution.py:194
  33.5 2.9 %collective-permute-start.8 = (bf16[64,512]{1,0:T(8,128)(2,1)S(1)}, bf16[64,512]{1,0:T(8,128)(2,1)S(1)}, u32[]{:S(2)}, u32[]{:S(2)}) collective-permute-start(bf16[64,512]{1,0:T(8,128)(2,1)S(1)} %get-tuple-element.37), channel_id=1, source_target_pairs={{0,12},{2,14},{4,0},{6,2},{8,4},{10,6},{12,8},{14,10},{16,28},{18,... | collective-permute-start | bytes 196616 | tf_op jit(solution)/shard_map/ppermute | solution.py:194
  37.1 1.6 %collective-permute-done.6 = bf16[64,512]{1,0:T(8,128)(2,1)S(1)} collective-permute-done((bf16[64,512]{1,0:T(8,128)(2,1)S(1)}, bf16[64,512]{1,0:T(8,128)(2,1)S(1)}, u32[]{:S(2)}, u32[]{:S(2)}) %collective-permute-start.6) | collective-permute-done | bytes 65568 | tf_op jit(solution)/shard_map/ppermute | solution.py:194
  40.8 3.4 %collective-permute-start.14 = (bf16[64,1024]{1,0:T(8,128)(2,1)S(1)}, bf16[64,1024]{1,0:T(8,128)(2,1)S(1)}, u32[]{:S(2)}, u32[]{:S(2)}) collective-permute-start(bf16[64,1024]{1,0:T(8,128)(2,1)S(1)} %fusion.19), channel_id=1, source_target_pairs={{0,12},{2,14},{4,0},{6,2},{8,4},{10,6},{12,8},{14,10},{16,28},{18,... | collective-permute-start | bytes 393224 | tf_op jit(solution)/shard_map/ppermute | solution.py:194
  44.8 1.5 %collective-permute-start.17 = (bf16[64,1024]{1,0:T(8,128)(2,1)S(1)}, bf16[64,1024]{1,0:T(8,128)(2,1)S(1)}, u32[]{:S(2)}, u32[]{:S(2)}) collective-permute-start(bf16[64,1024]{1,0:T(8,128)(2,1)S(1)} %fusion.19), channel_id=1, source_target_pairs={{0,2},{2,0},{4,6},{6,4},{8,10},{10,8},{12,14},{14,12},{16,18},{18,... | collective-permute-start | bytes 393224 | tf_op jit(solution)/shard_map/ppermute | solution.py:194
  46.3 1.7 %collective-permute-done.14 = bf16[64,1024]{1,0:T(8,128)(2,1)S(1)} collective-permute-done((bf16[64,1024]{1,0:T(8,128)(2,1)S(1)}, bf16[64,1024]{1,0:T(8,128)(2,1)S(1)}, u32[]{:S(2)}, u32[]{:S(2)}) %collective-permute-start.14) | collective-permute-done | bytes 131104 | tf_op jit(solution)/shard_map/ppermute | solution.py:194
  48.0 1.7 %collective-permute-start.18 = (bf16[64,1024]{1,0:T(8,128)(2,1)S(1)}, bf16[64,1024]{1,0:T(8,128)(2,1)S(1)}, u32[]{:S(2)}, u32[]{:S(2)}) collective-permute-start(bf16[64,1024]{1,0:T(8,128)(2,1)S(1)} %collective-permute-done.14), channel_id=1, source_target_pairs={{0,2},{2,0},{4,6},{6,4},{8,10},{10,8},{12,14},{14,12},{16,18},{18,... | collective-permute-start | bytes 393224 | tf_op jit(solution)/shard_map/ppermute | solution.py:194
  49.7 3.7 %collective-permute-done.15 = bf16[64,1024]{1,0:T(8,128)(2,1)S(1)} collective-permute-done((bf16[64,1024]{1,0:T(8,128)(2,1)S(1)}, bf16[64,1024]{1,0:T(8,128)(2,1)S(1)}, u32[]{:S(2)}, u32[]{:S(2)}) %collective-permute-start.15) | collective-permute-done | bytes 131104 | tf_op jit(solution)/shard_map/ppermute | solution.py:194
  55.9 3.0 %collective-permute-done.19 = bf16[64,1024]{1,0:T(8,128)(2,1)S(1)} collective-permute-done((bf16[64,1024]{1,0:T(8,128)(2,1)S(1)}, bf16[64,1024]{1,0:T(8,128)(2,1)S(1)}, u32[]{:S(2)}, u32[]{:S(2)}) %collective-permute-start.19) | collective-permute-done | bytes 131104 | tf_op jit(solution)/shard_map/ppermute | solution.py:194
  58.9 1.4 %collective-permute-done.20 = bf16[64,1024]{1,0:T(8,128)(2,1)S(1)} collective-permute-done((bf16[64,1024]{1,0:T(8,128)(2,1)S(1)}, bf16[64,1024]{1,0:T(8,128)(2,1)S(1)}, u32[]{:S(2)}, u32[]{:S(2)}) %collective-permute-start.20) | collective-permute-done | bytes 131104 | tf_op jit(solution)/shard_map/ppermute | solution.py:194
  61.0 1.3 %collective-permute-done.21 = bf16[8,16,512]{2,1,0:T(8,128)(2,1)S(1)} collective-permute-done((bf16[8,16,512]{2,1,0:T(8,128)(2,1)S(1)}, bf16[8,16,512]{2,1,0:T(8,128)(2,1)S(1)}, u32[]{:S(2)}, u32[]{:S(2)}) %collective-permute-start.21) | collective-permute-done | bytes 131104 | tf_op jit(solution)/shard_map/ppermute | solution.py:289
  62.4 10.0 %all_to_all.6 = bf16[8,16,512]{2,1,0:T(8,128)(2,1)S(1)} all-to-all(bf16[8,16,512]{2,1,0:T(8,128)(2,1)S(1)} %fusion.20), channel_id=1, replica_groups=mesh['seq'=2,'hist'=8,'chan'=2] {'hist'}, dimensions={0} | all-to-all | bytes 262144 | tf_op jit(solution)/shard_map/all_to_all | solution.py:294
  (46 shorter events, 11.6 us)
Async XLA Ops:
  0.0 55.4 %copy-start = (bf16[2048,512]{1,0:T(8,128)(2,1)S(1)}, bf16[2048,512]{1,0:T(8,128)(2,1)}, u32[]{:S(2)}) copy-start(bf16[2048,512]{1,0:T(8,128)(2,1)} %param.8) | copy-start | bytes 6291460
  1.5 10.9 %collective-permute-start = (bf16[256,512]{1,0:T(8,128)(2,1)S(1)}, bf16[256,512]{1,0:T(8,128)(2,1)S(1)}, u32[]{:S(2)}, u32[]{:S(2)}) collective-permute-start(bf16[256,512]{1,0:T(8,128)(2,1)S(1)} %get-tuple-element.24), channel_id=1, source_target_pairs={{0,2},{2,0},{4,6},{6,4},{8,10},{10,8},{12,14},{14,12},{16,18},{18,... | collective-permute-start | bytes 786440 | tf_op jit(solution)/shard_map/ppermute | solution.py:194
  4.5 11.7 %collective-permute-start.4 = (bf16[256,512]{1,0:T(8,128)(2,1)S(1)}, bf16[256,512]{1,0:T(8,128)(2,1)S(1)}, u32[]{:S(2)}, u32[]{:S(2)}) collective-permute-start(bf16[256,512]{1,0:T(8,128)(2,1)S(1)} %get-tuple-element.30), channel_id=1, source_target_pairs={{0,16},{2,18},{4,20},{6,22},{8,24},{10,26},{12,28},{14,30},{16,0},... | collective-permute-start | bytes 786440 | tf_op jit(solution)/shard_map/ppermute | solution.py:194
  6.0 13.6 %collective-permute-start.5 = (bf16[256,512]{1,0:T(8,128)(2,1)S(1)}, bf16[256,512]{1,0:T(8,128)(2,1)S(1)}, u32[]{:S(2)}, u32[]{:S(2)}) collective-permute-start(bf16[256,512]{1,0:T(8,128)(2,1)S(1)} %get-tuple-element.31), channel_id=1, source_target_pairs={{0,18},{2,16},{4,22},{6,20},{8,26},{10,24},{12,30},{14,28},{16,2},... | collective-permute-start | bytes 786440 | tf_op jit(solution)/shard_map/ppermute | solution.py:194
  6.1 14.3 %collective-permute-start.1 = (bf16[256,512]{1,0:T(8,128)(2,1)S(1)}, bf16[256,512]{1,0:T(8,128)(2,1)S(1)}, u32[]{:S(2)}, u32[]{:S(2)}) collective-permute-start(bf16[256,512]{1,0:T(8,128)(2,1)S(1)} %get-tuple-element.28), channel_id=1, source_target_pairs={{4,0},{8,4},{12,8},{20,16},{24,20},{28,24},{5,1},{9,5},{13,9},{21,... | collective-permute-start | bytes 786440 | tf_op jit(solution)/shard_map/ppermute | solution.py:194
  7.4 15.4 %collective-permute-start.3 = (bf16[256,512]{1,0:T(8,128)(2,1)S(1)}, bf16[256,512]{1,0:T(8,128)(2,1)S(1)}, u32[]{:S(2)}, u32[]{:S(2)}) collective-permute-start(bf16[256,512]{1,0:T(8,128)(2,1)S(1)} %get-tuple-element.29), channel_id=1, source_target_pairs={{0,2},{2,0},{4,6},{6,4},{8,10},{10,8},{12,14},{14,12},{16,18},{18,... | collective-permute-start | bytes 786440 | tf_op jit(solution)/shard_map/ppermute | solution.py:194
  12.4 10.4 %collective-permute-start.2 = (bf16[256,512]{1,0:T(8,128)(2,1)S(1)}, bf16[256,512]{1,0:T(8,128)(2,1)S(1)}, u32[]{:S(2)}, u32[]{:S(2)}) collective-permute-start(bf16[256,512]{1,0:T(8,128)(2,1)S(1)} %collective-permute-done.refs_0_), channel_id=1, source_target_pairs={{6,2},{10,6},{14,10},{22,18},{26,22},{30,26},{7,3},{11,7},{15,11},... | collective-permute-start | bytes 786440 | tf_op jit(solution)/shard_map/ppermute | solution.py:194
  16.2 17.0 %collective-permute-start.13 = (bf16[32,1024]{1,0:T(8,128)(2,1)S(1)}, bf16[32,1024]{1,0:T(8,128)(2,1)S(1)}, u32[]{:S(2)}, u32[]{:S(2)}) collective-permute-start(bf16[32,1024]{1,0:T(8,128)(2,1)S(1)} %get-tuple-element.42), channel_id=1, source_target_pairs={{0,2},{2,0},{4,6},{6,4},{8,10},{10,8},{12,14},{14,12},{16,18},{18,... | collective-permute-start | bytes 196616 | tf_op jit(solution)/shard_map/ppermute | solution.py:194
  22.8 14.1 %copy-start.5 = (bf16[32,2048]{1,0:T(8,128)(2,1)S(1)}, bf16[32,2048]{1,0:T(8,128)(2,1)}, u32[]{:S(2)}) copy-start(bf16[32,2048]{1,0:T(8,128)(2,1)} %gates.1) | copy-start | bytes 393220
  24.9 8.6 %collective-permute-start.10 = (bf16[64,512]{1,0:T(8,128)(2,1)S(1)}, bf16[64,512]{1,0:T(8,128)(2,1)S(1)}, u32[]{:S(2)}, u32[]{:S(2)}) collective-permute-start(bf16[64,512]{1,0:T(8,128)(2,1)S(1)} %get-tuple-element.39), channel_id=1, source_target_pairs={{0,20},{2,22},{4,24},{6,26},{8,28},{10,30},{12,16},{14,18},{16,4},... | collective-permute-start | bytes 196616 | tf_op jit(solution)/shard_map/ppermute | solution.py:194
  27.6 8.7 %collective-permute-start.11 = (bf16[64,512]{1,0:T(8,128)(2,1)S(1)}, bf16[64,512]{1,0:T(8,128)(2,1)S(1)}, u32[]{:S(2)}, u32[]{:S(2)}) collective-permute-start(bf16[64,512]{1,0:T(8,128)(2,1)S(1)} %get-tuple-element.40), channel_id=1, source_target_pairs={{0,24},{2,26},{4,28},{6,30},{8,16},{10,18},{12,20},{14,22},{16,8},... | collective-permute-start | bytes 196616 | tf_op jit(solution)/shard_map/ppermute | solution.py:194
  30.2 6.9 %collective-permute-start.12 = (bf16[64,512]{1,0:T(8,128)(2,1)S(1)}, bf16[64,512]{1,0:T(8,128)(2,1)S(1)}, u32[]{:S(2)}, u32[]{:S(2)}) collective-permute-start(bf16[64,512]{1,0:T(8,128)(2,1)S(1)} %get-tuple-element.41), channel_id=1, source_target_pairs={{0,28},{2,30},{4,16},{6,18},{8,20},{10,22},{12,24},{14,26},{16,12}... | collective-permute-start | bytes 196616 | tf_op jit(solution)/shard_map/ppermute | solution.py:194
  32.5 6.2 %collective-permute-start.6 = (bf16[64,512]{1,0:T(8,128)(2,1)S(1)}, bf16[64,512]{1,0:T(8,128)(2,1)S(1)}, u32[]{:S(2)}, u32[]{:S(2)}) collective-permute-start(bf16[64,512]{1,0:T(8,128)(2,1)S(1)} %get-tuple-element.35), channel_id=1, source_target_pairs={{0,4},{2,6},{4,8},{6,10},{8,12},{10,14},{12,0},{14,2},{16,20},{18,... | collective-permute-start | bytes 196616 | tf_op jit(solution)/shard_map/ppermute | solution.py:194
  33.2 6.7 %collective-permute-start.7 = (bf16[64,512]{1,0:T(8,128)(2,1)S(1)}, bf16[64,512]{1,0:T(8,128)(2,1)S(1)}, u32[]{:S(2)}, u32[]{:S(2)}) collective-permute-start(bf16[64,512]{1,0:T(8,128)(2,1)S(1)} %get-tuple-element.36), channel_id=1, source_target_pairs={{0,8},{2,10},{4,12},{6,14},{8,0},{10,2},{12,4},{14,6},{16,24},{18,... | collective-permute-start | bytes 196616 | tf_op jit(solution)/shard_map/ppermute | solution.py:194
  33.5 6.3 %collective-permute-start.8 = (bf16[64,512]{1,0:T(8,128)(2,1)S(1)}, bf16[64,512]{1,0:T(8,128)(2,1)S(1)}, u32[]{:S(2)}, u32[]{:S(2)}) collective-permute-start(bf16[64,512]{1,0:T(8,128)(2,1)S(1)} %get-tuple-element.37), channel_id=1, source_target_pairs={{0,12},{2,14},{4,0},{6,2},{8,4},{10,6},{12,8},{14,10},{16,28},{18,... | collective-permute-start | bytes 196616 | tf_op jit(solution)/shard_map/ppermute | solution.py:194
  36.4 4.3 %collective-permute-start.9 = (bf16[64,512]{1,0:T(8,128)(2,1)S(1)}, bf16[64,512]{1,0:T(8,128)(2,1)S(1)}, u32[]{:S(2)}, u32[]{:S(2)}) collective-permute-start(bf16[64,512]{1,0:T(8,128)(2,1)S(1)} %get-tuple-element.38), channel_id=1, source_target_pairs={{0,16},{2,18},{4,20},{6,22},{8,24},{10,26},{12,28},{14,30},{16,0},... | collective-permute-start | bytes 196616 | tf_op jit(solution)/shard_map/ppermute | solution.py:194
  40.8 7.2 %collective-permute-start.14 = (bf16[64,1024]{1,0:T(8,128)(2,1)S(1)}, bf16[64,1024]{1,0:T(8,128)(2,1)S(1)}, u32[]{:S(2)}, u32[]{:S(2)}) collective-permute-start(bf16[64,1024]{1,0:T(8,128)(2,1)S(1)} %fusion.19), channel_id=1, source_target_pairs={{0,12},{2,14},{4,0},{6,2},{8,4},{10,6},{12,8},{14,10},{16,28},{18,... | collective-permute-start | bytes 393224 | tf_op jit(solution)/shard_map/ppermute | solution.py:194
  44.2 9.2 %collective-permute-start.15 = (bf16[64,1024]{1,0:T(8,128)(2,1)S(1)}, bf16[64,1024]{1,0:T(8,128)(2,1)S(1)}, u32[]{:S(2)}, u32[]{:S(2)}) collective-permute-start(bf16[64,1024]{1,0:T(8,128)(2,1)S(1)} %fusion.19), channel_id=1, source_target_pairs={{0,8},{2,10},{4,12},{6,14},{8,0},{10,2},{12,4},{14,6},{16,24},{18,... | collective-permute-start | bytes 393224 | tf_op jit(solution)/shard_map/ppermute | solution.py:194
  44.2 10.4 %collective-permute-start.16 = (bf16[64,1024]{1,0:T(8,128)(2,1)S(1)}, bf16[64,1024]{1,0:T(8,128)(2,1)S(1)}, u32[]{:S(2)}, u32[]{:S(2)}) collective-permute-start(bf16[64,1024]{1,0:T(8,128)(2,1)S(1)} %fusion.19), channel_id=1, source_target_pairs={{0,4},{2,6},{4,8},{6,10},{8,12},{10,14},{12,0},{14,2},{16,20},{18,... | collective-permute-start | bytes 393224 | tf_op jit(solution)/shard_map/ppermute | solution.py:194
  44.8 11.0 %collective-permute-start.17 = (bf16[64,1024]{1,0:T(8,128)(2,1)S(1)}, bf16[64,1024]{1,0:T(8,128)(2,1)S(1)}, u32[]{:S(2)}, u32[]{:S(2)}) collective-permute-start(bf16[64,1024]{1,0:T(8,128)(2,1)S(1)} %fusion.19), channel_id=1, source_target_pairs={{0,2},{2,0},{4,6},{6,4},{8,10},{10,8},{12,14},{14,12},{16,18},{18,... | collective-permute-start | bytes 393224 | tf_op jit(solution)/shard_map/ppermute | solution.py:194
  48.0 7.9 %collective-permute-start.18 = (bf16[64,1024]{1,0:T(8,128)(2,1)S(1)}, bf16[64,1024]{1,0:T(8,128)(2,1)S(1)}, u32[]{:S(2)}, u32[]{:S(2)}) collective-permute-start(bf16[64,1024]{1,0:T(8,128)(2,1)S(1)} %collective-permute-done.14), channel_id=1, source_target_pairs={{0,2},{2,0},{4,6},{6,4},{8,10},{10,8},{12,14},{14,12},{16,18},{18,... | collective-permute-start | bytes 393224 | tf_op jit(solution)/shard_map/ppermute | solution.py:194
  53.4 5.5 %collective-permute-start.19 = (bf16[64,1024]{1,0:T(8,128)(2,1)S(1)}, bf16[64,1024]{1,0:T(8,128)(2,1)S(1)}, u32[]{:S(2)}, u32[]{:S(2)}) collective-permute-start(bf16[64,1024]{1,0:T(8,128)(2,1)S(1)} %collective-permute-done.15), channel_id=1, source_target_pairs={{0,2},{2,0},{4,6},{6,4},{8,10},{10,8},{12,14},{14,12},{16,18},{18,... | collective-permute-start | bytes 393224 | tf_op jit(solution)/shard_map/ppermute | solution.py:194
  54.6 5.8 %collective-permute-start.20 = (bf16[64,1024]{1,0:T(8,128)(2,1)S(1)}, bf16[64,1024]{1,0:T(8,128)(2,1)S(1)}, u32[]{:S(2)}, u32[]{:S(2)}) collective-permute-start(bf16[64,1024]{1,0:T(8,128)(2,1)S(1)} %collective-permute-done.16), channel_id=1, source_target_pairs={{0,2},{2,0},{4,6},{6,4},{8,10},{10,8},{12,14},{14,12},{16,18},{18,... | collective-permute-start | bytes 393224 | tf_op jit(solution)/shard_map/ppermute | solution.py:194
  60.9 1.4 %collective-permute-start.21 = (bf16[8,16,512]{2,1,0:T(8,128)(2,1)S(1)}, bf16[8,16,512]{2,1,0:T(8,128)(2,1)S(1)}, u32[]{:S(2)}, u32[]{:S(2)}) collective-permute-start(bf16[8,16,512]{2,1,0:T(8,128)(2,1)S(1)} %dynamic-slice_bitcast_fusion), channel_id=1, source_target_pairs={{0,1},{1,0},{2,3},{3,2},{4,5},{5,4},{6,7},{7,6},{8,9},{9,8},{10,11... | collective-permute-start | bytes 393224 | tf_op jit(solution)/shard_map/ppermute | solution.py:289
  (4 other events, 28.3 us)

commit v7 on v6

--- a/solution.py
+++ b/solution.py
@@ -182,11 +182,11 @@
     y = lax.axis_index("hist") % py
     z = lax.axis_index("hist") // py
 
-    def move(value, dx=0, dz=0, dy=0, wrap=True, only=None):
+    def move(value, dx=0, dz=0, dy=0, wrap=True, only=None, pair=False):
         pairs = []
         for s in range(seqs):
             for h in range(hists):
-                to_z = h // py + dz
+                to_z = (h // py) ^ dz if pair else h // py + dz
                 if (not wrap and not 0 <= to_z < nz) or only not in (None, h % py):
                     continue
                 target = (s ^ dx) * hists + (to_z % nz) * py + ((h % py) ^ dy)
@@ -272,14 +272,20 @@
     conv = jnp.concatenate(ordered(sx, sums), 1)
     gated = (conv * gate).astype(BF16)
 
-    along = [gated] + [move(gated, dz=-dz) for dz in range(1, nz)]
+    paired = nz & (nz - 1) == 0
+    along = [gated] + [move(gated, dz=dz if paired else -dz, pair=paired) for dz in range(1, nz)]
     total = 0.0
     for dy in range(py):
         across = [move(v, dy=dy) if dy else v for v in along]
         weight = lax.dynamic_slice_in_dim(out_weight, (y ^ dy) * wide, wide, 0)
         total = total + jnp.dot(jnp.concatenate(across, 0), weight, preferred_element_type=F32)
     total = total.astype(BF16).reshape(nz, group, -1)
-    total = jnp.roll(total, z, axis=0).reshape(tokens, -1)
+    if not paired:
+        total = jnp.roll(total, z, axis=0)
+    for bit in range(nz.bit_length() - 1 if paired else 0):
+        both = total.reshape(nz >> (bit + 1), 2, 1 << bit, group, total.shape[-1])
+        total = jnp.where((z >> bit) & 1 == 0, both, both[:, ::-1]).reshape(total.shape)
+    total = total.reshape(tokens, -1)
     share = owned // chans
     total = total.reshape(hists, chans, share, -1)
     if chans == 2:

time: 73.2 us -> 73.1 us (level)
  waiting for transfers between devices: 20.9 us -> 18.2 us
  blocking collectives: 9.97 us -> 11.5 us
  starting transfers between devices: 32.8 us -> 33.8 us
    ppermute x21, waiting for transfers between devices: 19.5 us -> 16.9 us  [move(): return lax.ppermute(value, ('seq', 'hist'), pairs)]
    all_to_all x1, blocking collectives: 9.97 us -> 11.5 us  [local(): lax.all_to_all(total, 'hist', split_axis=0, concat_axis=0, tiled=True)]
    ppermute x21, starting transfers between devices: 32.7 us -> 33.7 us  [move(): return lax.ppermute(value, ('seq', 'hist'), pairs)]
  transfers between devices with their start and end apart: 22 -> 22, of which waited for: 11 -> 10; matrix products, arithmetic and copies ran while one was open for 1% -> 1% of each run, Pallas kernels for 5% -> 5%
where the time goes in v7:
time: 73.1 us; the launch traced here: 72.9 us
  starting transfers between devices  33.8 us (46%)
  waiting for transfers between devices  18.2 us (25%)
  blocking collectives  11.5 us (16%)
  Pallas kernels  5.23 us (7%)
  local copies, waits for them, and re-layouts  2.82 us (4%)
  matrix products  0.87 us (1%)
    ppermute x21, starting transfers between devices, move(): return lax.ppermute(value, ('seq', 'hist'), pairs)  33.7 us
    ppermute x21, waiting for transfers between devices, move(): return lax.ppermute(value, ('seq', 'hist'), pairs)  16.9 us
    all_to_all x1, blocking collectives, local(): lax.all_to_all(total, 'hist', split_axis=0, concat_axis=0, tiled=True)  11.5 us
    unnamed x12, local copies, waits for them, and re-layouts  2.14 us
    pallas_call x1, Pallas kernels, local(): pl.pallas_call(functools.partial(conv_kernel, px, py, nz, tile), out_shap...  2.08 us
    pallas_call x1, Pallas kernels, local(): pl.pallas_call(functools.partial(pick_kernel, px, py, width), out_shape=s...  1.47 us
  transfers between devices with their start and end apart: 22, of which 10 were waited for; matrix products, arithmetic and copies ran while one was open for 1% of the time, Pallas kernels for 5%

profile of v7, /device:TPU:0, one launch (start us, length us, event | category | flops | bytes accessed | tf_op | source)
XLA Modules:
  0.0 72.9 jit_solution(17092714631417024532)
XLA Ops:
  0.0 1.5 %shard_map.55 = (bf16[256,512]{1,0:T(8,128)(2,1)S(1)}, bf16[256,512]{1,0:T(8,128)(2,1)S(1)}, bf16[256,512]{1,0:T(8,128)(2,1)S(1)}, bf16[256,512]{1,0:T(8,128)(2,1)S(1)}, bf16[256,512]{1,0:T(8,128)(2,1)S(1)}) custom-call(bf16[256,2048]{1,0:T(8,128)(2,1)} %history.3, bf16[256,2048]{1,0:T(8,128)(2,1)} %taps.3), custom_call_target="tpu_custom_call" | custom-call | tf_op jit(solution)/shard_map/pallas_call | solution.py:207
  1.5 3.1 %collective-permute-start = (bf16[256,512]{1,0:T(8,128)(2,1)S(1)}, bf16[256,512]{1,0:T(8,128)(2,1)S(1)}, u32[]{:S(2)}, u32[]{:S(2)}) collective-permute-start(bf16[256,512]{1,0:T(8,128)(2,1)S(1)} %get-tuple-element.24), channel_id=1, source_target_pairs={{0,2},{2,0},{4,6},{6,4},{8,10},{10,8},{12,14},{14,12},{16,18},{18,... | collective-permute-start | bytes 786440 | tf_op jit(solution)/shard_map/ppermute | solution.py:194
  4.5 1.5 %collective-permute-start.4 = (bf16[256,512]{1,0:T(8,128)(2,1)S(1)}, bf16[256,512]{1,0:T(8,128)(2,1)S(1)}, u32[]{:S(2)}, u32[]{:S(2)}) collective-permute-start(bf16[256,512]{1,0:T(8,128)(2,1)S(1)} %get-tuple-element.30), channel_id=1, source_target_pairs={{0,16},{2,18},{4,20},{6,22},{8,24},{10,26},{12,28},{14,30},{16,0},... | collective-permute-start | bytes 786440 | tf_op jit(solution)/shard_map/ppermute | solution.py:194
  6.1 1.3 %collective-permute-start.1 = (bf16[256,512]{1,0:T(8,128)(2,1)S(1)}, bf16[256,512]{1,0:T(8,128)(2,1)S(1)}, u32[]{:S(2)}, u32[]{:S(2)}) collective-permute-start(bf16[256,512]{1,0:T(8,128)(2,1)S(1)} %get-tuple-element.28), channel_id=1, source_target_pairs={{4,0},{8,4},{12,8},{20,16},{24,20},{28,24},{5,1},{9,5},{13,9},{21,... | collective-permute-start | bytes 786440 | tf_op jit(solution)/shard_map/ppermute | solution.py:194
  7.4 1.4 %collective-permute-start.3 = (bf16[256,512]{1,0:T(8,128)(2,1)S(1)}, bf16[256,512]{1,0:T(8,128)(2,1)S(1)}, u32[]{:S(2)}, u32[]{:S(2)}) collective-permute-start(bf16[256,512]{1,0:T(8,128)(2,1)S(1)} %get-tuple-element.29), channel_id=1, source_target_pairs={{0,2},{2,0},{4,6},{6,4},{8,10},{10,8},{12,14},{14,12},{16,18},{18,... | collective-permute-start | bytes 786440 | tf_op jit(solution)/shard_map/ppermute | solution.py:194
  8.8 3.6 %collective-permute-done.refs_0_ = bf16[256,512]{1,0:T(8,128)(2,1)S(1)} collective-permute-done((bf16[256,512]{1,0:T(8,128)(2,1)S(1)}, bf16[256,512]{1,0:T(8,128)(2,1)S(1)}, u32[]{:S(2)}, u32[]{:S(2)}) %collective-permute-start) | collective-permute-done | bytes 262176 | tf_op jit(solution)/shard_map/ppermute | solution.py:194
  13.1 1.2 %copy-done.3 = bf16[256,2048]{1,0:T(8,128)(2,1)S(1)} copy-done((bf16[256,2048]{1,0:T(8,128)(2,1)S(1)}, bf16[256,2048]{1,0:T(8,128)(2,1)}, u32[]{:S(2)}) %copy-start.3) | copy-done | bytes 1048600
  16.2 3.4 %collective-permute-start.13 = (bf16[32,1024]{1,0:T(8,128)(2,1)S(1)}, bf16[32,1024]{1,0:T(8,128)(2,1)S(1)}, u32[]{:S(2)}, u32[]{:S(2)}) collective-permute-start(bf16[32,1024]{1,0:T(8,128)(2,1)S(1)} %get-tuple-element.42), channel_id=1, source_target_pairs={{0,2},{2,0},{4,6},{6,4},{8,10},{10,8},{12,14},{14,12},{16,18},{18,... | collective-permute-start | bytes 196616 | tf_op jit(solution)/shard_map/ppermute | solution.py:194
  20.4 2.4 %collective-permute-done.3.refs_5_ = bf16[256,512]{1,0:T(8,128)(2,1)S(1)} collective-permute-done((bf16[256,512]{1,0:T(8,128)(2,1)S(1)}, bf16[256,512]{1,0:T(8,128)(2,1)S(1)}, u32[]{:S(2)}, u32[]{:S(2)}) %collective-permute-start.3) | collective-permute-done | bytes 262176 | tf_op jit(solution)/shard_map/ppermute | solution.py:194
  22.8 2.1 %shard_map.58 = (f32[64,512]{1,0:T(8,128)S(1)}, bf16[64,512]{1,0:T(8,128)(2,1)S(1)}, bf16[64,512]{1,0:T(8,128)(2,1)S(1)}, bf16[64,512]{1,0:T(8,128)(2,1)S(1)}, b...) custom-call(bf16[1024,512]{1,0:T(8,128)(2,1)S(1)} %copy-done.1, ...), custom_call_target="tpu_custom_call" | custom-call | flops 1879048192 | bytes 1048576 | tf_op jit(solution)/shard_map/pallas_call | solution.py:254
  24.9 2.8 %collective-permute-start.10 = (bf16[64,512]{1,0:T(8,128)(2,1)S(1)}, bf16[64,512]{1,0:T(8,128)(2,1)S(1)}, u32[]{:S(2)}, u32[]{:S(2)}) collective-permute-start(bf16[64,512]{1,0:T(8,128)(2,1)S(1)} %get-tuple-element.39), channel_id=1, source_target_pairs={{0,20},{2,22},{4,24},{6,26},{8,28},{10,30},{12,16},{14,18},{16,4},... | collective-permute-start | bytes 196616 | tf_op jit(solution)/shard_map/ppermute | solution.py:194
  27.6 2.6 %collective-permute-start.11 = (bf16[64,512]{1,0:T(8,128)(2,1)S(1)}, bf16[64,512]{1,0:T(8,128)(2,1)S(1)}, u32[]{:S(2)}, u32[]{:S(2)}) collective-permute-start(bf16[64,512]{1,0:T(8,128)(2,1)S(1)} %get-tuple-element.40), channel_id=1, source_target_pairs={{0,24},{2,26},{4,28},{6,30},{8,16},{10,18},{12,20},{14,22},{16,8},... | collective-permute-start | bytes 196616 | tf_op jit(solution)/shard_map/ppermute | solution.py:194
  30.2 2.3 %collective-permute-start.12 = (bf16[64,512]{1,0:T(8,128)(2,1)S(1)}, bf16[64,512]{1,0:T(8,128)(2,1)S(1)}, u32[]{:S(2)}, u32[]{:S(2)}) collective-permute-start(bf16[64,512]{1,0:T(8,128)(2,1)S(1)} %get-tuple-element.41), channel_id=1, source_target_pairs={{0,28},{2,30},{4,16},{6,18},{8,20},{10,22},{12,24},{14,26},{16,12}... | collective-permute-start | bytes 196616 | tf_op jit(solution)/shard_map/ppermute | solution.py:194
  33.5 2.9 %collective-permute-start.8 = (bf16[64,512]{1,0:T(8,128)(2,1)S(1)}, bf16[64,512]{1,0:T(8,128)(2,1)S(1)}, u32[]{:S(2)}, u32[]{:S(2)}) collective-permute-start(bf16[64,512]{1,0:T(8,128)(2,1)S(1)} %get-tuple-element.37), channel_id=1, source_target_pairs={{0,12},{2,14},{4,0},{6,2},{8,4},{10,6},{12,8},{14,10},{16,28},{18,... | collective-permute-start | bytes 196616 | tf_op jit(solution)/shard_map/ppermute | solution.py:194
  37.1 1.6 %collective-permute-done.6 = bf16[64,512]{1,0:T(8,128)(2,1)S(1)} collective-permute-done((bf16[64,512]{1,0:T(8,128)(2,1)S(1)}, bf16[64,512]{1,0:T(8,128)(2,1)S(1)}, u32[]{:S(2)}, u32[]{:S(2)}) %collective-permute-start.6) | collective-permute-done | bytes 65568 | tf_op jit(solution)/shard_map/ppermute | solution.py:194
  41.4 3.4 %collective-permute-start.15 = (bf16[64,1024]{1,0:T(8,128)(2,1)S(1)}, bf16[64,1024]{1,0:T(8,128)(2,1)S(1)}, u32[]{:S(2)}, u32[]{:S(2)}) collective-permute-start(bf16[64,1024]{1,0:T(8,128)(2,1)S(1)} %fusion.19), channel_id=1, source_target_pairs={{0,8},{2,10},{4,12},{6,14},{8,0},{10,2},{12,4},{14,6},{16,24},{18,... | collective-permute-start | bytes 393224 | tf_op jit(solution)/shard_map/ppermute | solution.py:194
  45.2 1.5 %collective-permute-start.17 = (bf16[64,1024]{1,0:T(8,128)(2,1)S(1)}, bf16[64,1024]{1,0:T(8,128)(2,1)S(1)}, u32[]{:S(2)}, u32[]{:S(2)}) collective-permute-start(bf16[64,1024]{1,0:T(8,128)(2,1)S(1)} %fusion.19), channel_id=1, source_target_pairs={{0,2},{2,0},{4,6},{6,4},{8,10},{10,8},{12,14},{14,12},{16,18},{18,... | collective-permute-start | bytes 393224 | tf_op jit(solution)/shard_map/ppermute | solution.py:194
  46.7 2.3 %collective-permute-start.18 = (bf16[64,1024]{1,0:T(8,128)(2,1)S(1)}, bf16[64,1024]{1,0:T(8,128)(2,1)S(1)}, u32[]{:S(2)}, u32[]{:S(2)}) collective-permute-start(bf16[64,1024]{1,0:T(8,128)(2,1)S(1)} %collective-permute-done.14), channel_id=1, source_target_pairs={{0,2},{2,0},{4,6},{6,4},{8,10},{10,8},{12,14},{14,12},{16,18},{18,... | collective-permute-start | bytes 393224 | tf_op jit(solution)/shard_map/ppermute | solution.py:194
  49.1 3.2 %collective-permute-done.15 = bf16[64,1024]{1,0:T(8,128)(2,1)S(1)} collective-permute-done((bf16[64,1024]{1,0:T(8,128)(2,1)S(1)}, bf16[64,1024]{1,0:T(8,128)(2,1)S(1)}, u32[]{:S(2)}, u32[]{:S(2)}) %collective-permute-start.15) | collective-permute-done | bytes 131104 | tf_op jit(solution)/shard_map/ppermute | solution.py:194
  52.3 1.2 %collective-permute-start.19 = (bf16[64,1024]{1,0:T(8,128)(2,1)S(1)}, bf16[64,1024]{1,0:T(8,128)(2,1)S(1)}, u32[]{:S(2)}, u32[]{:S(2)}) collective-permute-start(bf16[64,1024]{1,0:T(8,128)(2,1)S(1)} %collective-permute-done.15), channel_id=1, source_target_pairs={{0,2},{2,0},{4,6},{6,4},{8,10},{10,8},{12,14},{14,12},{16,18},{18,... | collective-permute-start | bytes 393224 | tf_op jit(solution)/shard_map/ppermute | solution.py:194
  54.8 2.5 %collective-permute-done.19 = bf16[64,1024]{1,0:T(8,128)(2,1)S(1)} collective-permute-done((bf16[64,1024]{1,0:T(8,128)(2,1)S(1)}, bf16[64,1024]{1,0:T(8,128)(2,1)S(1)}, u32[]{:S(2)}, u32[]{:S(2)}) %collective-permute-start.19) | collective-permute-done | bytes 131104 | tf_op jit(solution)/shard_map/ppermute | solution.py:194
  57.3 1.4 %collective-permute-done.20 = bf16[64,1024]{1,0:T(8,128)(2,1)S(1)} collective-permute-done((bf16[64,1024]{1,0:T(8,128)(2,1)S(1)}, bf16[64,1024]{1,0:T(8,128)(2,1)S(1)}, u32[]{:S(2)}, u32[]{:S(2)}) %collective-permute-start.20) | collective-permute-done | bytes 131104 | tf_op jit(solution)/shard_map/ppermute | solution.py:194
  59.3 1.3 %collective-permute-done.21 = bf16[8,16,512]{2,1,0:T(8,128)(2,1)S(1)} collective-permute-done((bf16[8,16,512]{2,1,0:T(8,128)(2,1)S(1)}, bf16[8,16,512]{2,1,0:T(8,128)(2,1)S(1)}, u32[]{:S(2)}, u32[]{:S(2)}) %collective-permute-start.21) | collective-permute-done | bytes 131104 | tf_op jit(solution)/shard_map/ppermute | solution.py:295
  60.7 11.5 %all_to_all.6 = bf16[8,16,512]{2,1,0:T(8,128)(2,1)S(1)} all-to-all(bf16[8,16,512]{2,1,0:T(8,128)(2,1)S(1)} %fusion.20), channel_id=1, replica_groups=mesh['seq'=2,'hist'=8,'chan'=2] {'hist'}, dimensions={0} | all-to-all | bytes 262144 | tf_op jit(solution)/shard_map/all_to_all | solution.py:300
  (47 shorter events, 10.9 us)
Async XLA Ops:
  0.0 54.3 %copy-start = (bf16[2048,512]{1,0:T(8,128)(2,1)S(1)}, bf16[2048,512]{1,0:T(8,128)(2,1)}, u32[]{:S(2)}) copy-start(bf16[2048,512]{1,0:T(8,128)(2,1)} %param.8) | copy-start | bytes 6291460
  1.5 10.9 %collective-permute-start = (bf16[256,512]{1,0:T(8,128)(2,1)S(1)}, bf16[256,512]{1,0:T(8,128)(2,1)S(1)}, u32[]{:S(2)}, u32[]{:S(2)}) collective-permute-start(bf16[256,512]{1,0:T(8,128)(2,1)S(1)} %get-tuple-element.24), channel_id=1, source_target_pairs={{0,2},{2,0},{4,6},{6,4},{8,10},{10,8},{12,14},{14,12},{16,18},{18,... | collective-permute-start | bytes 786440 | tf_op jit(solution)/shard_map/ppermute | solution.py:194
  4.5 11.7 %collective-permute-start.4 = (bf16[256,512]{1,0:T(8,128)(2,1)S(1)}, bf16[256,512]{1,0:T(8,128)(2,1)S(1)}, u32[]{:S(2)}, u32[]{:S(2)}) collective-permute-start(bf16[256,512]{1,0:T(8,128)(2,1)S(1)} %get-tuple-element.30), channel_id=1, source_target_pairs={{0,16},{2,18},{4,20},{6,22},{8,24},{10,26},{12,28},{14,30},{16,0},... | collective-permute-start | bytes 786440 | tf_op jit(solution)/shard_map/ppermute | solution.py:194
  6.0 13.6 %collective-permute-start.5 = (bf16[256,512]{1,0:T(8,128)(2,1)S(1)}, bf16[256,512]{1,0:T(8,128)(2,1)S(1)}, u32[]{:S(2)}, u32[]{:S(2)}) collective-permute-start(bf16[256,512]{1,0:T(8,128)(2,1)S(1)} %get-tuple-element.31), channel_id=1, source_target_pairs={{0,18},{2,16},{4,22},{6,20},{8,26},{10,24},{12,30},{14,28},{16,2},... | collective-permute-start | bytes 786440 | tf_op jit(solution)/shard_map/ppermute | solution.py:194
  6.1 14.3 %collective-permute-start.1 = (bf16[256,512]{1,0:T(8,128)(2,1)S(1)}, bf16[256,512]{1,0:T(8,128)(2,1)S(1)}, u32[]{:S(2)}, u32[]{:S(2)}) collective-permute-start(bf16[256,512]{1,0:T(8,128)(2,1)S(1)} %get-tuple-element.28), channel_id=1, source_target_pairs={{4,0},{8,4},{12,8},{20,16},{24,20},{28,24},{5,1},{9,5},{13,9},{21,... | collective-permute-start | bytes 786440 | tf_op jit(solution)/shard_map/ppermute | solution.py:194
  7.4 15.4 %collective-permute-start.3 = (bf16[256,512]{1,0:T(8,128)(2,1)S(1)}, bf16[256,512]{1,0:T(8,128)(2,1)S(1)}, u32[]{:S(2)}, u32[]{:S(2)}) collective-permute-start(bf16[256,512]{1,0:T(8,128)(2,1)S(1)} %get-tuple-element.29), channel_id=1, source_target_pairs={{0,2},{2,0},{4,6},{6,4},{8,10},{10,8},{12,14},{14,12},{16,18},{18,... | collective-permute-start | bytes 786440 | tf_op jit(solution)/shard_map/ppermute | solution.py:194
  12.4 10.4 %collective-permute-start.2 = (bf16[256,512]{1,0:T(8,128)(2,1)S(1)}, bf16[256,512]{1,0:T(8,128)(2,1)S(1)}, u32[]{:S(2)}, u32[]{:S(2)}) collective-permute-start(bf16[256,512]{1,0:T(8,128)(2,1)S(1)} %collective-permute-done.refs_0_), channel_id=1, source_target_pairs={{6,2},{10,6},{14,10},{22,18},{26,22},{30,26},{7,3},{11,7},{15,11},... | collective-permute-start | bytes 786440 | tf_op jit(solution)/shard_map/ppermute | solution.py:194
  16.2 17.0 %collective-permute-start.13 = (bf16[32,1024]{1,0:T(8,128)(2,1)S(1)}, bf16[32,1024]{1,0:T(8,128)(2,1)S(1)}, u32[]{:S(2)}, u32[]{:S(2)}) collective-permute-start(bf16[32,1024]{1,0:T(8,128)(2,1)S(1)} %get-tuple-element.42), channel_id=1, source_target_pairs={{0,2},{2,0},{4,6},{6,4},{8,10},{10,8},{12,14},{14,12},{16,18},{18,... | collective-permute-start | bytes 196616 | tf_op jit(solution)/shard_map/ppermute | solution.py:194
  22.8 14.1 %copy-start.5 = (bf16[32,2048]{1,0:T(8,128)(2,1)S(1)}, bf16[32,2048]{1,0:T(8,128)(2,1)}, u32[]{:S(2)}) copy-start(bf16[32,2048]{1,0:T(8,128)(2,1)} %gates.1) | copy-start | bytes 393220
  24.9 8.6 %collective-permute-start.10 = (bf16[64,512]{1,0:T(8,128)(2,1)S(1)}, bf16[64,512]{1,0:T(8,128)(2,1)S(1)}, u32[]{:S(2)}, u32[]{:S(2)}) collective-permute-start(bf16[64,512]{1,0:T(8,128)(2,1)S(1)} %get-tuple-element.39), channel_id=1, source_target_pairs={{0,20},{2,22},{4,24},{6,26},{8,28},{10,30},{12,16},{14,18},{16,4},... | collective-permute-start | bytes 196616 | tf_op jit(solution)/shard_map/ppermute | solution.py:194
  27.6 8.7 %collective-permute-start.11 = (bf16[64,512]{1,0:T(8,128)(2,1)S(1)}, bf16[64,512]{1,0:T(8,128)(2,1)S(1)}, u32[]{:S(2)}, u32[]{:S(2)}) collective-permute-start(bf16[64,512]{1,0:T(8,128)(2,1)S(1)} %get-tuple-element.40), channel_id=1, source_target_pairs={{0,24},{2,26},{4,28},{6,30},{8,16},{10,18},{12,20},{14,22},{16,8},... | collective-permute-start | bytes 196616 | tf_op jit(solution)/shard_map/ppermute | solution.py:194
  30.2 6.9 %collective-permute-start.12 = (bf16[64,512]{1,0:T(8,128)(2,1)S(1)}, bf16[64,512]{1,0:T(8,128)(2,1)S(1)}, u32[]{:S(2)}, u32[]{:S(2)}) collective-permute-start(bf16[64,512]{1,0:T(8,128)(2,1)S(1)} %get-tuple-element.41), channel_id=1, source_target_pairs={{0,28},{2,30},{4,16},{6,18},{8,20},{10,22},{12,24},{14,26},{16,12}... | collective-permute-start | bytes 196616 | tf_op jit(solution)/shard_map/ppermute | solution.py:194
  32.5 6.2 %collective-permute-start.6 = (bf16[64,512]{1,0:T(8,128)(2,1)S(1)}, bf16[64,512]{1,0:T(8,128)(2,1)S(1)}, u32[]{:S(2)}, u32[]{:S(2)}) collective-permute-start(bf16[64,512]{1,0:T(8,128)(2,1)S(1)} %get-tuple-element.35), channel_id=1, source_target_pairs={{0,4},{2,6},{4,8},{6,10},{8,12},{10,14},{12,0},{14,2},{16,20},{18,... | collective-permute-start | bytes 196616 | tf_op jit(solution)/shard_map/ppermute | solution.py:194
  33.2 6.7 %collective-permute-start.7 = (bf16[64,512]{1,0:T(8,128)(2,1)S(1)}, bf16[64,512]{1,0:T(8,128)(2,1)S(1)}, u32[]{:S(2)}, u32[]{:S(2)}) collective-permute-start(bf16[64,512]{1,0:T(8,128)(2,1)S(1)} %get-tuple-element.36), channel_id=1, source_target_pairs={{0,8},{2,10},{4,12},{6,14},{8,0},{10,2},{12,4},{14,6},{16,24},{18,... | collective-permute-start | bytes 196616 | tf_op jit(solution)/shard_map/ppermute | solution.py:194
  33.5 6.3 %collective-permute-start.8 = (bf16[64,512]{1,0:T(8,128)(2,1)S(1)}, bf16[64,512]{1,0:T(8,128)(2,1)S(1)}, u32[]{:S(2)}, u32[]{:S(2)}) collective-permute-start(bf16[64,512]{1,0:T(8,128)(2,1)S(1)} %get-tuple-element.37), channel_id=1, source_target_pairs={{0,12},{2,14},{4,0},{6,2},{8,4},{10,6},{12,8},{14,10},{16,28},{18,... | collective-permute-start | bytes 196616 | tf_op jit(solution)/shard_map/ppermute | solution.py:194
  36.4 4.3 %collective-permute-start.9 = (bf16[64,512]{1,0:T(8,128)(2,1)S(1)}, bf16[64,512]{1,0:T(8,128)(2,1)S(1)}, u32[]{:S(2)}, u32[]{:S(2)}) collective-permute-start(bf16[64,512]{1,0:T(8,128)(2,1)S(1)} %get-tuple-element.38), channel_id=1, source_target_pairs={{0,16},{2,18},{4,20},{6,22},{8,24},{10,26},{12,28},{14,30},{16,0},... | collective-permute-start | bytes 196616 | tf_op jit(solution)/shard_map/ppermute | solution.py:194
  40.8 6.0 %collective-permute-start.14 = (bf16[64,1024]{1,0:T(8,128)(2,1)S(1)}, bf16[64,1024]{1,0:T(8,128)(2,1)S(1)}, u32[]{:S(2)}, u32[]{:S(2)}) collective-permute-start(bf16[64,1024]{1,0:T(8,128)(2,1)S(1)} %fusion.19), channel_id=1, source_target_pairs={{0,4},{2,6},{4,0},{6,2},{8,12},{10,14},{12,8},{14,10},{16,20},{18,... | collective-permute-start | bytes 393224 | tf_op jit(solution)/shard_map/ppermute | solution.py:194
  41.4 10.9 %collective-permute-start.15 = (bf16[64,1024]{1,0:T(8,128)(2,1)S(1)}, bf16[64,1024]{1,0:T(8,128)(2,1)S(1)}, u32[]{:S(2)}, u32[]{:S(2)}) collective-permute-start(bf16[64,1024]{1,0:T(8,128)(2,1)S(1)} %fusion.19), channel_id=1, source_target_pairs={{0,8},{2,10},{4,12},{6,14},{8,0},{10,2},{12,4},{14,6},{16,24},{18,... | collective-permute-start | bytes 393224 | tf_op jit(solution)/shard_map/ppermute | solution.py:194
  44.8 8.7 %collective-permute-start.16 = (bf16[64,1024]{1,0:T(8,128)(2,1)S(1)}, bf16[64,1024]{1,0:T(8,128)(2,1)S(1)}, u32[]{:S(2)}, u32[]{:S(2)}) collective-permute-start(bf16[64,1024]{1,0:T(8,128)(2,1)S(1)} %fusion.19), channel_id=1, source_target_pairs={{0,12},{2,14},{4,8},{6,10},{8,4},{10,6},{12,0},{14,2},{16,28},{18,... | collective-permute-start | bytes 393224 | tf_op jit(solution)/shard_map/ppermute | solution.py:194
  45.2 9.5 %collective-permute-start.17 = (bf16[64,1024]{1,0:T(8,128)(2,1)S(1)}, bf16[64,1024]{1,0:T(8,128)(2,1)S(1)}, u32[]{:S(2)}, u32[]{:S(2)}) collective-permute-start(bf16[64,1024]{1,0:T(8,128)(2,1)S(1)} %fusion.19), channel_id=1, source_target_pairs={{0,2},{2,0},{4,6},{6,4},{8,10},{10,8},{12,14},{14,12},{16,18},{18,... | collective-permute-start | bytes 393224 | tf_op jit(solution)/shard_map/ppermute | solution.py:194
  46.7 8.0 %collective-permute-start.18 = (bf16[64,1024]{1,0:T(8,128)(2,1)S(1)}, bf16[64,1024]{1,0:T(8,128)(2,1)S(1)}, u32[]{:S(2)}, u32[]{:S(2)}) collective-permute-start(bf16[64,1024]{1,0:T(8,128)(2,1)S(1)} %collective-permute-done.14), channel_id=1, source_target_pairs={{0,2},{2,0},{4,6},{6,4},{8,10},{10,8},{12,14},{14,12},{16,18},{18,... | collective-permute-start | bytes 393224 | tf_op jit(solution)/shard_map/ppermute | solution.py:194
  52.3 5.0 %collective-permute-start.19 = (bf16[64,1024]{1,0:T(8,128)(2,1)S(1)}, bf16[64,1024]{1,0:T(8,128)(2,1)S(1)}, u32[]{:S(2)}, u32[]{:S(2)}) collective-permute-start(bf16[64,1024]{1,0:T(8,128)(2,1)S(1)} %collective-permute-done.15), channel_id=1, source_target_pairs={{0,2},{2,0},{4,6},{6,4},{8,10},{10,8},{12,14},{14,12},{16,18},{18,... | collective-permute-start | bytes 393224 | tf_op jit(solution)/shard_map/ppermute | solution.py:194
  53.5 5.2 %collective-permute-start.20 = (bf16[64,1024]{1,0:T(8,128)(2,1)S(1)}, bf16[64,1024]{1,0:T(8,128)(2,1)S(1)}, u32[]{:S(2)}, u32[]{:S(2)}) collective-permute-start(bf16[64,1024]{1,0:T(8,128)(2,1)S(1)} %collective-permute-done.16), channel_id=1, source_target_pairs={{0,2},{2,0},{4,6},{6,4},{8,10},{10,8},{12,14},{14,12},{16,18},{18,... | collective-permute-start | bytes 393224 | tf_op jit(solution)/shard_map/ppermute | solution.py:194
  59.2 1.4 %collective-permute-start.21 = (bf16[8,16,512]{2,1,0:T(8,128)(2,1)S(1)}, bf16[8,16,512]{2,1,0:T(8,128)(2,1)S(1)}, u32[]{:S(2)}, u32[]{:S(2)}) collective-permute-start(bf16[8,16,512]{2,1,0:T(8,128)(2,1)S(1)} %dynamic-slice_bitcast_fusion), channel_id=1, source_target_pairs={{0,1},{1,0},{2,3},{3,2},{4,5},{5,4},{6,7},{7,6},{8,9},{9,8},{10,11... | collective-permute-start | bytes 393224 | tf_op jit(solution)/shard_map/ppermute | solution.py:295
  (4 other events, 28.3 us)
